TPU v7x, 128 devices: a whole 4x4x4 slice. The times are simulated.
128 devices in a mesh: row: 8 (over y, core), col: 16 (over x, z).
Axes of the slice: x: 4, y: 4, z: 4, core: 2. Of those that a mesh axis runs over, the one named last changes fastest.
Arguments:
- lower_blocks: float32 [6, 1024, 1024], P(None, 'col', 'row'), may hold values from -0.125 to 0.125
- inverses: float32 [4, 1024, 1024], P(None, 'col', 'row'), may hold values from -0.0625 to 1.5, as said below
- panel_right: float32 [4, 1024, 1024], P(None, 'row'), may hold values from -6 to 6
- trail_factor: float32 [4, 1024, 65536], P(None, 'col', 'row'), may hold values from -0.125 to 0.125
- trail_right: float32 [65536, 1024], P(('row', 'col')), may hold values from -6 to 6
Outputs:
- solution: float32 [4, 1024, 1024], P(None, 'col', 'row')
- updated: float32 [65536, 1024], P(('row', 'col'))
Inputs may be any that keep to these rules, and one draw needn't show every extreme that they name: inverses holds float32 matrices with diagonal entries between 0.5 and 1.5.
All inputs are finite; a program needn't handle non-finite values.
Results may differ from a plain program's by a relative error of at most 0.00011.
Values sent between devices are 32-bit elements; how exact they have to be, the bound alone decides.
No kernel may reach another device: no remote copies, remote signals or barrier semaphores. Data moves between devices by JAX's collectives and lax.ppermute only.
A program may use at most 192 MiB of HBM per device.

v0:
```python
import jax
import jax.numpy as jnp
from jax import lax
from jax.sharding import PartitionSpec as P


def first_contract(left, right):
    return lax.dot_general(
        left,
        right,
        (((0,), (0,)), ((), ())),
        precision=lax.Precision.HIGHEST,
        preferred_element_type=jnp.float32,
    )


def per_device(lower_blocks, inverses, panel_right, trail_factor, trail_right):
    highest = lax.Precision.HIGHEST
    steps = inverses.shape[0]
    col_part = lower_blocks.shape[1]
    row_part = lower_blocks.shape[2]
    queries = panel_right.shape[2]
    solved_rows = []
    pieces = []
    for step in range(steps):
        partial_value = jnp.zeros((row_part, queries), jnp.float32)
        for prior in range(step):
            index = step * (step - 1) // 2 + prior
            partial_value = partial_value + first_contract(lower_blocks[index], solved_rows[prior])
        if step > 0:
            remaining = panel_right[step] - lax.psum(partial_value, "col")
        else:
            remaining = panel_right[step]
        block_term = jnp.dot(
            inverses[step], remaining, precision=highest, preferred_element_type=jnp.float32
        )
        own_piece = lax.psum_scatter(block_term, "row", scatter_dimension=1, tiled=True)
        pieces.append(own_piece)
        solved_rows.append(lax.all_gather(own_piece, "row", axis=1, tiled=True))
    solution = jnp.stack(pieces)
    stacked_rows = jnp.stack(solved_rows)
    flat_factor = trail_factor.reshape(steps * col_part, trail_factor.shape[2])
    flat_solved = stacked_rows.reshape(steps * col_part, queries)
    update = lax.psum_scatter(
        first_contract(flat_factor, flat_solved), "col", scatter_dimension=0, tiled=True
    )
    return (solution, trail_right - update)


def solution(mesh):
    in_specs = (
        P(None, "col", "row"),
        P(None, "col", "row"),
        P(None, "row", None),
        P(None, "col", "row"),
        P(("row", "col"), None),
    )
    out_specs = (P(None, "col", "row"), P(("row", "col"), None))
    return jax.shard_map(
        per_device, mesh=mesh, in_specs=in_specs, out_specs=out_specs, check_vma=False
    )
```

profile of v0, /device:TPU:1, one launch (start us, length us, event | category | flops | bytes accessed | tf_op | source)
XLA Modules:
  0.0 696.3 jit_solution(1158782214824556713)
XLA Ops:
  7.2 0.0 copy-start.6
  7.2 0.0 copy-start
  7.2 0.0 copy-start.1
  7.2 0.0 reduce-scatter.6.cloned.1.call-start
  7.2 2.3 fusion.9
  9.6 0.0 reduce-scatter.6.cloned.1.call-update
  9.6 0.0 all-reduce.4.cloned.1.call-start
  9.7 32.4 %reduce-scatter.6.cloned.1.call-done = f32[64,128]{1,0:T(8,128)} async-done(((f32[64,1024]{1,0:T(8,128)}), f32[64,128]{1,0:T(8,128)}) %reduce-scatter.6.cloned.1.call-update) | async-done | bytes 32784 | tf_op jit(solution)/shard_map/reduce_scatter | solution.py:37
  42.0 16.3 %all_gather.12 = f32[64,1024]{1,0:T(8,128)S(1)} all-gather(f32[64,128]{1,0:T(8,128)} %reduce-scatter.6.cloned.1.call-done), channel_id=1, replica_groups=mesh['row'=8,'col'=16] {'row'}, dimensions={1}, use_global_device_ids=true | all-gather | bytes 294912 | tf_op jit(solution)/shard_map/all_gather | solution.py:39
  58.3 2.2 convolution_bitcast_fusion.1
  60.4 0.0 all-reduce.4.cloned.1.call-update
  60.5 0.0 reduce-scatter.8.cloned.1.call-start
  60.5 83.4 %all-reduce.4.cloned.1.call-done = f32[128,1024]{1,0:T(8,128)} async-done(((f32[128,1024]{1,0:T(8,128)}), f32[128,1024]{1,0:T(8,128)}) %all-reduce.4.cloned.1.call-update) | async-done | bytes 524304 | tf_op jit(solution)/shard_map/psum | solution.py:31
  143.9 0.0 copy-done.6
  143.9 2.2 convolution_bitcast_fusion.4
  146.1 0.0 reduce-scatter.8.cloned.1.call-update
  146.1 0.0 all-reduce.6.cloned.1.call-start
  146.2 0.0 copy-done.1
  146.2 0.6 fusion.22
  146.8 28.5 %reduce-scatter.8.cloned.1.call-done = f32[64,128]{1,0:T(8,128)} async-done(((f32[64,1024]{1,0:T(8,128)}), f32[64,128]{1,0:T(8,128)}) %reduce-scatter.8.cloned.1.call-update) | async-done | bytes 32784 | tf_op jit(solution)/shard_map/reduce_scatter | solution.py:37
  175.3 16.2 %all_gather.13 = f32[64,1024]{1,0:T(8,128)S(1)} all-gather(f32[64,128]{1,0:T(8,128)} %reduce-scatter.8.cloned.1.call-done), channel_id=1, replica_groups=mesh['row'=8,'col'=16] {'row'}, dimensions={1}, use_global_device_ids=true | all-gather | bytes 294912 | tf_op jit(solution)/shard_map/all_gather | solution.py:39
  191.5 1.4 fusion.1
  193.0 0.0 all-reduce.6.cloned.1.call-update
  193.0 0.0 reduce-scatter.10.cloned.1.call-start
  193.0 83.3 %all-reduce.6.cloned.1.call-done = f32[128,1024]{1,0:T(8,128)} async-done(((f32[128,1024]{1,0:T(8,128)}), f32[128,1024]{1,0:T(8,128)}) %all-reduce.6.cloned.1.call-update) | async-done | bytes 524304 | tf_op jit(solution)/shard_map/psum | solution.py:31
  276.3 2.2 convolution_bitcast_fusion.3
  278.5 0.0 reduce-scatter.10.cloned.1.call-update
  278.5 0.0 all-reduce.8.cloned.1.call-start
  278.6 0.6 fusion.18
  279.2 1.4 convolution_add_fusion.1
  280.6 26.5 %reduce-scatter.10.cloned.1.call-done = f32[64,128]{1,0:T(8,128)} async-done(((f32[64,1024]{1,0:T(8,128)}), f32[64,128]{1,0:T(8,128)}) %reduce-scatter.10.cloned.1.call-update) | async-done | bytes 32784 | tf_op jit(solution)/shard_map/reduce_scatter | solution.py:37
  307.1 16.2 %all_gather.14 = f32[64,1024]{1,0:T(8,128)S(1)} all-gather(f32[64,128]{1,0:T(8,128)} %reduce-scatter.10.cloned.1.call-done), channel_id=1, replica_groups=mesh['row'=8,'col'=16] {'row'}, dimensions={1}, use_global_device_ids=true | all-gather | bytes 294912 | tf_op jit(solution)/shard_map/all_gather | solution.py:39
  323.3 2.5 fusion
  325.8 0.0 all-reduce.8.cloned.1.call-update
  325.8 0.0 reduce-scatter.12.cloned.1.call-start
  325.9 83.3 %all-reduce.8.cloned.1.call-done = f32[128,1024]{1,0:T(8,128)} async-done(((f32[128,1024]{1,0:T(8,128)}), f32[128,1024]{1,0:T(8,128)}) %all-reduce.8.cloned.1.call-update) | async-done | bytes 524304 | tf_op jit(solution)/shard_map/psum | solution.py:31
  409.2 2.2 convolution_bitcast_fusion.2
  411.4 0.0 reduce-scatter.12.cloned.1.call-update
  411.4 0.0 reduce-scatter.14.cloned.1.call-start
  411.4 29.1 %reduce-scatter.12.cloned.1.call-done = f32[64,128]{1,0:T(8,128)} async-done(((f32[64,1024]{1,0:T(8,128)}), f32[64,128]{1,0:T(8,128)}) %reduce-scatter.12.cloned.1.call-update) | async-done | bytes 32784 | tf_op jit(solution)/shard_map/reduce_scatter | solution.py:37
  440.6 16.4 %all_gather.15 = f32[64,1024]{1,0:T(8,128)S(1)} all-gather(f32[64,128]{1,0:T(8,128)} %reduce-scatter.12.cloned.1.call-done), channel_id=1, replica_groups=mesh['row'=8,'col'=16] {'row'}, dimensions={1}, use_global_device_ids=true | all-gather | bytes 294912 | tf_op jit(solution)/shard_map/all_gather | solution.py:39
  457.0 31.9 %convolution_bitcast_fusion = f32[8192,1024]{0,1:T(8,128)} fusion(f32[4,64,8192]{2,1,0:T(8,128)} %param.8, f32[1,64,1024]{2,1,0:T(8,128)S(1)} %bitcast.76, f32[1,64,1024]{2,1,0:T(8,128)S(1)} %bitcast.75, f32[1,64,1024]{2,1,0:T(8,128)S(1)} %bitcast.74, f32[1,64,1024]{2,1,0:T(8,128)S(1)} %bitcast.73), kind=kOutput, calls=%fused_computation | convolution fusion | flops 25770590208 | bytes 42991616 | tf_op jit(solution)/shard_map/dot_general | solution.py:8
  488.9 0.0 reduce-scatter.14.cloned.1.call-update
  489.0 1.9 copy.7
  491.0 0.7 pad_maximum_fusion
  491.6 191.5 %reduce-scatter.14.cloned.1.call-done = f32[512,1024]{0,1:T(8,128)} async-done(((f32[8192,1024]{0,1:T(8,128)}), f32[512,1024]{0,1:T(8,128)}) %reduce-scatter.14.cloned.1.call-update) | async-done | bytes 2097168 | tf_op jit(solution)/shard_map/reduce_scatter | solution.py:44
  683.2 3.4 sub.15
  686.6 2.9 copy.8
  (9 shorter events, 0.0 us)
Async XLA Ops:
  7.2 136.8 %copy-start.6 = (f32[4,64,128]{2,1,0:T(8,128)S(1)}, f32[4,64,128]{2,1,0:T(8,128)}, u32[]{:S(2)}) copy-start(f32[4,64,128]{2,1,0:T(8,128)} %param.6) | copy-start | bytes 393220
  7.2 136.7 %copy-start = (f32[4,128,1024]{2,1,0:T(8,128)S(1)}, f32[4,128,1024]{2,1,0:T(8,128)}, u32[]{:S(2)}) copy-start(f32[4,128,1024]{2,1,0:T(8,128)} %param.7) | copy-start | bytes 6291460
  7.2 139.0 %copy-start.1 = (f32[6,64,128]{2,1,0:T(8,128)S(1)}, f32[6,64,128]{2,1,0:T(8,128)}, u32[]{:S(2)}) copy-start(f32[6,64,128]{2,1,0:T(8,128)} %param.5) | copy-start | bytes 589828
  7.2 34.8 %reduce-scatter.6.cloned.1.call-start = ((), (), s32[]{:S(2)}) async-start(), calls=%async_computation.5 | async-start | bytes 294912 | tf_op jit(solution)/shard_map/reduce_scatter | solution.py:37
  9.6 134.3 %all-reduce.4.cloned.1.call-start = ((), (), s32[]{:S(2)}) async-start(), calls=%async_computation.6 | async-start | bytes 1048576 | tf_op jit(solution)/shard_map/psum | solution.py:31
  60.5 114.8 %reduce-scatter.8.cloned.1.call-start = ((), (), s32[]{:S(2)}) async-start(), calls=%async_computation.7 | async-start | bytes 294912 | tf_op jit(solution)/shard_map/reduce_scatter | solution.py:37
  146.1 130.2 %all-reduce.6.cloned.1.call-start = ((), (), s32[]{:S(2)}) async-start(), calls=%async_computation.8 | async-start | bytes 1048576 | tf_op jit(solution)/shard_map/psum | solution.py:31
  193.0 114.1 %reduce-scatter.10.cloned.1.call-start = ((), (), s32[]{:S(2)}) async-start(), calls=%async_computation.9 | async-start | bytes 294912 | tf_op jit(solution)/shard_map/reduce_scatter | solution.py:37
  278.5 130.6 %all-reduce.8.cloned.1.call-start = ((), (), s32[]{:S(2)}) async-start(), calls=%async_computation.10 | async-start | bytes 1048576 | tf_op jit(solution)/shard_map/psum | solution.py:31
  325.8 114.7 %reduce-scatter.12.cloned.1.call-start = ((), (), s32[]{:S(2)}) async-start(), calls=%async_computation.11 | async-start | bytes 294912 | tf_op jit(solution)/shard_map/reduce_scatter | solution.py:37
  411.4 271.8 %reduce-scatter.14.cloned.1.call-start = ((), (), s32[]{:S(2)}) async-start(), calls=%async_computation.12 | async-start | bytes 35651584 | tf_op jit(solution)/shard_map/reduce_scatter | solution.py:44
  488.9 2.0 copy-start.2
  488.9 2.0 copy-start.3
  488.9 2.0 copy-start.4
  489.0 2.0 copy-start.5
Sparse Core Ops, SparseCore 0:
  11.0 31.0 reduce-scatter.5
  60.6 83.2 all-reduce.3
  146.8 28.4 reduce-scatter.7
  193.1 83.1 all-reduce.5
  278.7 28.4 reduce-scatter.9
  326.0 83.1 all-reduce.7
  412.1 28.4 reduce-scatter.11
  489.0 194.0 reduce-scatter.13
where the time goes:
time: 697 us; the launch traced here: 696 us
  waiting for transfers between devices  558 us (80%)
  blocking collectives  65.1 us (9%)
  matrix products  49.5 us (7%)
  between operations  14.3 us (2%)
    psum x3, waiting for transfers between devices, per_device(): remaining = panel_right[step] - lax.psum(partial_value, 'col')  250 us
    reduce_scatter x1, waiting for transfers between devices, per_device(): lax.psum_scatter(first_contract(flat_factor, flat_solved), 'col', scatter...  192 us
    reduce_scatter x4, waiting for transfers between devices, per_device(): lax.psum_scatter(block_term, 'row', scatter_dimension=1, tiled=True)  116 us
    all_gather x4, blocking collectives, per_device(): solved_rows.append(lax.all_gather(own_piece, 'row', axis=1, tiled=True))  65.1 us
    dot_general x7, matrix products, first_contract(): lax.dot_general(left, right, (((0,), (0,)), ((), ())), precision=lax.Prec...  40.7 us
  transfers between devices with their start and end apart: 8, of which 8 were waited for; matrix products, arithmetic and copies ran while one was open for 1% of the time, Pallas kernels for 0%

commit v1 on v0

v1 whole, which is shorter than its diff:
```python
import jax
import jax.numpy as jnp
from jax import lax
from jax.experimental import pallas as pl
from jax.experimental.pallas import tpu as pltpu
from jax.sharding import PartitionSpec as P

F32 = jnp.float32
BF16 = jnp.bfloat16


def col_perm(dx, dz):
    return [(((x + dx) % 4) * 4 + (z + dz) % 4, x * 4 + z) for x in range(4) for z in range(4)]


def y_perm(dy):
    return [(2 * ((y + dy) % 4) + c, 2 * y + c) for y in range(4) for c in range(2)]


CORE_PERM = [(i, i ^ 1) for i in range(8)]


def from_x(value, d):
    return lax.ppermute(value, "col", col_perm(d, 0))


def from_z(value, d):
    return lax.ppermute(value, "col", col_perm(0, d))


def from_y(value, d):
    return lax.ppermute(value, "row", y_perm(d))


def from_core(value):
    return lax.ppermute(value, "row", CORE_PERM)


def ring_stack(value, fetch):
    far = {d: fetch(value, d) for d in (1, 3, 2)}
    return jnp.stack([value, far[1], far[2], far[3]])


def gather_blocks(set_a, set_b):
    near_a = ring_stack(set_a, from_x)
    near_b = ring_stack(set_b, from_z)
    near_a, near_b = lax.optimization_barrier((near_a, near_b))
    all_a = jnp.swapaxes(ring_stack(near_a, from_z), 0, 1)
    all_b = ring_stack(near_b, from_x)
    return all_a.reshape((-1,) + set_a.shape), all_b.reshape((-1,) + set_b.shape)


def split_bf16(value):
    high = value.astype(BF16)
    low = (value - high.astype(F32)).astype(BF16)
    return high, low


def dot3(a, b, dims):
    ah, al = split_bf16(a)
    bh, bl = split_bf16(b)

    def one(p, q):
        return lax.dot_general(p, q, (dims, ((), ())), preferred_element_type=F32)

    return one(ah, bh) + (one(ah, bl) + one(al, bh))


def dot_nn(a, b):
    return dot3(a, b, ((1,), (0,)))


def dot_nt(a, b):
    return dot3(a, b, ((1,), (1,)))


def flat(ref):
    value = ref[:, 0]
    return value.reshape(value.shape[0] * value.shape[1], value.shape[2])


def take_piece(place_ref, piece_ref, total):
    x, y, z = place_ref[0], place_ref[1], place_ref[2]
    width = piece_ref.shape[1]
    shift = lax.rem(y - x + 4, 4)
    quarter = total[:, 0:width]
    for d in range(1, 4):
        quarter = jnp.where(shift == d, total[:, d * width:(d + 1) * width], quarter)
    piece_ref[...] = pltpu.roll(quarter, z * (width // 4), 1)


def first_step_kernel(rem_ref, inv_own, inv_far, part_ref):
    half = inv_own.shape[3]
    rem = rem_ref[0]
    part_ref[...] = dot_nt(rem[:, :half], flat(inv_own)) + dot_nt(rem[:, half:], flat(inv_far))


def step_kernel(place_ref, p0, p1, p2, p3, rem_ref, low_own, low_far, inv_own, inv_far, x_ref, piece_ref, part_ref):
    half = inv_own.shape[3]
    total = (p0[...] + p1[...]) + (p2[...] + p3[...])
    x_ref[...] = total
    take_piece(place_ref, piece_ref, total)
    rem = rem_ref[0]
    left = rem[:, :half] - dot_nn(total, flat(low_own))
    right = rem[:, half:] - dot_nn(total, flat(low_far))
    part_ref[...] = dot_nt(left, flat(inv_own)) + dot_nt(right, flat(inv_far))


def last_step_kernel(place_ref, p0, p1, p2, p3, piece_ref):
    take_piece(place_ref, piece_ref, (p0[...] + p1[...]) + (p2[...] + p3[...]))


def ahead_kernel(x_ref, rem_ref, low_own, low_far, o_ref):
    half = low_own.shape[3]
    total = x_ref[...]
    o_ref[0, :, :half] = rem_ref[0, :, :half] - dot_nn(total, flat(low_own))
    o_ref[0, :, half:] = rem_ref[0, :, half:] - dot_nn(total, flat(low_far))


def block_spec(place):
    where, index = place
    shape = where.shape
    return pl.BlockSpec((shape[0], 1) + shape[2:], lambda *_: (0, index, 0, 0))


def whole_spec(array):
    zeros = (0,) * len(array.shape)
    return pl.BlockSpec(array.shape, lambda *_: zeros)


def small_call(kernel, place, plain, blocks, outs):
    specs = [whole_spec(v) for v in plain] + [block_spec(v) for v in blocks]
    return pl.pallas_call(
        kernel,
        grid_spec=pltpu.PrefetchScalarGridSpec(
            num_scalar_prefetch=0 if place is None else 1,
            grid=(1,),
            in_specs=specs,
            out_specs=[whole_spec(v) for v in outs],
        ),
        out_shape=outs,
        compiler_params=pltpu.CompilerParams(vmem_limit_bytes=40 * 2**20),
    )(*([] if place is None else [place]), *plain, *[v[0] for v in blocks])


def split_kernel(f_ref, o_ref):
    parts = o_ref.shape[0]
    width = o_ref.shape[3]
    for d in range(parts):
        o_ref[d, 0] = f_ref[0, :, d * width:(d + 1) * width]


def split_by_owner(factor, first, count, owners):
    rows = factor.shape[1]
    width = factor.shape[2] // owners
    per = 4
    return pl.pallas_call(
        split_kernel,
        grid=(count, owners // per),
        in_specs=[pl.BlockSpec((1, rows, per * width), lambda k, g: (first + k, 0, g))],
        out_specs=pl.BlockSpec((per, 1, rows, width), lambda k, g: (g, k, 0, 0)),
        out_shape=jax.ShapeDtypeStruct((owners, count, rows, width), F32),
        compiler_params=pltpu.CompilerParams(vmem_limit_bytes=32 * 2**20),
    )(factor)


def dot_b(a, b):
    return lax.dot_general(a, b, (((1,), (1,)), ((), ())), preferred_element_type=F32)


def update_kernel(place_ref, f_ref, *refs):
    x_refs = refs[:8]
    base_ref, o_ref, s_ref, high_ref, low_ref = refs[8:]
    step = pl.program_id(0)
    x, y, z, core, row = [place_ref[i] for i in range(5)]
    half = o_ref.shape[1] // 2
    width = x_refs[0].shape[3]

    @pl.when(step == 0)
    def _():
        o_ref[...] = base_ref[...]

    for d in range(4):
        quarter = pl.ds(pl.multiple_of(lax.rem(y + d, 4) * width, width), width)
        for side in range(2):
            part = x_refs[2 * d + side][:, 0]
            part = part.reshape(part.shape[0] * part.shape[1], width)
            high, low = split_bf16(part)
            high_ref[side, :, quarter] = high
            low_ref[side, :, quarter] = low

    block = s_ref.shape[1]
    for d in range(4):
        for side in range(2):
            mine = (lax.rem(x - y + 4, 4) == d) & ((row // 4 == core) == (side == 0))

            @pl.when(mine)
            def _(part_ref=x_refs[2 * d + side]):
                part = part_ref[pl.ds(4 * lax.rem(row, 4), 4), 0]
                part = part.reshape(part.shape[0] * part.shape[1], width)
                part = pltpu.roll(part, lax.rem(4 - z, 4) * block, 1)
                s_ref[0] = part[:, :128].T[:block]

    f = f_ref[:, 0]
    f = f.reshape(f.shape[0] * f.shape[1], f.shape[2]).T
    fh, fl = split_bf16(f)
    for side in range(2):
        where = core if side == 0 else 1 - core
        cols = pl.ds(pl.multiple_of(where * half, half), half)
        xh = high_ref[side]
        o_ref[:, cols] -= dot_b(fh, xh) + (dot_b(fh, low_ref[side]) + dot_b(fl, xh))


def update(place, factor, f_first, xs, x_first, count, base, s_rows, s_cols):
    owners, _, rows, width = factor.shape
    _, _, q, m = xs[0].shape
    whole = pl.BlockSpec(base.shape, lambda k, p: (0, 0))
    grid_spec = pltpu.PrefetchScalarGridSpec(
        num_scalar_prefetch=1,
        grid=(count,),
        in_specs=[pl.BlockSpec((owners, 1, rows, width), lambda k, p: (0, f_first + k, 0, 0))]
        + [pl.BlockSpec((owners, 1, q, m), lambda k, p: (0, x_first + k, 0, 0))] * 8
        + [whole],
        out_specs=[whole, pl.BlockSpec((1, s_rows, s_cols), lambda k, p: (k, 0, 0))],
        scratch_shapes=[
            pltpu.VMEM((2, owners * q, 4 * m), BF16),
            pltpu.VMEM((2, owners * q, 4 * m), BF16),
        ],
    )
    return pl.pallas_call(
        update_kernel,
        grid_spec=grid_spec,
        out_shape=[
            jax.ShapeDtypeStruct(base.shape, F32),
            jax.ShapeDtypeStruct((count, s_rows, s_cols), F32),
        ],
        compiler_params=pltpu.CompilerParams(vmem_limit_bytes=56 * 2**20),
    )(place, factor, *xs, base)


def per_device(lower_blocks, inverses, panel_right, trail_factor, trail_right):
    row = lax.axis_index("row")
    col = lax.axis_index("col")
    y, core = row // 2, row % 2
    x, z = col // 4, col % 4

    place = jnp.stack([x, y, z, core, row]).astype(jnp.int32)
    steps = inverses.shape[0]
    order = inverses.shape[1] * 16
    q_all = panel_right.shape[2]
    share = q_all // 32

    def columns(which):
        return lax.dynamic_slice_in_dim(panel_right, which * (q_all // 2) + col * share, share, 2)

    right_own = jnp.swapaxes(columns(core), 1, 2)
    right_far = from_core(jnp.swapaxes(columns(1 - core), 1, 2))
    right = jnp.concatenate([right_own, right_far], axis=2)

    set_a = jnp.concatenate([inverses[0:1], lower_blocks[0:1], inverses[1:2], lower_blocks[1:3]])
    set_b = jnp.concatenate([inverses[2:4], lower_blocks[3:6]])
    got_a, got_b = gather_blocks(set_a, set_b)
    far_a = from_core(got_a)
    far_b = from_core(got_b)
    inv = [(0, 0), (0, 2), (1, 0), (1, 1)]
    low = {(1, 0): (0, 1), (2, 0): (0, 3), (2, 1): (0, 4), (3, 0): (1, 2), (3, 1): (1, 3), (3, 2): (1, 4)}

    def both(where):
        pair = ((got_a, far_a), (got_b, far_b))[where[0]]
        return [(v, where[1]) for v in pair]

    split_0 = split_by_owner(trail_factor, 0, 1, 16)
    split_1 = split_by_owner(trail_factor, 1, 1, 16)
    split_2 = split_by_owner(trail_factor, 2, 2, 16)

    def after(value, *earlier):
        return lax.optimization_barrier((value,) + earlier)[0]

    factor_0 = lax.all_to_all(after(split_0, got_a, got_b, split_1, split_2), "col", 0, 0)

    x_shape = jax.ShapeDtypeStruct((share, order), F32)
    piece_shape = jax.ShapeDtypeStruct((share, order // 4), F32)
    rem_shape = jax.ShapeDtypeStruct((1, share, right.shape[2]), F32)
    rem = [right[k:k + 1] for k in range(steps)]

    pieces = []
    (part,) = small_call(first_step_kernel, None, [rem[0]], both(inv[0]), [x_shape])
    for k in range(1, steps + 1):
        parts = [part] + [from_y(part, d) for d in (1, 3, 2)]
        if k == steps:
            (piece,) = small_call(last_step_kernel, place, parts, [], [piece_shape])
        else:
            solved, piece, part = small_call(
                step_kernel, place, parts + [rem[k]], both(low[(k, k - 1)]) + both(inv[k]),
                [x_shape, piece_shape, x_shape],
            )
            for later in range(k + 1, steps):
                (rem[later],) = small_call(ahead_kernel, None, [solved, rem[later]], both(low[(later, k - 1)]), [rem_shape])
        pieces.append(piece)

    def spread(two):
        return jnp.broadcast_to(jnp.stack(two)[None], (16, 2) + two[0].shape)

    def core_pairs(parts):
        out = []
        for part in parts:
            out += [part, from_core(part)]
        return out

    block = (inverses.shape[1], inverses.shape[2])
    x_01 = lax.all_to_all(after(spread(pieces[0:2]), factor_0), "col", 0, 0)
    factor_1 = lax.all_to_all(after(split_1, x_01), "col", 0, 0)
    up_01, down_01 = from_y(x_01, 1), from_y(x_01, 3)
    x_23 = lax.all_to_all(after(spread(pieces[2:4]), factor_1, up_01, down_01), "col", 0, 0)
    across_01 = from_y(after(x_01, up_01, down_01), 2)
    factor_2 = lax.all_to_all(after(split_2, x_23), "col", 0, 0)
    xs_01 = core_pairs([x_01, up_01, across_01, down_01])
    out, solved_0 = update(place, factor_0, 0, xs_01, 0, 1, trail_right, *block)
    out, solved_1 = update(place, factor_1, 0, xs_01, 1, 1, out, *block)
    x_23 = after(x_23, across_01)
    up_23, down_23 = from_y(x_23, 1), from_y(x_23, 3)
    across_23 = from_y(after(x_23, out, up_23, down_23), 2)
    xs_23 = core_pairs([x_23, up_23, across_23, down_23])
    out, solved_2 = update(place, factor_2, 0, xs_23, 0, 2, out, *block)
    return (jnp.concatenate([solved_0, solved_1, solved_2]), out)


def solution(mesh):
    in_specs = (
        P(None, "col", "row"),
        P(None, "col", "row"),
        P(None, "row", None),
        P(None, "col", "row"),
        P(("row", "col"), None),
    )
    out_specs = (P(None, "col", "row"), P(("row", "col"), None))
    return jax.shard_map(
        per_device, mesh=mesh, in_specs=in_specs, out_specs=out_specs, check_vma=False
    )
```

time: 697 us -> 274 us (0.39)
  waiting for transfers between devices: 558 us -> 98.8 us
  starting transfers between devices: 0.33 us -> 84.6 us
  Pallas kernels: 0 us -> 50.9 us
  matrix products: 49.5 us -> 0 us
  blocking collectives: 65.1 us -> 19.4 us
  between operations: 14.3 us -> 1.03 us
  local copies, waits for them, and re-layouts: 4.85 us -> 16.2 us
    reduce_scatter x5 -> x0, waiting for transfers between devices: 308 us -> none  [the longest x1 192 us: per_device(): lax.psum_scatter(first_contract(flat_factor, flat_solved), 'col', scatter...]
    psum x3 -> x0, waiting for transfers between devices: 250 us -> none  [per_device(): remaining = panel_right[step] - lax.psum(partial_value, 'col')]
    ppermute x0 -> x41, waiting for transfers between devices: none -> 96.4 us  [the longest x18 62 us: from_y(): return lax.ppermute(value, 'row', y_perm(d))]
    all_gather x4 -> x0, blocking collectives: 65.1 us -> none  [per_device(): solved_rows.append(lax.all_gather(own_piece, 'row', axis=1, tiled=True))]
    ppermute x0 -> x41, starting transfers between devices: none -> 65 us  [the longest x11 26.5 us: from_core(): return lax.ppermute(value, 'row', CORE_PERM)]
    pallas_call x0 -> x14, Pallas kernels: none -> 50.9 us  [the longest x3 33.5 us: update(): pl.pallas_call(update_kernel, grid_spec=grid_spec, out_shape=[jax.ShapeDt...]
    dot_general x11 -> x0, matrix products: 49.5 us -> none  [the longest x7 40.7 us: first_contract(): lax.dot_general(left, right, (((0,), (0,)), ((), ())), precision=lax.Prec...]
    all_to_all x0 -> x4, starting transfers between devices: none -> 19.6 us  [the longest x1 6.17 us: per_device(): lax.all_to_all(after(spread(pieces[2:4]), factor_1, up_01, down_01), 'col...]
  transfers between devices with their start and end apart: 8 -> 45, of which waited for: 8 -> 26; matrix products, arithmetic and copies ran while one was open for 1% -> 2% of each run, Pallas kernels for 0% -> 14%
where the time goes in v1:
time: 274 us; the launch traced here: 273 us
  waiting for transfers between devices  98.8 us (36%)
  starting transfers between devices  84.6 us (31%)
  Pallas kernels  50.9 us (19%)
  blocking collectives  19.4 us (7%)
  local copies, waits for them, and re-layouts  16.2 us (6%)
    ppermute x18, waiting for transfers between devices, from_y(): return lax.ppermute(value, 'row', y_perm(d))  62 us
    pallas_call x3, Pallas kernels, update(): pl.pallas_call(update_kernel, grid_spec=grid_spec, out_shape=[jax.ShapeDt...  33.5 us
    ppermute x6, waiting for transfers between devices, from_z(): return lax.ppermute(value, 'col', col_perm(0, d))  30.6 us
    ppermute x11, starting transfers between devices, from_core(): return lax.ppermute(value, 'row', CORE_PERM)  26.5 us
    ppermute x18, starting transfers between devices, from_y(): return lax.ppermute(value, 'row', y_perm(d))  20.6 us
    all_to_all x1, blocking collectives, per_device(): x_01 = lax.all_to_all(after(spread(pieces[0:2]), factor_0), 'col', 0, 0)  19.4 us
    pallas_call x8, Pallas kernels, small_call(): pl.pallas_call(kernel, grid_spec=pltpu.PrefetchScalarGridSpec(num_scalar_...  15.6 us
    ppermute x6, starting transfers between devices, from_z(): return lax.ppermute(value, 'col', col_perm(0, d))  10.7 us
  transfers between devices with their start and end apart: 45, of which 26 were waited for; matrix products, arithmetic and copies ran while one was open for 2% of the time, Pallas kernels for 14%

profile of v1, /device:TPU:1, one launch (start us, length us, event | category | flops | bytes accessed | tf_op | source)
XLA Modules:
  0.0 273.2 jit_solution(13546238935092996668)
XLA Ops:
  3.0 2.1 collective-permute-start.2
  5.2 2.5 collective-permute-start.1
  10.5 1.7 collective-permute-start.5
  12.2 3.3 %collective-permute-start.4 = (f32[5,64,128]{2,1,0:T(8,128)S(1)}, f32[5,64,128]{2,1,0:T(8,128)S(1)}, u32[]{:S(2)}, u32[]{:S(2)}) collective-permute-start(f32[5,64,128]{2,1,0:T(8,128)S(1)} %get-tuple-element.53), channel_id=1, source_target_pairs={{2,0},{3,1},{0,2},{1,3},{6,4},{7,5},{4,6},{5,7},{10,8},{11,9},{8,1... | collective-permute-start | bytes 491528 | tf_op jit(solution)/shard_map/ppermute | solution.py:28
  17.1 4.4 %collective-permute-done.4 = f32[5,64,128]{2,1,0:T(8,128)S(1)} collective-permute-done((f32[5,64,128]{2,1,0:T(8,128)S(1)}, f32[5,64,128]{2,1,0:T(8,128)S(1)}, u32[]{:S(2)}, u32[]{:S(2)}) %collective-permute-start.4) | collective-permute-done | bytes 163872 | tf_op jit(solution)/shard_map/ppermute | solution.py:28
  21.8 2.5 collective-permute-start.8
  28.1 9.3 %collective-permute-done.8 = f32[4,5,64,128]{3,2,1,0:T(8,128)S(1)} collective-permute-done((f32[4,5,64,128]{3,2,1,0:T(8,128)S(1)}, f32[4,5,64,128]{3,2,1,0:T(8,128)S(1)}, u32[]{:S(2)}, u32[]{:S(2)}) %collective-permute-start.8) | collective-permute-done | bytes 655392 | tf_op jit(solution)/shard_map/ppermute | solution.py:28
  37.5 15.2 %collective-permute-done.7 = f32[4,5,64,128]{3,2,1,0:T(8,128)S(1)} collective-permute-done((f32[4,5,64,128]{3,2,1,0:T(8,128)S(1)}, f32[4,5,64,128]{3,2,1,0:T(8,128)S(1)}, u32[]{:S(2)}, u32[]{:S(2)}) %collective-permute-start.7) | collective-permute-done | bytes 655392 | tf_op jit(solution)/shard_map/ppermute | solution.py:28
  53.7 1.8 copy.7
  55.5 2.0 collective-permute-start.13
  57.9 2.2 collective-permute-start.20
  61.2 2.0 copy-done
  66.5 4.4 %all-to-all-start = ((f32[16,1,64,512]{3,2,1,0:T(8,128)}), f32[16,1,64,512]{3,2,1,0:T(8,128)}, u32[]{:S(2)}, u32[]{:S(2)}) async-start(f32[16,1,64,512]{3,2,1,0:T(8,128)} %copy-done.2), calls=%async_computation | async-start | bytes 4194304 | tf_op jit(solution)/shard_map/all_to_all | solution.py:279
  73.7 1.8 shard_map.71.p0
  75.5 2.8 %collective-permute-start.14 = (f32[32,1024]{1,0:T(8,128)S(1)}, f32[32,1024]{1,0:T(8,128)S(1)}, u32[]{:S(2)}, u32[]{:S(2)}) collective-permute-start(f32[32,1024]{1,0:T(8,128)S(1)} %shard_map.71.p0), channel_id=1, source_target_pairs={{32,0},{48,16},{64,32},{80,48},{96,64},{112,80},{0,96},{16,112},{3... | collective-permute-start | bytes 393224 | tf_op jit(solution)/shard_map/ppermute | solution.py:32
  78.3 1.6 collective-permute-start.16
  81.1 6.0 %collective-permute-done.15.p2 = f32[32,1024]{1,0:T(8,128)S(1)} collective-permute-done((f32[32,1024]{1,0:T(8,128)S(1)}, f32[32,1024]{1,0:T(8,128)S(1)}, u32[]{:S(2)}, u32[]{:S(2)}) %collective-permute-start.15) | collective-permute-done | bytes 131104 | tf_op jit(solution)/shard_map/ppermute | solution.py:32
  87.1 3.0 %shard_map.72 = (f32[32,1024]{1,0:T(8,128)S(1)}, f32[32,256]{1,0:T(8,128)S(1)}, f32[32,1024]{1,0:T(8,128)S(1)}) custom-call(s32[5]{0:T(128)S(1)} %stack.101.place_ref, f32[32,1024]{1,0:T(8,128)S(1)} %shard_map.71.p0, f32[32,1024]{1,0:T(8,128)S(1)} %collective-permute-done.14.p1, f32[32,1024]{1,0:T(8,128)S(1)} %collective-permute-done.15.p2, ...), custom_call_target="tpu_custom_call" | custom-call | tf_op jit(solution)/shard_map/pallas_call | solution.py:133
  90.1 1.5 collective-permute-start.18
  92.2 1.6 shard_map.73.rem_ref
  95.6 2.3 collective-permute-done.19.p3
  97.9 2.8 %shard_map.74 = (f32[32,1024]{1,0:T(8,128)S(1)}, f32[32,256]{1,0:T(8,128)S(1)}, f32[32,1024]{1,0:T(8,128)S(1)}) custom-call(s32[5]{0:T(128)S(1)} %stack.101.place_ref, f32[32,1024]{1,0:T(8,128)S(1)} %get-tuple-element.30.p0, f32[32,1024]{1,0:T(8,128)S(1)} %collective-permute-done.17.p1, f32[32,1024]{1,0:T(8,128)S(1)} %collective-permute-done.18.p2, ...), custom_call_target="tpu_custom_call" | custom-call | tf_op jit(solution)/shard_map/pallas_call | solution.py:133
  100.9 19.4 %all_to_all.25.refs_0_ = f32[16,2,32,256]{3,2,1,0:T(8,128)} all-to-all(f32[16,2,32,256]{3,2,1,0:T(8,128)S(1)} %broadcast_in_dim.4), channel_id=1, replica_groups=mesh['row'=8,'col'=16] {'col'}, dimensions={0} | all-to-all | bytes 2097152 | tf_op jit(solution)/shard_map/all_to_all | solution.py:311
  120.3 4.4 %all-to-all-start.2 = ((f32[16,1,64,512]{3,2,1,0:T(8,128)}), f32[16,1,64,512]{3,2,1,0:T(8,128)}, u32[]{:S(2)}, u32[]{:S(2)}) async-start(f32[16,1,64,512]{3,2,1,0:T(8,128)} %copy-done.1), calls=%async_computation.2 | async-start | bytes 4194304 | tf_op jit(solution)/shard_map/all_to_all | solution.py:312
  124.7 4.0 %collective-permute-start.22 = (f32[16,2,32,256]{3,2,1,0:T(8,128)}, f32[16,2,32,256]{3,2,1,0:T(8,128)}, u32[]{:S(2)}, u32[]{:S(2)}) collective-permute-start(f32[16,2,32,256]{3,2,1,0:T(8,128)} %all_to_all.25.refs_0_), channel_id=1, source_target_pairs={{32,0},{48,16},{64,32},{80,48},{96,64},{112,80},{0,96},{16,112},{3... | collective-permute-start | bytes 3145736 | tf_op jit(solution)/shard_map/ppermute | solution.py:32
  128.8 2.7 collective-permute-start.28
  132.6 1.5 shard_map.77.rem_ref
  134.1 1.5 shard_map.78.rem_ref
  135.6 16.9 %collective-permute-done.28.p1 = f32[32,1024]{1,0:T(8,128)S(1)} collective-permute-done((f32[32,1024]{1,0:T(8,128)S(1)}, f32[32,1024]{1,0:T(8,128)S(1)}, u32[]{:S(2)}, u32[]{:S(2)}) %collective-permute-start.28) | collective-permute-done | bytes 131104 | tf_op jit(solution)/shard_map/ppermute | solution.py:32
  152.4 2.8 %collective-permute-done.29.p2 = f32[32,1024]{1,0:T(8,128)S(1)} collective-permute-done((f32[32,1024]{1,0:T(8,128)S(1)}, f32[32,1024]{1,0:T(8,128)S(1)}, u32[]{:S(2)}, u32[]{:S(2)}) %collective-permute-start.29) | collective-permute-done | bytes 131104 | tf_op jit(solution)/shard_map/ppermute | solution.py:32
  155.7 2.9 %shard_map.79 = (f32[32,1024]{1,0:T(8,128)}, f32[32,256]{1,0:T(8,128)S(1)}, f32[32,1024]{1,0:T(8,128)S(1)}) custom-call(s32[5]{0:T(128)S(1)} %stack.101.place_ref, f32[32,1024]{1,0:T(8,128)S(1)} %get-tuple-element.39.p0, f32[32,1024]{1,0:T(8,128)S(1)} %collective-permute-done.28.p1, f32[32,1024]{1,0:T(8,128)S(1)} %collective-permute-done.29.p2, ...), custom_call_target="tpu_custom_call" | custom-call | tf_op jit(solution)/shard_map/pallas_call | solution.py:133
  160.1 1.6 collective-permute-start.33
  163.9 1.6 collective-permute-done.33.p3
  167.2 6.2 %all-to-all-start.3 = ((f32[16,2,32,256]{3,2,1,0:T(8,128)}), f32[16,2,32,256]{3,2,1,0:T(8,128)}, u32[]{:S(2)}, u32[]{:S(2)}) async-start(f32[16,2,32,256]{3,2,1,0:T(8,128)} %broadcast_in_dim.5), calls=%async_computation.3 | async-start | bytes 2097152 | tf_op jit(solution)/shard_map/all_to_all | solution.py:314
  173.4 1.6 collective-permute-start.25
  175.1 7.8 %collective-permute-start.21 = (f32[16,2,32,256]{3,2,1,0:T(8,128)S(1)}, f32[16,2,32,256]{3,2,1,0:T(8,128)S(1)}, u32[]{:S(2)}, u32[]{:S(2)}) collective-permute-start(f32[16,2,32,256]{3,2,1,0:T(8,128)S(1)} %copy-done.4), channel_id=1, source_target_pairs={{0,16},{16,0},{32,48},{48,32},{64,80},{80,64},{96,112},{112,96},{1... | collective-permute-start | bytes 3145736 | tf_op jit(solution)/shard_map/ppermute | solution.py:36
  182.8 2.4 all-to-all-done.3.refs_0_
  185.2 4.6 %all-to-all-start.4 = ((f32[16,2,64,512]{3,2,1,0:T(8,128)}), f32[16,2,64,512]{3,2,1,0:T(8,128)}, u32[]{:S(2)}, u32[]{:S(2)}) async-start(f32[16,2,64,512]{3,2,1,0:T(8,128)} %copy-done), calls=%async_computation.4 | async-start | bytes 8388608 | tf_op jit(solution)/shard_map/all_to_all | solution.py:316
  189.8 9.1 %collective-permute-start.23 = (f32[16,2,32,256]{3,2,1,0:T(8,128)}, f32[16,2,32,256]{3,2,1,0:T(8,128)S(1)}, u32[]{:S(2)}, u32[]{:S(2)}) collective-permute-start(f32[16,2,32,256]{3,2,1,0:T(8,128)} %collective-permute-done.22.refs_2_), channel_id=1, source_target_pairs={{0,16},{16,0},{32,48},{48,32},{64,80},{80,64},{96,112},{112,96},{1... | collective-permute-start | bytes 3145736 | tf_op jit(solution)/shard_map/ppermute | solution.py:36
  199.0 1.6 collective-permute-start.26
  200.6 1.4 collective-permute-start.35
  205.2 9.7 %shard_map.75 = (f32[512,1024]{1,0:T(8,128)}, f32[1,64,128]{2,1,0:T(8,128)}) custom-call(s32[5]{0:T(128)} %copy-done.3, f32[16,1,64,512]{3,2,1,0:T(8,128)} %all-to-all-done.f_ref, f32[16,2,32,256]{3,2,1,0:T(8,128)} %all_to_all.25.refs_0_, f32[16,2,32,256]{3,2,1,0:T(8,128)} %copy-done.6, f32[16,2,32,256]{3,2,1,0:T(8,128)} %collective-permute-done.22.refs_2_, ...), custom_call_target="tpu_custom_call" | custom-call | tf_op jit(solution)/shard_map/pallas_call | solution.py:230
  214.9 9.9 %shard_map.76 = (f32[512,1024]{1,0:T(8,128)}, f32[1,64,128]{2,1,0:T(8,128)}) custom-call(s32[5]{0:T(128)} %copy-done.3, f32[16,1,64,512]{3,2,1,0:T(8,128)} %all-to-all-done.2.f_ref, f32[16,2,32,256]{3,2,1,0:T(8,128)} %all_to_all.25.refs_0_, f32[16,2,32,256]{3,2,1,0:T(8,128)} %copy-done.6, f32[16,2,32,256]{3,2,1,0:T(8,128)} %collective-permute-done.22.refs_2_, ...), custom_call_target="tpu_custom_call" | custom-call | tf_op jit(solution)/shard_map/pallas_call | solution.py:230
  225.7 2.3 collective-permute-done.37.refs_6_
  229.6 23.7 %collective-permute-done.38.refs_4_ = f32[16,2,32,256]{3,2,1,0:T(8,128)S(1)} collective-permute-done((f32[16,2,32,256]{3,2,1,0:T(8,128)}, f32[16,2,32,256]{3,2,1,0:T(8,128)S(1)}, u32[]{:S(2)}, u32[]{:S(2)}) %collective-permute-start.38) | collective-permute-done | bytes 1048608 | tf_op jit(solution)/shard_map/ppermute | solution.py:32
  253.3 2.0 collective-permute-start.39
  257.7 13.9 %shard_map.81 = (f32[512,1024]{1,0:T(8,128)}, f32[2,64,128]{2,1,0:T(8,128)}) custom-call(s32[5]{0:T(128)} %copy-done.3, f32[16,2,64,512]{3,2,1,0:T(8,128)} %all-to-all-done.4.f_ref, f32[16,2,32,256]{3,2,1,0:T(8,128)} %all-to-all-done.3.refs_0_, f32[16,2,32,256]{3,2,1,0:T(8,128)} %copy-done.13, f32[16,2,32,256]{3,2,1,0:T(8,128)} %copy-done.10, ...), custom_call_target="tpu_custom_call" | custom-call | tf_op jit(solution)/shard_map/pallas_call | solution.py:230
  271.7 1.5 pad_maximum_fusion.5
  (120 shorter events, 38.5 us)
Async XLA Ops:
  3.0 12.5 %collective-permute-start.2 = (f32[5,64,128]{2,1,0:T(8,128)S(1)}, f32[5,64,128]{2,1,0:T(8,128)S(1)}, u32[]{:S(2)}, u32[]{:S(2)}) collective-permute-start(f32[5,64,128]{2,1,0:T(8,128)S(1)} %get-tuple-element.55), channel_id=1, source_target_pairs={{12,0},{13,1},{14,2},{15,3},{0,4},{1,5},{2,6},{3,7},{4,8},{5,9},{6... | collective-permute-start | bytes 491528 | tf_op jit(solution)/shard_map/ppermute | solution.py:24
  5.2 11.1 %collective-permute-start.1 = (f32[5,64,128]{2,1,0:T(8,128)S(1)}, f32[5,64,128]{2,1,0:T(8,128)S(1)}, u32[]{:S(2)}, u32[]{:S(2)}) collective-permute-start(f32[5,64,128]{2,1,0:T(8,128)S(1)} %get-tuple-element.55), channel_id=1, source_target_pairs={{8,0},{9,1},{10,2},{11,3},{12,4},{13,5},{14,6},{15,7},{0,8},{1,9},... | collective-permute-start | bytes 491528 | tf_op jit(solution)/shard_map/ppermute | solution.py:24
  7.6 8.7 %collective-permute-start = (f32[5,64,128]{2,1,0:T(8,128)S(1)}, f32[5,64,128]{2,1,0:T(8,128)S(1)}, u32[]{:S(2)}, u32[]{:S(2)}) collective-permute-start(f32[5,64,128]{2,1,0:T(8,128)S(1)} %get-tuple-element.55), channel_id=1, source_target_pairs={{4,0},{5,1},{6,2},{7,3},{8,4},{9,5},{10,6},{11,7},{12,8},{13,9},{1... | collective-permute-start | bytes 491528 | tf_op jit(solution)/shard_map/ppermute | solution.py:24
  10.5 6.5 %collective-permute-start.5 = (f32[5,64,128]{2,1,0:T(8,128)S(1)}, f32[5,64,128]{2,1,0:T(8,128)S(1)}, u32[]{:S(2)}, u32[]{:S(2)}) collective-permute-start(f32[5,64,128]{2,1,0:T(8,128)S(1)} %get-tuple-element.53), channel_id=1, source_target_pairs={{3,0},{0,1},{1,2},{2,3},{7,4},{4,5},{5,6},{6,7},{11,8},{8,9},{9,10... | collective-permute-start | bytes 491528 | tf_op jit(solution)/shard_map/ppermute | solution.py:28
  12.2 9.2 %collective-permute-start.4 = (f32[5,64,128]{2,1,0:T(8,128)S(1)}, f32[5,64,128]{2,1,0:T(8,128)S(1)}, u32[]{:S(2)}, u32[]{:S(2)}) collective-permute-start(f32[5,64,128]{2,1,0:T(8,128)S(1)} %get-tuple-element.53), channel_id=1, source_target_pairs={{2,0},{3,1},{0,2},{1,3},{6,4},{7,5},{4,6},{5,7},{10,8},{11,9},{8,1... | collective-permute-start | bytes 491528 | tf_op jit(solution)/shard_map/ppermute | solution.py:28
  15.5 6.2 %collective-permute-start.3 = (f32[5,64,128]{2,1,0:T(8,128)S(1)}, f32[5,64,128]{2,1,0:T(8,128)S(1)}, u32[]{:S(2)}, u32[]{:S(2)}) collective-permute-start(f32[5,64,128]{2,1,0:T(8,128)S(1)} %get-tuple-element.53), channel_id=1, source_target_pairs={{1,0},{2,1},{3,2},{0,3},{5,4},{6,5},{7,6},{4,7},{9,8},{10,9},{11,1... | collective-permute-start | bytes 491528 | tf_op jit(solution)/shard_map/ppermute | solution.py:28
  21.8 15.6 %collective-permute-start.8 = (f32[4,5,64,128]{3,2,1,0:T(8,128)S(1)}, f32[4,5,64,128]{3,2,1,0:T(8,128)S(1)}, u32[]{:S(2)}, u32[]{:S(2)}) collective-permute-start(f32[4,5,64,128]{3,2,1,0:T(8,128)S(1)} %pad_maximum_fusion.1), channel_id=1, source_target_pairs={{3,0},{0,1},{1,2},{2,3},{7,4},{4,5},{5,6},{6,7},{11,8},{8,9},{9,10... | collective-permute-start | bytes 1966088 | tf_op jit(solution)/shard_map/ppermute | solution.py:28
  24.3 28.4 %collective-permute-start.7 = (f32[4,5,64,128]{3,2,1,0:T(8,128)S(1)}, f32[4,5,64,128]{3,2,1,0:T(8,128)S(1)}, u32[]{:S(2)}, u32[]{:S(2)}) collective-permute-start(f32[4,5,64,128]{3,2,1,0:T(8,128)S(1)} %pad_maximum_fusion.1), channel_id=1, source_target_pairs={{2,0},{3,1},{0,2},{1,3},{6,4},{7,5},{4,6},{5,7},{10,8},{11,9},{8,1... | collective-permute-start | bytes 1966088 | tf_op jit(solution)/shard_map/ppermute | solution.py:28
  25.7 27.7 %collective-permute-start.6 = (f32[4,5,64,128]{3,2,1,0:T(8,128)S(1)}, f32[4,5,64,128]{3,2,1,0:T(8,128)S(1)}, u32[]{:S(2)}, u32[]{:S(2)}) collective-permute-start(f32[4,5,64,128]{3,2,1,0:T(8,128)S(1)} %pad_maximum_fusion.1), channel_id=1, source_target_pairs={{1,0},{2,1},{3,2},{0,3},{5,4},{6,5},{7,6},{4,7},{9,8},{10,9},{11,1... | collective-permute-start | bytes 1966088 | tf_op jit(solution)/shard_map/ppermute | solution.py:28
  26.8 30.7 %collective-permute-start.11 = (f32[4,5,64,128]{3,2,1,0:T(8,128)S(1)}, f32[4,5,64,128]{3,2,1,0:T(8,128)S(1)}, u32[]{:S(2)}, u32[]{:S(2)}) collective-permute-start(f32[4,5,64,128]{3,2,1,0:T(8,128)S(1)} %pad_maximum_fusion.2), channel_id=1, source_target_pairs={{12,0},{13,1},{14,2},{15,3},{0,4},{1,5},{2,6},{3,7},{4,8},{5,9},{6... | collective-permute-start | bytes 1966088 | tf_op jit(solution)/shard_map/ppermute | solution.py:24
  27.1 30.4 %collective-permute-start.10 = (f32[4,5,64,128]{3,2,1,0:T(8,128)S(1)}, f32[4,5,64,128]{3,2,1,0:T(8,128)S(1)}, u32[]{:S(2)}, u32[]{:S(2)}) collective-permute-start(f32[4,5,64,128]{3,2,1,0:T(8,128)S(1)} %pad_maximum_fusion.2), channel_id=1, source_target_pairs={{8,0},{9,1},{10,2},{11,3},{12,4},{13,5},{14,6},{15,7},{0,8},{1,9},... | collective-permute-start | bytes 1966088 | tf_op jit(solution)/shard_map/ppermute | solution.py:24
  37.4 20.4 %collective-permute-start.9 = (f32[4,5,64,128]{3,2,1,0:T(8,128)S(1)}, f32[4,5,64,128]{3,2,1,0:T(8,128)S(1)}, u32[]{:S(2)}, u32[]{:S(2)}) collective-permute-start(f32[4,5,64,128]{3,2,1,0:T(8,128)S(1)} %pad_maximum_fusion.2), channel_id=1, source_target_pairs={{4,0},{5,1},{6,2},{7,3},{8,4},{9,5},{10,6},{11,7},{12,8},{13,9},{1... | collective-permute-start | bytes 1966088 | tf_op jit(solution)/shard_map/ppermute | solution.py:24
  55.5 18.2 %collective-permute-start.13 = (f32[16,5,64,128]{3,2,1,0:T(8,128)}, f32[16,5,64,128]{3,2,1,0:T(8,128)}, u32[]{:S(2)}, u32[]{:S(2)}) collective-permute-start(f32[16,5,64,128]{3,2,1,0:T(8,128)} %bitcast.18.inv_own.low_own), channel_id=1, source_target_pairs={{0,16},{16,0},{32,48},{48,32},{64,80},{80,64},{96,112},{112,96},{1... | collective-permute-start | bytes 7864328 | tf_op jit(solution)/shard_map/ppermute | solution.py:36
  57.9 35.8 %collective-permute-start.20 = (f32[16,5,64,128]{3,2,1,0:T(8,128)S(1)}, f32[16,5,64,128]{3,2,1,0:T(8,128)}, u32[]{:S(2)}, u32[]{:S(2)}) collective-permute-start(f32[16,5,64,128]{3,2,1,0:T(8,128)S(1)} %bitcast.33), channel_id=1, source_target_pairs={{0,16},{16,0},{32,48},{48,32},{64,80},{80,64},{96,112},{112,96},{1... | collective-permute-start | bytes 7864328 | tf_op jit(solution)/shard_map/ppermute | solution.py:36
  66.5 34.2 %all-to-all-start = ((f32[16,1,64,512]{3,2,1,0:T(8,128)}), f32[16,1,64,512]{3,2,1,0:T(8,128)}, u32[]{:S(2)}, u32[]{:S(2)}) async-start(f32[16,1,64,512]{3,2,1,0:T(8,128)} %copy-done.2), calls=%async_computation | async-start | bytes 4194304 | tf_op jit(solution)/shard_map/all_to_all | solution.py:279
  72.3 1.3 collective-permute-start.12
  75.5 5.5 %collective-permute-start.14 = (f32[32,1024]{1,0:T(8,128)S(1)}, f32[32,1024]{1,0:T(8,128)S(1)}, u32[]{:S(2)}, u32[]{:S(2)}) collective-permute-start(f32[32,1024]{1,0:T(8,128)S(1)} %shard_map.71.p0), channel_id=1, source_target_pairs={{32,0},{48,16},{64,32},{80,48},{96,64},{112,80},{0,96},{16,112},{3... | collective-permute-start | bytes 393224 | tf_op jit(solution)/shard_map/ppermute | solution.py:32
  78.3 8.8 %collective-permute-start.15 = (f32[32,1024]{1,0:T(8,128)S(1)}, f32[32,1024]{1,0:T(8,128)S(1)}, u32[]{:S(2)}, u32[]{:S(2)}) collective-permute-start(f32[32,1024]{1,0:T(8,128)S(1)} %shard_map.71.p0), channel_id=1, source_target_pairs={{96,0},{112,16},{0,32},{16,48},{32,64},{48,80},{64,96},{80,112},{9... | collective-permute-start | bytes 393224 | tf_op jit(solution)/shard_map/ppermute | solution.py:32
  78.3 8.8 %collective-permute-start.16 = (f32[32,1024]{1,0:T(8,128)S(1)}, f32[32,1024]{1,0:T(8,128)S(1)}, u32[]{:S(2)}, u32[]{:S(2)}) collective-permute-start(f32[32,1024]{1,0:T(8,128)S(1)} %shard_map.71.p0), channel_id=1, source_target_pairs={{64,0},{80,16},{96,32},{112,48},{0,64},{16,80},{32,96},{48,112},{6... | collective-permute-start | bytes 393224 | tf_op jit(solution)/shard_map/ppermute | solution.py:32
  80.0 85.4 %copy-start.3 = (s32[5]{0:T(128)}, s32[5]{0:T(128)S(1)}, u32[]{:S(2)}) copy-start(s32[5]{0:T(128)S(1)} %stack.101.place_ref) | copy-start | bytes 64
  90.0 4.3 %collective-permute-start.17 = (f32[32,1024]{1,0:T(8,128)S(1)}, f32[32,1024]{1,0:T(8,128)S(1)}, u32[]{:S(2)}, u32[]{:S(2)}) collective-permute-start(f32[32,1024]{1,0:T(8,128)S(1)} %get-tuple-element.30.p0), channel_id=1, source_target_pairs={{32,0},{48,16},{64,32},{80,48},{96,64},{112,80},{0,96},{16,112},{3... | collective-permute-start | bytes 393224 | tf_op jit(solution)/shard_map/ppermute | solution.py:32
  90.1 5.5 %collective-permute-start.18 = (f32[32,1024]{1,0:T(8,128)S(1)}, f32[32,1024]{1,0:T(8,128)S(1)}, u32[]{:S(2)}, u32[]{:S(2)}) collective-permute-start(f32[32,1024]{1,0:T(8,128)S(1)} %get-tuple-element.30.p0), channel_id=1, source_target_pairs={{96,0},{112,16},{0,32},{16,48},{32,64},{48,80},{64,96},{80,112},{9... | collective-permute-start | bytes 393224 | tf_op jit(solution)/shard_map/ppermute | solution.py:32
  91.5 6.4 %collective-permute-start.19 = (f32[32,1024]{1,0:T(8,128)S(1)}, f32[32,1024]{1,0:T(8,128)S(1)}, u32[]{:S(2)}, u32[]{:S(2)}) collective-permute-start(f32[32,1024]{1,0:T(8,128)S(1)} %get-tuple-element.30.p0), channel_id=1, source_target_pairs={{64,0},{80,16},{96,32},{112,48},{0,64},{16,80},{32,96},{48,112},{6... | collective-permute-start | bytes 393224 | tf_op jit(solution)/shard_map/ppermute | solution.py:32
  120.3 45.8 %all-to-all-start.2 = ((f32[16,1,64,512]{3,2,1,0:T(8,128)}), f32[16,1,64,512]{3,2,1,0:T(8,128)}, u32[]{:S(2)}, u32[]{:S(2)}) async-start(f32[16,1,64,512]{3,2,1,0:T(8,128)} %copy-done.1), calls=%async_computation.2 | async-start | bytes 4194304 | tf_op jit(solution)/shard_map/all_to_all | solution.py:312
  124.7 41.4 %collective-permute-start.22 = (f32[16,2,32,256]{3,2,1,0:T(8,128)}, f32[16,2,32,256]{3,2,1,0:T(8,128)}, u32[]{:S(2)}, u32[]{:S(2)}) collective-permute-start(f32[16,2,32,256]{3,2,1,0:T(8,128)} %all_to_all.25.refs_0_), channel_id=1, source_target_pairs={{32,0},{48,16},{64,32},{80,48},{96,64},{112,80},{0,96},{16,112},{3... | collective-permute-start | bytes 3145736 | tf_op jit(solution)/shard_map/ppermute | solution.py:32
  128.7 37.4 %collective-permute-start.24 = (f32[16,2,32,256]{3,2,1,0:T(8,128)}, f32[16,2,32,256]{3,2,1,0:T(8,128)}, u32[]{:S(2)}, u32[]{:S(2)}) collective-permute-start(f32[16,2,32,256]{3,2,1,0:T(8,128)} %all_to_all.25.refs_0_), channel_id=1, source_target_pairs={{96,0},{112,16},{0,32},{16,48},{32,64},{48,80},{64,96},{80,112},{9... | collective-permute-start | bytes 3145736 | tf_op jit(solution)/shard_map/ppermute | solution.py:32
  128.8 23.7 %collective-permute-start.28 = (f32[32,1024]{1,0:T(8,128)S(1)}, f32[32,1024]{1,0:T(8,128)S(1)}, u32[]{:S(2)}, u32[]{:S(2)}) collective-permute-start(f32[32,1024]{1,0:T(8,128)S(1)} %get-tuple-element.39.p0), channel_id=1, source_target_pairs={{32,0},{48,16},{64,32},{80,48},{96,64},{112,80},{0,96},{16,112},{3... | collective-permute-start | bytes 393224 | tf_op jit(solution)/shard_map/ppermute | solution.py:32
  131.4 23.8 %collective-permute-start.29 = (f32[32,1024]{1,0:T(8,128)S(1)}, f32[32,1024]{1,0:T(8,128)S(1)}, u32[]{:S(2)}, u32[]{:S(2)}) collective-permute-start(f32[32,1024]{1,0:T(8,128)S(1)} %get-tuple-element.39.p0), channel_id=1, source_target_pairs={{96,0},{112,16},{0,32},{16,48},{32,64},{48,80},{64,96},{80,112},{9... | collective-permute-start | bytes 393224 | tf_op jit(solution)/shard_map/ppermute | solution.py:32
  131.4 24.3 %collective-permute-start.30 = (f32[32,1024]{1,0:T(8,128)S(1)}, f32[32,1024]{1,0:T(8,128)S(1)}, u32[]{:S(2)}, u32[]{:S(2)}) collective-permute-start(f32[32,1024]{1,0:T(8,128)S(1)} %get-tuple-element.39.p0), channel_id=1, source_target_pairs={{64,0},{80,16},{96,32},{112,48},{0,64},{16,80},{32,96},{48,112},{6... | collective-permute-start | bytes 393224 | tf_op jit(solution)/shard_map/ppermute | solution.py:32
  158.6 3.8 %collective-permute-start.31 = (f32[32,1024]{1,0:T(8,128)S(1)}, f32[32,1024]{1,0:T(8,128)S(1)}, u32[]{:S(2)}, u32[]{:S(2)}) collective-permute-start(f32[32,1024]{1,0:T(8,128)S(1)} %get-tuple-element.42.p0), channel_id=1, source_target_pairs={{32,0},{48,16},{64,32},{80,48},{96,64},{112,80},{0,96},{16,112},{3... | collective-permute-start | bytes 393224 | tf_op jit(solution)/shard_map/ppermute | solution.py:32
  158.8 5.0 %collective-permute-start.32 = (f32[32,1024]{1,0:T(8,128)S(1)}, f32[32,1024]{1,0:T(8,128)S(1)}, u32[]{:S(2)}, u32[]{:S(2)}) collective-permute-start(f32[32,1024]{1,0:T(8,128)S(1)} %get-tuple-element.42.p0), channel_id=1, source_target_pairs={{96,0},{112,16},{0,32},{16,48},{32,64},{48,80},{64,96},{80,112},{9... | collective-permute-start | bytes 393224 | tf_op jit(solution)/shard_map/ppermute | solution.py:32
  160.1 5.4 %collective-permute-start.33 = (f32[32,1024]{1,0:T(8,128)S(1)}, f32[32,1024]{1,0:T(8,128)S(1)}, u32[]{:S(2)}, u32[]{:S(2)}) collective-permute-start(f32[32,1024]{1,0:T(8,128)S(1)} %get-tuple-element.42.p0), channel_id=1, source_target_pairs={{64,0},{80,16},{96,32},{112,48},{0,64},{16,80},{32,96},{48,112},{6... | collective-permute-start | bytes 393224 | tf_op jit(solution)/shard_map/ppermute | solution.py:32
  167.2 18.0 %all-to-all-start.3 = ((f32[16,2,32,256]{3,2,1,0:T(8,128)}), f32[16,2,32,256]{3,2,1,0:T(8,128)}, u32[]{:S(2)}, u32[]{:S(2)}) async-start(f32[16,2,32,256]{3,2,1,0:T(8,128)} %broadcast_in_dim.5), calls=%async_computation.3 | async-start | bytes 2097152 | tf_op jit(solution)/shard_map/all_to_all | solution.py:314
  173.4 25.6 %collective-permute-start.25 = (f32[16,2,32,256]{3,2,1,0:T(8,128)S(1)}, f32[16,2,32,256]{3,2,1,0:T(8,128)S(1)}, u32[]{:S(2)}, u32[]{:S(2)}) collective-permute-start(f32[16,2,32,256]{3,2,1,0:T(8,128)S(1)} %copy-done.4), channel_id=1, source_target_pairs={{64,0},{80,16},{96,32},{112,48},{0,64},{16,80},{32,96},{48,112},{6... | collective-permute-start | bytes 3145736 | tf_op jit(solution)/shard_map/ppermute | solution.py:32
  175.1 27.0 %collective-permute-start.21 = (f32[16,2,32,256]{3,2,1,0:T(8,128)S(1)}, f32[16,2,32,256]{3,2,1,0:T(8,128)S(1)}, u32[]{:S(2)}, u32[]{:S(2)}) collective-permute-start(f32[16,2,32,256]{3,2,1,0:T(8,128)S(1)} %copy-done.4), channel_id=1, source_target_pairs={{0,16},{16,0},{32,48},{48,32},{64,80},{80,64},{96,112},{112,96},{1... | collective-permute-start | bytes 3145736 | tf_op jit(solution)/shard_map/ppermute | solution.py:36
  185.2 72.5 %all-to-all-start.4 = ((f32[16,2,64,512]{3,2,1,0:T(8,128)}), f32[16,2,64,512]{3,2,1,0:T(8,128)}, u32[]{:S(2)}, u32[]{:S(2)}) async-start(f32[16,2,64,512]{3,2,1,0:T(8,128)} %copy-done), calls=%async_computation.4 | async-start | bytes 8388608 | tf_op jit(solution)/shard_map/all_to_all | solution.py:316
  189.8 12.3 %collective-permute-start.23 = (f32[16,2,32,256]{3,2,1,0:T(8,128)}, f32[16,2,32,256]{3,2,1,0:T(8,128)S(1)}, u32[]{:S(2)}, u32[]{:S(2)}) collective-permute-start(f32[16,2,32,256]{3,2,1,0:T(8,128)} %collective-permute-done.22.refs_2_), channel_id=1, source_target_pairs={{0,16},{16,0},{32,48},{48,32},{64,80},{80,64},{96,112},{112,96},{1... | collective-permute-start | bytes 3145736 | tf_op jit(solution)/shard_map/ppermute | solution.py:36
  198.9 4.0 %collective-permute-start.27 = (f32[16,2,32,256]{3,2,1,0:T(8,128)}, f32[16,2,32,256]{3,2,1,0:T(8,128)S(1)}, u32[]{:S(2)}, u32[]{:S(2)}) collective-permute-start(f32[16,2,32,256]{3,2,1,0:T(8,128)} %collective-permute-done.24.refs_6_), channel_id=1, source_target_pairs={{0,16},{16,0},{32,48},{48,32},{64,80},{80,64},{96,112},{112,96},{1... | collective-permute-start | bytes 3145736 | tf_op jit(solution)/shard_map/ppermute | solution.py:36
  199.0 5.2 %collective-permute-start.26 = (f32[16,2,32,256]{3,2,1,0:T(8,128)S(1)}, f32[16,2,32,256]{3,2,1,0:T(8,128)S(1)}, u32[]{:S(2)}, u32[]{:S(2)}) collective-permute-start(f32[16,2,32,256]{3,2,1,0:T(8,128)S(1)} %collective-permute-done.25.refs_4_), channel_id=1, source_target_pairs={{0,16},{16,0},{32,48},{48,32},{64,80},{80,64},{96,112},{112,96},{1... | collective-permute-start | bytes 3145736 | tf_op jit(solution)/shard_map/ppermute | solution.py:36
  200.6 25.1 %collective-permute-start.35 = (f32[16,2,32,256]{3,2,1,0:T(8,128)}, f32[16,2,32,256]{3,2,1,0:T(8,128)S(1)}, u32[]{:S(2)}, u32[]{:S(2)}) collective-permute-start(f32[16,2,32,256]{3,2,1,0:T(8,128)} %all-to-all-done.3.refs_0_), channel_id=1, source_target_pairs={{32,0},{48,16},{64,32},{80,48},{96,64},{112,80},{0,96},{16,112},{3... | collective-permute-start | bytes 3145736 | tf_op jit(solution)/shard_map/ppermute | solution.py:32
  202.0 26.0 %collective-permute-start.37 = (f32[16,2,32,256]{3,2,1,0:T(8,128)}, f32[16,2,32,256]{3,2,1,0:T(8,128)S(1)}, u32[]{:S(2)}, u32[]{:S(2)}) collective-permute-start(f32[16,2,32,256]{3,2,1,0:T(8,128)} %all-to-all-done.3.refs_0_), channel_id=1, source_target_pairs={{96,0},{112,16},{0,32},{16,48},{32,64},{48,80},{64,96},{80,112},{9... | collective-permute-start | bytes 3145736 | tf_op jit(solution)/shard_map/ppermute | solution.py:32
  228.0 43.7 %copy-start.16 = (f32[1,64,128]{2,1,0:T(8,128)S(1)}, f32[1,64,128]{2,1,0:T(8,128)}, u32[]{:S(2)}) copy-start(f32[1,64,128]{2,1,0:T(8,128)} %get-tuple-element.35) | copy-start | bytes 98308
  228.0 43.7 %copy-start.17 = (f32[1,64,128]{2,1,0:T(8,128)S(1)}, f32[1,64,128]{2,1,0:T(8,128)}, u32[]{:S(2)}) copy-start(f32[1,64,128]{2,1,0:T(8,128)} %get-tuple-element.38) | copy-start | bytes 98308
  228.0 25.3 %collective-permute-start.38 = (f32[16,2,32,256]{3,2,1,0:T(8,128)}, f32[16,2,32,256]{3,2,1,0:T(8,128)S(1)}, u32[]{:S(2)}, u32[]{:S(2)}) collective-permute-start(f32[16,2,32,256]{3,2,1,0:T(8,128)} %all-to-all-done.3.refs_0_), channel_id=1, source_target_pairs={{64,0},{80,16},{96,32},{112,48},{0,64},{16,80},{32,96},{48,112},{6... | collective-permute-start | bytes 3145736 | tf_op jit(solution)/shard_map/ppermute | solution.py:32
  228.0 27.3 %collective-permute-start.34 = (f32[16,2,32,256]{3,2,1,0:T(8,128)}, f32[16,2,32,256]{3,2,1,0:T(8,128)S(1)}, u32[]{:S(2)}, u32[]{:S(2)}) collective-permute-start(f32[16,2,32,256]{3,2,1,0:T(8,128)} %all-to-all-done.3.refs_0_), channel_id=1, source_target_pairs={{0,16},{16,0},{32,48},{48,32},{64,80},{80,64},{96,112},{112,96},{1... | collective-permute-start | bytes 3145736 | tf_op jit(solution)/shard_map/ppermute | solution.py:36
  229.1 26.2 %collective-permute-start.36 = (f32[16,2,32,256]{3,2,1,0:T(8,128)S(1)}, f32[16,2,32,256]{3,2,1,0:T(8,128)S(1)}, u32[]{:S(2)}, u32[]{:S(2)}) collective-permute-start(f32[16,2,32,256]{3,2,1,0:T(8,128)S(1)} %collective-permute-done.35.refs_2_), channel_id=1, source_target_pairs={{0,16},{16,0},{32,48},{48,32},{64,80},{80,64},{96,112},{112,96},{1... | collective-permute-start | bytes 3145736 | tf_op jit(solution)/shard_map/ppermute | solution.py:36
  229.2 26.1 %collective-permute-start.40 = (f32[16,2,32,256]{3,2,1,0:T(8,128)S(1)}, f32[16,2,32,256]{3,2,1,0:T(8,128)S(1)}, u32[]{:S(2)}, u32[]{:S(2)}) collective-permute-start(f32[16,2,32,256]{3,2,1,0:T(8,128)S(1)} %collective-permute-done.37.refs_6_), channel_id=1, source_target_pairs={{0,16},{16,0},{32,48},{48,32},{64,80},{80,64},{96,112},{112,96},{1... | collective-permute-start | bytes 3145736 | tf_op jit(solution)/shard_map/ppermute | solution.py:36
  253.3 4.4 %collective-permute-start.39 = (f32[16,2,32,256]{3,2,1,0:T(8,128)S(1)}, f32[16,2,32,256]{3,2,1,0:T(8,128)}, u32[]{:S(2)}, u32[]{:S(2)}) collective-permute-start(f32[16,2,32,256]{3,2,1,0:T(8,128)S(1)} %collective-permute-done.38.refs_4_), channel_id=1, source_target_pairs={{0,16},{16,0},{32,48},{48,32},{64,80},{80,64},{96,112},{112,96},{1... | collective-permute-start | bytes 3145736 | tf_op jit(solution)/shard_map/ppermute | solution.py:36
  (17 other events, 86.4 us)

commit v2 on v1

--- a/solution.py
+++ b/solution.py
@@ -41,13 +41,13 @@
     return jnp.stack([value, far[1], far[2], far[3]])
 
 
-def gather_blocks(set_a, set_b):
+def gather_blocks(set_a, set_b, *others):
     near_a = ring_stack(set_a, from_x)
     near_b = ring_stack(set_b, from_z)
-    near_a, near_b = lax.optimization_barrier((near_a, near_b))
+    near_a, near_b, *others = lax.optimization_barrier((near_a, near_b) + others)
     all_a = jnp.swapaxes(ring_stack(near_a, from_z), 0, 1)
     all_b = ring_stack(near_b, from_x)
-    return all_a.reshape((-1,) + set_a.shape), all_b.reshape((-1,) + set_b.shape)
+    return all_a.reshape((-1,) + set_a.shape), all_b.reshape((-1,) + set_b.shape), *others
 
 
 def split_bf16(value):
@@ -259,7 +259,9 @@
 
     set_a = jnp.concatenate([inverses[0:1], lower_blocks[0:1], inverses[1:2], lower_blocks[1:3]])
     set_b = jnp.concatenate([inverses[2:4], lower_blocks[3:6]])
-    got_a, got_b = gather_blocks(set_a, set_b)
+    split_0 = split_by_owner(trail_factor, 0, 2, 16)
+    split_2 = split_by_owner(trail_factor, 2, 2, 16)
+    got_a, got_b, right, split_0 = gather_blocks(set_a, set_b, right, split_0)
     far_a = from_core(got_a)
     far_b = from_core(got_b)
     inv = [(0, 0), (0, 2), (1, 0), (1, 1)]
@@ -269,14 +271,10 @@
         pair = ((got_a, far_a), (got_b, far_b))[where[0]]
         return [(v, where[1]) for v in pair]
 
-    split_0 = split_by_owner(trail_factor, 0, 1, 16)
-    split_1 = split_by_owner(trail_factor, 1, 1, 16)
-    split_2 = split_by_owner(trail_factor, 2, 2, 16)
-
     def after(value, *earlier):
         return lax.optimization_barrier((value,) + earlier)[0]
 
-    factor_0 = lax.all_to_all(after(split_0, got_a, got_b, split_1, split_2), "col", 0, 0)
+    factor_01 = lax.all_to_all(after(split_0, got_a, got_b), "col", 0, 0)
 
     x_shape = jax.ShapeDtypeStruct((share, order), F32)
     piece_shape = jax.ShapeDtypeStruct((share, order // 4), F32)
@@ -308,21 +306,23 @@
         return out
 
     block = (inverses.shape[1], inverses.shape[2])
-    x_01 = lax.all_to_all(after(spread(pieces[0:2]), factor_0), "col", 0, 0)
-    factor_1 = lax.all_to_all(after(split_1, x_01), "col", 0, 0)
+    def far_part(up, down):
+        cut = up.shape[0] // 2
+        return jnp.concatenate([from_y(up[:cut], 1), from_y(down[cut:], 3)])
+
+    x_01 = lax.all_to_all(after(spread(pieces[0:2]), factor_01, pieces[3]), "col", 0, 0)
     up_01, down_01 = from_y(x_01, 1), from_y(x_01, 3)
-    x_23 = lax.all_to_all(after(spread(pieces[2:4]), factor_1, up_01, down_01), "col", 0, 0)
-    across_01 = from_y(after(x_01, up_01, down_01), 2)
-    factor_2 = lax.all_to_all(after(split_2, x_23), "col", 0, 0)
+    x_23 = lax.all_to_all(after(spread(pieces[2:4]), x_01), "col", 0, 0)
+    factor_23 = lax.all_to_all(after(split_2, x_23, up_01, down_01), "col", 0, 0)
+    across_01 = far_part(up_01, down_01)
     xs_01 = core_pairs([x_01, up_01, across_01, down_01])
-    out, solved_0 = update(place, factor_0, 0, xs_01, 0, 1, trail_right, *block)
-    out, solved_1 = update(place, factor_1, 0, xs_01, 1, 1, out, *block)
+    out, solved_0 = update(place, factor_01, 0, xs_01, 0, 2, trail_right, *block)
     x_23 = after(x_23, across_01)
     up_23, down_23 = from_y(x_23, 1), from_y(x_23, 3)
-    across_23 = from_y(after(x_23, out, up_23, down_23), 2)
+    across_23 = far_part(after(up_23, out), down_23)
     xs_23 = core_pairs([x_23, up_23, across_23, down_23])
-    out, solved_2 = update(place, factor_2, 0, xs_23, 0, 2, out, *block)
-    return (jnp.concatenate([solved_0, solved_1, solved_2]), out)
+    out, solved_2 = update(place, factor_23, 0, xs_23, 0, 2, out, *block)
+    return (jnp.concatenate([solved_0, solved_2]), out)
 
 
 def solution(mesh):

time: 274 us -> 273 us (level)
  starting transfers between devices: 84.6 us -> 63.1 us
  waiting for transfers between devices: 98.8 us -> 112 us
  local copies, waits for them, and re-layouts: 16.2 us -> 27 us
  Pallas kernels: 50.9 us -> 41.2 us
  blocking collectives: 19.4 us -> 25.1 us
    ppermute x11, starting transfers between devices: 26.5 us -> 12.2 us  [from_core(): return lax.ppermute(value, 'row', CORE_PERM)]
    unnamed x42 -> x50, local copies, waits for them, and re-layouts: 7.81 us -> 18.1 us
    all_to_all x4 -> x3, waiting for transfers between devices: 2.41 us -> 9.98 us  [the longest x1 6.99 us: per_device(): x_23 = lax.all_to_all(after(spread(pieces[2:4]), x_01), 'col', 0, 0)]
    pallas_call x3 -> x2, Pallas kernels: 33.5 us -> 27.8 us  [update(): pl.pallas_call(update_kernel, grid_spec=grid_spec, out_shape=[jax.ShapeDt...]
    all_to_all x1, blocking collectives: 19.4 us -> 25.1 us  [per_device(): lax.all_to_all(after(spread(pieces[0:2]), factor_01, pieces[3]), 'col', 0...]
    ppermute x6, waiting for transfers between devices: 30.6 us -> 35.9 us  [from_z(): return lax.ppermute(value, 'col', col_perm(0, d))]
    ppermute x11, waiting for transfers between devices: 3.57 us -> 8.44 us  [from_core(): return lax.ppermute(value, 'row', CORE_PERM)]
    ppermute x6, starting transfers between devices: 10.7 us -> 6.13 us  [from_z(): return lax.ppermute(value, 'col', col_perm(0, d))]
  transfers between devices with their start and end apart: 45 -> 46, of which waited for: 26 -> 24; matrix products, arithmetic and copies ran while one was open for 2% -> 3% of each run, Pallas kernels for 14% -> 10%
where the time goes in v2:
time: 273 us; the launch traced here: 272 us
  waiting for transfers between devices  112 us (41%)
  starting transfers between devices  63.1 us (23%)
  Pallas kernels  41.2 us (15%)
  local copies, waits for them, and re-layouts  27 us (10%)
  blocking collectives  25.1 us (9%)
    ppermute x20, waiting for transfers between devices, from_y(): return lax.ppermute(value, 'row', y_perm(d))  57.8 us
    ppermute x6, waiting for transfers between devices, from_z(): return lax.ppermute(value, 'col', col_perm(0, d))  35.9 us
    pallas_call x2, Pallas kernels, update(): pl.pallas_call(update_kernel, grid_spec=grid_spec, out_shape=[jax.ShapeDt...  27.8 us
    all_to_all x1, blocking collectives, per_device(): lax.all_to_all(after(spread(pieces[0:2]), factor_01, pieces[3]), 'col', 0...  25.1 us
    ppermute x20, starting transfers between devices, from_y(): return lax.ppermute(value, 'row', y_perm(d))  20.1 us
    unnamed x50, local copies, waits for them, and re-layouts  18.1 us
    ppermute x11, starting transfers between devices, from_core(): return lax.ppermute(value, 'row', CORE_PERM)  12.2 us
    pallas_call x8, Pallas kernels, small_call(): pl.pallas_call(kernel, grid_spec=pltpu.PrefetchScalarGridSpec(num_scalar_...  11.4 us
  transfers between devices with their start and end apart: 46, of which 24 were waited for; matrix products, arithmetic and copies ran while one was open for 3% of the time, Pallas kernels for 10%

profile of v2, /device:TPU:1, one launch (start us, length us, event | category | flops | bytes accessed | tf_op | source)
XLA Modules:
  0.0 272.0 jit_solution(242913299003509602)
XLA Ops:
  3.1 3.4 %collective-permute-start = (f32[5,64,128]{2,1,0:T(8,128)S(1)}, f32[5,64,128]{2,1,0:T(8,128)S(1)}, u32[]{:S(2)}, u32[]{:S(2)}) collective-permute-start(f32[5,64,128]{2,1,0:T(8,128)S(1)} %get-tuple-element.51), channel_id=1, source_target_pairs={{4,0},{5,1},{6,2},{7,3},{8,4},{9,5},{10,6},{11,7},{12,8},{13,9},{1... | collective-permute-start | bytes 491528 | tf_op jit(solution)/shard_map/ppermute | solution.py:24
  9.0 1.6 collective-permute-start.6
  10.6 3.8 %collective-permute-start.3 = (f32[5,64,128]{2,1,0:T(8,128)S(1)}, f32[5,64,128]{2,1,0:T(8,128)S(1)}, u32[]{:S(2)}, u32[]{:S(2)}) collective-permute-start(f32[5,64,128]{2,1,0:T(8,128)S(1)} %get-tuple-element.49), channel_id=1, source_target_pairs={{1,0},{2,1},{3,2},{0,3},{5,4},{6,5},{7,6},{4,7},{9,8},{10,9},{11,1... | collective-permute-start | bytes 491528 | tf_op jit(solution)/shard_map/ppermute | solution.py:28
  14.5 3.4 %copy-done.5 = f32[4,64,8192]{2,1,0:T(8,128)S(1)} copy-done((f32[4,64,8192]{2,1,0:T(8,128)S(1)}, f32[4,64,8192]{2,1,0:T(8,128)}, u32[]{:S(2)}) %copy-start.5) | copy-done | bytes 8388632
  19.8 6.2 %collective-permute-done.4 = f32[5,64,128]{2,1,0:T(8,128)S(1)} collective-permute-done((f32[5,64,128]{2,1,0:T(8,128)S(1)}, f32[5,64,128]{2,1,0:T(8,128)S(1)}, u32[]{:S(2)}, u32[]{:S(2)}) %collective-permute-start.4) | collective-permute-done | bytes 163872 | tf_op jit(solution)/shard_map/ppermute | solution.py:28
  26.0 3.7 %collective-permute-done.5 = f32[5,64,128]{2,1,0:T(8,128)S(1)} collective-permute-done((f32[5,64,128]{2,1,0:T(8,128)S(1)}, f32[5,64,128]{2,1,0:T(8,128)S(1)}, u32[]{:S(2)}, u32[]{:S(2)}) %collective-permute-start.5) | collective-permute-done | bytes 163872 | tf_op jit(solution)/shard_map/ppermute | solution.py:28
  31.3 2.1 collective-permute-start.10
  34.6 10.8 %collective-permute-done.7 = f32[4,5,64,128]{3,2,1,0:T(8,128)S(1)} collective-permute-done((f32[4,5,64,128]{3,2,1,0:T(8,128)S(1)}, f32[4,5,64,128]{3,2,1,0:T(8,128)S(1)}, u32[]{:S(2)}, u32[]{:S(2)}) %collective-permute-start.7) | collective-permute-done | bytes 655392 | tf_op jit(solution)/shard_map/ppermute | solution.py:28
  45.4 1.5 collective-permute-start.12
  46.9 15.2 %collective-permute-done.9 = f32[4,5,64,128]{3,2,1,0:T(8,128)S(1)} collective-permute-done((f32[4,5,64,128]{3,2,1,0:T(8,128)S(1)}, f32[4,5,64,128]{3,2,1,0:T(8,128)S(1)}, u32[]{:S(2)}, u32[]{:S(2)}) %collective-permute-start.9) | collective-permute-done | bytes 655392 | tf_op jit(solution)/shard_map/ppermute | solution.py:28
  62.5 1.6 copy.9
  64.5 7.2 %all-to-all-start = ((f32[16,2,64,512]{3,2,1,0:T(8,128)}), f32[16,2,64,512]{3,2,1,0:T(8,128)}, u32[]{:S(2)}, u32[]{:S(2)}) async-start(f32[16,2,64,512]{3,2,1,0:T(8,128)} %copy-done.7), calls=%async_computation | async-start | bytes 8388608 | tf_op jit(solution)/shard_map/all_to_all | solution.py:277
  72.7 7.5 %collective-permute-done.13.inv_far.low_far = f32[16,5,64,128]{3,2,1,0:T(8,128)S(1)} collective-permute-done((f32[16,5,64,128]{3,2,1,0:T(8,128)}, f32[16,5,64,128]{3,2,1,0:T(8,128)S(1)}, u32[]{:S(2)}, u32[]{:S(2)}) %collective-permute-start.13) | collective-permute-done | bytes 2621472 | tf_op jit(solution)/shard_map/ppermute | solution.py:36
  80.2 2.7 copy-done
  83.5 2.8 %collective-permute-start.14 = (f32[32,1024]{1,0:T(8,128)S(1)}, f32[32,1024]{1,0:T(8,128)S(1)}, u32[]{:S(2)}, u32[]{:S(2)}) collective-permute-start(f32[32,1024]{1,0:T(8,128)S(1)} %shard_map.69.p0), channel_id=1, source_target_pairs={{32,0},{48,16},{64,32},{80,48},{96,64},{112,80},{0,96},{16,112},{3... | collective-permute-start | bytes 393224 | tf_op jit(solution)/shard_map/ppermute | solution.py:32
  86.3 1.6 collective-permute-start.16
  88.8 6.2 %collective-permute-done.15.p2 = f32[32,1024]{1,0:T(8,128)S(1)} collective-permute-done((f32[32,1024]{1,0:T(8,128)S(1)}, f32[32,1024]{1,0:T(8,128)S(1)}, u32[]{:S(2)}, u32[]{:S(2)}) %collective-permute-start.15) | collective-permute-done | bytes 131104 | tf_op jit(solution)/shard_map/ppermute | solution.py:32
  95.0 1.7 copy-done.1
  96.8 1.7 copy-done.4
  102.2 2.0 collective-permute-done.17.p1
  105.5 2.3 collective-permute-done.19.p3
  107.8 2.6 shard_map.72
  110.4 2.0 collective-permute-start.21
  116.6 3.1 %collective-permute-done.22.p2 = f32[32,1024]{1,0:T(8,128)S(1)} collective-permute-done((f32[32,1024]{1,0:T(8,128)S(1)}, f32[32,1024]{1,0:T(8,128)S(1)}, u32[]{:S(2)}, u32[]{:S(2)}) %collective-permute-start.22) | collective-permute-done | bytes 131104 | tf_op jit(solution)/shard_map/ppermute | solution.py:32
  119.7 2.9 %shard_map.75 = (f32[32,1024]{1,0:T(8,128)}, f32[32,256]{1,0:T(8,128)S(1)}, f32[32,1024]{1,0:T(8,128)S(1)}) custom-call(s32[5]{0:T(128)S(1)} %stack.101.place_ref, f32[32,1024]{1,0:T(8,128)S(1)} %get-tuple-element.33.p0, f32[32,1024]{1,0:T(8,128)S(1)} %collective-permute-done.21.p1, f32[32,1024]{1,0:T(8,128)S(1)} %collective-permute-done.22.p2, ...), custom_call_target="tpu_custom_call" | custom-call | tf_op jit(solution)/shard_map/pallas_call | solution.py:133
  122.6 1.8 collective-permute-start.24
  126.4 4.4 %collective-permute-done.25.p2 = f32[32,1024]{1,0:T(8,128)S(1)} collective-permute-done((f32[32,1024]{1,0:T(8,128)S(1)}, f32[32,1024]{1,0:T(8,128)S(1)}, u32[]{:S(2)}, u32[]{:S(2)}) %collective-permute-start.25) | collective-permute-done | bytes 131104 | tf_op jit(solution)/shard_map/ppermute | solution.py:32
  131.5 3.0 %all-to-all-done.f_ref = f32[16,2,64,512]{3,2,1,0:T(8,128)} async-done(((f32[16,2,64,512]{3,2,1,0:T(8,128)}), f32[16,2,64,512]{3,2,1,0:T(8,128)}, u32[]{:S(2)}, u32[]{:S(2)}) %all-to-all-start) | async-done | bytes 4194336 | tf_op jit(solution)/shard_map/all_to_all | solution.py:277
  134.6 25.1 %all_to_all.20.refs_0_ = f32[16,2,32,256]{3,2,1,0:T(8,128)S(1)} all-to-all(f32[16,2,32,256]{3,2,1,0:T(8,128)S(1)} %broadcast_in_dim.4), channel_id=1, replica_groups=mesh['row'=8,'col'=16] {'col'}, dimensions={0} | all-to-all | bytes 2097152 | tf_op jit(solution)/shard_map/all_to_all | solution.py:313
  159.7 2.7 %collective-permute-start.28 = (f32[16,2,32,256]{3,2,1,0:T(8,128)S(1)}, f32[16,2,32,256]{3,2,1,0:T(8,128)}, u32[]{:S(2)}, u32[]{:S(2)}) collective-permute-start(f32[16,2,32,256]{3,2,1,0:T(8,128)S(1)} %all_to_all.20.refs_0_), channel_id=1, source_target_pairs={{32,0},{48,16},{64,32},{80,48},{96,64},{112,80},{0,96},{16,112},{3... | collective-permute-start | bytes 3145736 | tf_op jit(solution)/shard_map/ppermute | solution.py:32
  163.5 3.7 %all-to-all-start.2 = ((f32[16,2,32,256]{3,2,1,0:T(8,128)}), f32[16,2,32,256]{3,2,1,0:T(8,128)S(1)}, u32[]{:S(2)}, u32[]{:S(2)}) async-start(f32[16,2,32,256]{3,2,1,0:T(8,128)} %broadcast_in_dim.5), calls=%async_computation.2 | async-start | bytes 2097152 | tf_op jit(solution)/shard_map/all_to_all | solution.py:315
  167.2 3.4 %copy-done.6 = f32[4,64,8192]{2,1,0:T(8,128)S(1)} copy-done((f32[4,64,8192]{2,1,0:T(8,128)S(1)}, f32[4,64,8192]{2,1,0:T(8,128)}, u32[]{:S(2)}) %copy-start.6) | copy-done | bytes 8388632
  171.6 2.1 copy-done.8
  173.7 7.0 %all-to-all-done.2.refs_0_ = f32[16,2,32,256]{3,2,1,0:T(8,128)S(1)} async-done(((f32[16,2,32,256]{3,2,1,0:T(8,128)}), f32[16,2,32,256]{3,2,1,0:T(8,128)S(1)}, u32[]{:S(2)}, u32[]{:S(2)}) %all-to-all-start.2) | async-done | bytes 1048608 | tf_op jit(solution)/shard_map/all_to_all | solution.py:315
  181.8 3.2 %collective-permute-done.31.refs_6_ = f32[16,2,32,256]{3,2,1,0:T(8,128)} collective-permute-done((f32[16,2,32,256]{3,2,1,0:T(8,128)S(1)}, f32[16,2,32,256]{3,2,1,0:T(8,128)}, u32[]{:S(2)}, u32[]{:S(2)}) %collective-permute-start.31) | collective-permute-done | bytes 1048608 | tf_op jit(solution)/shard_map/ppermute | solution.py:32
  185.1 4.5 %all-to-all-start.3 = ((f32[16,2,64,512]{3,2,1,0:T(8,128)}), f32[16,2,64,512]{3,2,1,0:T(8,128)}, u32[]{:S(2)}, u32[]{:S(2)}) async-start(f32[16,2,64,512]{3,2,1,0:T(8,128)} %copy-done.8), calls=%async_computation.3 | async-start | bytes 8388608 | tf_op jit(solution)/shard_map/all_to_all | solution.py:316
  189.6 4.3 %collective-permute-start.27 = (f32[16,2,32,256]{3,2,1,0:T(8,128)S(1)}, f32[16,2,32,256]{3,2,1,0:T(8,128)S(1)}, u32[]{:S(2)}, u32[]{:S(2)}) collective-permute-start(f32[16,2,32,256]{3,2,1,0:T(8,128)S(1)} %all_to_all.20.refs_0_), channel_id=1, source_target_pairs={{0,16},{16,0},{32,48},{48,32},{64,80},{80,64},{96,112},{112,96},{1... | collective-permute-start | bytes 3145736 | tf_op jit(solution)/shard_map/ppermute | solution.py:36
  196.2 1.5 collective-permute-start.32
  198.3 10.5 %collective-permute-done.30 = f32[8,2,32,256]{3,2,1,0:T(8,128)S(1)} collective-permute-done((f32[8,2,32,256]{3,2,1,0:T(8,128)S(1)}, f32[8,2,32,256]{3,2,1,0:T(8,128)S(1)}, u32[]{:S(2)}, u32[]{:S(2)}) %collective-permute-start.30) | collective-permute-done | bytes 524320 | tf_op jit(solution)/shard_map/ppermute | solution.py:32
  208.8 2.0 collective-permute-done.32
  212.0 1.5 collective-permute-start.39
  214.8 13.9 %shard_map.77 = (f32[512,1024]{1,0:T(8,128)}, f32[2,64,128]{2,1,0:T(8,128)}) custom-call(s32[5]{0:T(128)} %copy-done.9, f32[16,2,64,512]{3,2,1,0:T(8,128)} %all-to-all-done.f_ref, f32[16,2,32,256]{3,2,1,0:T(8,128)} %copy-done.11, f32[16,2,32,256]{3,2,1,0:T(8,128)} %copy-done.16, f32[16,2,32,256]{3,2,1,0:T(8,128)} %collective-permute-done.28.refs_2_, ...), custom_call_target="tpu_custom_call" | custom-call | tf_op jit(solution)/shard_map/pallas_call | solution.py:230
  228.6 8.1 %collective-permute-done.36.refs_2_ = f32[16,2,32,256]{3,2,1,0:T(8,128)S(1)} collective-permute-done((f32[16,2,32,256]{3,2,1,0:T(8,128)S(1)}, f32[16,2,32,256]{3,2,1,0:T(8,128)S(1)}, u32[]{:S(2)}, u32[]{:S(2)}) %collective-permute-start.36) | collective-permute-done | bytes 1048608 | tf_op jit(solution)/shard_map/ppermute | solution.py:32
  240.3 9.3 %collective-permute-done.38 = f32[8,2,32,256]{3,2,1,0:T(8,128)S(1)} collective-permute-done((f32[8,2,32,256]{3,2,1,0:T(8,128)S(1)}, f32[8,2,32,256]{3,2,1,0:T(8,128)S(1)}, u32[]{:S(2)}, u32[]{:S(2)}) %collective-permute-start.38) | collective-permute-done | bytes 524320 | tf_op jit(solution)/shard_map/ppermute | solution.py:32
  249.6 2.6 collective-permute-done.40
  252.3 1.8 collective-permute-start.41
  256.5 13.9 %shard_map.79 = (f32[512,1024]{1,0:T(8,128)}, f32[2,64,128]{2,1,0:T(8,128)}) custom-call(s32[5]{0:T(128)} %copy-done.9, f32[16,2,64,512]{3,2,1,0:T(8,128)} %all-to-all-done.3.f_ref, f32[16,2,32,256]{3,2,1,0:T(8,128)} %copy-done.10, f32[16,2,32,256]{3,2,1,0:T(8,128)} %copy-done.17, f32[16,2,32,256]{3,2,1,0:T(8,128)} %copy-done.12, ...), custom_call_target="tpu_custom_call" | custom-call | tf_op jit(solution)/shard_map/pallas_call | solution.py:230
  270.5 1.5 pad_maximum_fusion.6
  (136 shorter events, 39.3 us)
Async XLA Ops:
  3.1 15.9 %collective-permute-start = (f32[5,64,128]{2,1,0:T(8,128)S(1)}, f32[5,64,128]{2,1,0:T(8,128)S(1)}, u32[]{:S(2)}, u32[]{:S(2)}) collective-permute-start(f32[5,64,128]{2,1,0:T(8,128)S(1)} %get-tuple-element.51), channel_id=1, source_target_pairs={{4,0},{5,1},{6,2},{7,3},{8,4},{9,5},{10,6},{11,7},{12,8},{13,9},{1... | collective-permute-start | bytes 491528 | tf_op jit(solution)/shard_map/ppermute | solution.py:24
  6.5 13.2 %collective-permute-start.1 = (f32[5,64,128]{2,1,0:T(8,128)S(1)}, f32[5,64,128]{2,1,0:T(8,128)S(1)}, u32[]{:S(2)}, u32[]{:S(2)}) collective-permute-start(f32[5,64,128]{2,1,0:T(8,128)S(1)} %get-tuple-element.51), channel_id=1, source_target_pairs={{8,0},{9,1},{10,2},{11,3},{12,4},{13,5},{14,6},{15,7},{0,8},{1,9},... | collective-permute-start | bytes 491528 | tf_op jit(solution)/shard_map/ppermute | solution.py:24
  7.0 12.7 %collective-permute-start.2 = (f32[5,64,128]{2,1,0:T(8,128)S(1)}, f32[5,64,128]{2,1,0:T(8,128)S(1)}, u32[]{:S(2)}, u32[]{:S(2)}) collective-permute-start(f32[5,64,128]{2,1,0:T(8,128)S(1)} %get-tuple-element.51), channel_id=1, source_target_pairs={{12,0},{13,1},{14,2},{15,3},{0,4},{1,5},{2,6},{3,7},{4,8},{5,9},{6... | collective-permute-start | bytes 491528 | tf_op jit(solution)/shard_map/ppermute | solution.py:24
  9.0 10.0 %collective-permute-start.6 = (f32[4,32,128]{2,1,0:T(8,128)S(1)}, f32[4,32,128]{2,1,0:T(8,128)S(1)}, u32[]{:S(2)}, u32[]{:S(2)}) collective-permute-start(f32[4,32,128]{2,1,0:T(8,128)S(1)} %bitcast.64), channel_id=1, source_target_pairs={{0,16},{16,0},{32,48},{48,32},{64,80},{80,64},{96,112},{112,96},{1... | collective-permute-start | bytes 196616 | tf_op jit(solution)/shard_map/ppermute | solution.py:36
  10.6 9.2 %collective-permute-start.3 = (f32[5,64,128]{2,1,0:T(8,128)S(1)}, f32[5,64,128]{2,1,0:T(8,128)S(1)}, u32[]{:S(2)}, u32[]{:S(2)}) collective-permute-start(f32[5,64,128]{2,1,0:T(8,128)S(1)} %get-tuple-element.49), channel_id=1, source_target_pairs={{1,0},{2,1},{3,2},{0,3},{5,4},{6,5},{7,6},{4,7},{9,8},{10,9},{11,1... | collective-permute-start | bytes 491528 | tf_op jit(solution)/shard_map/ppermute | solution.py:28
  18.9 43.6 %copy-start.7 = (f32[16,2,64,512]{3,2,1,0:T(8,128)}, f32[16,2,64,512]{3,2,1,0:T(8,128)S(1)}, u32[]{:S(2)}) copy-start(f32[16,2,64,512]{3,2,1,0:T(8,128)S(1)} %shard_map.68) | copy-start | bytes 12582916
  18.9 7.1 %collective-permute-start.4 = (f32[5,64,128]{2,1,0:T(8,128)S(1)}, f32[5,64,128]{2,1,0:T(8,128)S(1)}, u32[]{:S(2)}, u32[]{:S(2)}) collective-permute-start(f32[5,64,128]{2,1,0:T(8,128)S(1)} %get-tuple-element.49), channel_id=1, source_target_pairs={{2,0},{3,1},{0,2},{1,3},{6,4},{7,5},{4,6},{5,7},{10,8},{11,9},{8,1... | collective-permute-start | bytes 491528 | tf_op jit(solution)/shard_map/ppermute | solution.py:28
  19.0 10.7 %collective-permute-start.5 = (f32[5,64,128]{2,1,0:T(8,128)S(1)}, f32[5,64,128]{2,1,0:T(8,128)S(1)}, u32[]{:S(2)}, u32[]{:S(2)}) collective-permute-start(f32[5,64,128]{2,1,0:T(8,128)S(1)} %get-tuple-element.49), channel_id=1, source_target_pairs={{3,0},{0,1},{1,2},{2,3},{7,4},{4,5},{5,6},{6,7},{11,8},{8,9},{9,10... | collective-permute-start | bytes 491528 | tf_op jit(solution)/shard_map/ppermute | solution.py:28
  29.8 15.6 %collective-permute-start.7 = (f32[4,5,64,128]{3,2,1,0:T(8,128)S(1)}, f32[4,5,64,128]{3,2,1,0:T(8,128)S(1)}, u32[]{:S(2)}, u32[]{:S(2)}) collective-permute-start(f32[4,5,64,128]{3,2,1,0:T(8,128)S(1)} %pad_maximum_fusion.1), channel_id=1, source_target_pairs={{1,0},{2,1},{3,2},{0,3},{5,4},{6,5},{7,6},{4,7},{9,8},{10,9},{11,1... | collective-permute-start | bytes 1966088 | tf_op jit(solution)/shard_map/ppermute | solution.py:28
  29.9 17.0 %collective-permute-start.8 = (f32[4,5,64,128]{3,2,1,0:T(8,128)S(1)}, f32[4,5,64,128]{3,2,1,0:T(8,128)S(1)}, u32[]{:S(2)}, u32[]{:S(2)}) collective-permute-start(f32[4,5,64,128]{3,2,1,0:T(8,128)S(1)} %pad_maximum_fusion.1), channel_id=1, source_target_pairs={{2,0},{3,1},{0,2},{1,3},{6,4},{7,5},{4,6},{5,7},{10,8},{11,9},{8,1... | collective-permute-start | bytes 1966088 | tf_op jit(solution)/shard_map/ppermute | solution.py:28
  30.4 31.8 %collective-permute-start.9 = (f32[4,5,64,128]{3,2,1,0:T(8,128)S(1)}, f32[4,5,64,128]{3,2,1,0:T(8,128)S(1)}, u32[]{:S(2)}, u32[]{:S(2)}) collective-permute-start(f32[4,5,64,128]{3,2,1,0:T(8,128)S(1)} %pad_maximum_fusion.1), channel_id=1, source_target_pairs={{3,0},{0,1},{1,2},{2,3},{7,4},{4,5},{5,6},{6,7},{11,8},{8,9},{9,10... | collective-permute-start | bytes 1966088 | tf_op jit(solution)/shard_map/ppermute | solution.py:28
  31.3 32.8 %collective-permute-start.10 = (f32[4,5,64,128]{3,2,1,0:T(8,128)S(1)}, f32[4,5,64,128]{3,2,1,0:T(8,128)S(1)}, u32[]{:S(2)}, u32[]{:S(2)}) collective-permute-start(f32[4,5,64,128]{3,2,1,0:T(8,128)S(1)} %pad_maximum_fusion.2), channel_id=1, source_target_pairs={{4,0},{5,1},{6,2},{7,3},{8,4},{9,5},{10,6},{11,7},{12,8},{13,9},{1... | collective-permute-start | bytes 1966088 | tf_op jit(solution)/shard_map/ppermute | solution.py:24
  33.4 30.7 %collective-permute-start.11 = (f32[4,5,64,128]{3,2,1,0:T(8,128)S(1)}, f32[4,5,64,128]{3,2,1,0:T(8,128)S(1)}, u32[]{:S(2)}, u32[]{:S(2)}) collective-permute-start(f32[4,5,64,128]{3,2,1,0:T(8,128)S(1)} %pad_maximum_fusion.2), channel_id=1, source_target_pairs={{8,0},{9,1},{10,2},{11,3},{12,4},{13,5},{14,6},{15,7},{0,8},{1,9},... | collective-permute-start | bytes 1966088 | tf_op jit(solution)/shard_map/ppermute | solution.py:24
  45.4 18.9 %collective-permute-start.12 = (f32[4,5,64,128]{3,2,1,0:T(8,128)S(1)}, f32[4,5,64,128]{3,2,1,0:T(8,128)S(1)}, u32[]{:S(2)}, u32[]{:S(2)}) collective-permute-start(f32[4,5,64,128]{3,2,1,0:T(8,128)S(1)} %pad_maximum_fusion.2), channel_id=1, source_target_pairs={{12,0},{13,1},{14,2},{15,3},{0,4},{1,5},{2,6},{3,7},{4,8},{5,9},{6... | collective-permute-start | bytes 1966088 | tf_op jit(solution)/shard_map/ppermute | solution.py:24
  64.5 69.9 %all-to-all-start = ((f32[16,2,64,512]{3,2,1,0:T(8,128)}), f32[16,2,64,512]{3,2,1,0:T(8,128)}, u32[]{:S(2)}, u32[]{:S(2)}) async-start(f32[16,2,64,512]{3,2,1,0:T(8,128)} %copy-done.7), calls=%async_computation | async-start | bytes 8388608 | tf_op jit(solution)/shard_map/all_to_all | solution.py:277
  71.8 8.4 %collective-permute-start.13 = (f32[16,5,64,128]{3,2,1,0:T(8,128)}, f32[16,5,64,128]{3,2,1,0:T(8,128)S(1)}, u32[]{:S(2)}, u32[]{:S(2)}) collective-permute-start(f32[16,5,64,128]{3,2,1,0:T(8,128)} %bitcast.39), channel_id=1, source_target_pairs={{0,16},{16,0},{32,48},{48,32},{64,80},{80,64},{96,112},{112,96},{1... | collective-permute-start | bytes 7864328 | tf_op jit(solution)/shard_map/ppermute | solution.py:36
  72.6 29.6 %collective-permute-start.20 = (f32[16,5,64,128]{3,2,1,0:T(8,128)S(1)}, f32[16,5,64,128]{3,2,1,0:T(8,128)}, u32[]{:S(2)}, u32[]{:S(2)}) collective-permute-start(f32[16,5,64,128]{3,2,1,0:T(8,128)S(1)} %bitcast.33), channel_id=1, source_target_pairs={{0,16},{16,0},{32,48},{48,32},{64,80},{80,64},{96,112},{112,96},{1... | collective-permute-start | bytes 7864328 | tf_op jit(solution)/shard_map/ppermute | solution.py:36
  83.5 5.3 %collective-permute-start.14 = (f32[32,1024]{1,0:T(8,128)S(1)}, f32[32,1024]{1,0:T(8,128)S(1)}, u32[]{:S(2)}, u32[]{:S(2)}) collective-permute-start(f32[32,1024]{1,0:T(8,128)S(1)} %shard_map.69.p0), channel_id=1, source_target_pairs={{32,0},{48,16},{64,32},{80,48},{96,64},{112,80},{0,96},{16,112},{3... | collective-permute-start | bytes 393224 | tf_op jit(solution)/shard_map/ppermute | solution.py:32
  86.3 8.7 %collective-permute-start.15 = (f32[32,1024]{1,0:T(8,128)S(1)}, f32[32,1024]{1,0:T(8,128)S(1)}, u32[]{:S(2)}, u32[]{:S(2)}) collective-permute-start(f32[32,1024]{1,0:T(8,128)S(1)} %shard_map.69.p0), channel_id=1, source_target_pairs={{96,0},{112,16},{0,32},{16,48},{32,64},{48,80},{64,96},{80,112},{9... | collective-permute-start | bytes 393224 | tf_op jit(solution)/shard_map/ppermute | solution.py:32
  86.3 8.7 %collective-permute-start.16 = (f32[32,1024]{1,0:T(8,128)S(1)}, f32[32,1024]{1,0:T(8,128)S(1)}, u32[]{:S(2)}, u32[]{:S(2)}) collective-permute-start(f32[32,1024]{1,0:T(8,128)S(1)} %shard_map.69.p0), channel_id=1, source_target_pairs={{64,0},{80,16},{96,32},{112,48},{0,64},{16,80},{32,96},{48,112},{6... | collective-permute-start | bytes 393224 | tf_op jit(solution)/shard_map/ppermute | solution.py:32
  99.9 4.3 %collective-permute-start.17 = (f32[32,1024]{1,0:T(8,128)S(1)}, f32[32,1024]{1,0:T(8,128)S(1)}, u32[]{:S(2)}, u32[]{:S(2)}) collective-permute-start(f32[32,1024]{1,0:T(8,128)S(1)} %get-tuple-element.30.p0), channel_id=1, source_target_pairs={{32,0},{48,16},{64,32},{80,48},{96,64},{112,80},{0,96},{16,112},{3... | collective-permute-start | bytes 393224 | tf_op jit(solution)/shard_map/ppermute | solution.py:32
  100.0 5.5 %collective-permute-start.18 = (f32[32,1024]{1,0:T(8,128)S(1)}, f32[32,1024]{1,0:T(8,128)S(1)}, u32[]{:S(2)}, u32[]{:S(2)}) collective-permute-start(f32[32,1024]{1,0:T(8,128)S(1)} %get-tuple-element.30.p0), channel_id=1, source_target_pairs={{96,0},{112,16},{0,32},{16,48},{32,64},{48,80},{64,96},{80,112},{9... | collective-permute-start | bytes 393224 | tf_op jit(solution)/shard_map/ppermute | solution.py:32
  101.5 6.4 %collective-permute-start.19 = (f32[32,1024]{1,0:T(8,128)S(1)}, f32[32,1024]{1,0:T(8,128)S(1)}, u32[]{:S(2)}, u32[]{:S(2)}) collective-permute-start(f32[32,1024]{1,0:T(8,128)S(1)} %get-tuple-element.30.p0), channel_id=1, source_target_pairs={{64,0},{80,16},{96,32},{112,48},{0,64},{16,80},{32,96},{48,112},{6... | collective-permute-start | bytes 393224 | tf_op jit(solution)/shard_map/ppermute | solution.py:32
  110.4 6.2 %collective-permute-start.21 = (f32[32,1024]{1,0:T(8,128)S(1)}, f32[32,1024]{1,0:T(8,128)S(1)}, u32[]{:S(2)}, u32[]{:S(2)}) collective-permute-start(f32[32,1024]{1,0:T(8,128)S(1)} %get-tuple-element.33.p0), channel_id=1, source_target_pairs={{32,0},{48,16},{64,32},{80,48},{96,64},{112,80},{0,96},{16,112},{3... | collective-permute-start | bytes 393224 | tf_op jit(solution)/shard_map/ppermute | solution.py:32
  112.4 7.3 %collective-permute-start.22 = (f32[32,1024]{1,0:T(8,128)S(1)}, f32[32,1024]{1,0:T(8,128)S(1)}, u32[]{:S(2)}, u32[]{:S(2)}) collective-permute-start(f32[32,1024]{1,0:T(8,128)S(1)} %get-tuple-element.33.p0), channel_id=1, source_target_pairs={{96,0},{112,16},{0,32},{16,48},{32,64},{48,80},{64,96},{80,112},{9... | collective-permute-start | bytes 393224 | tf_op jit(solution)/shard_map/ppermute | solution.py:32
  112.4 7.3 %collective-permute-start.23 = (f32[32,1024]{1,0:T(8,128)S(1)}, f32[32,1024]{1,0:T(8,128)S(1)}, u32[]{:S(2)}, u32[]{:S(2)}) collective-permute-start(f32[32,1024]{1,0:T(8,128)S(1)} %get-tuple-element.33.p0), channel_id=1, source_target_pairs={{64,0},{80,16},{96,32},{112,48},{0,64},{16,80},{32,96},{48,112},{6... | collective-permute-start | bytes 393224 | tf_op jit(solution)/shard_map/ppermute | solution.py:32
  122.6 3.8 %collective-permute-start.24 = (f32[32,1024]{1,0:T(8,128)S(1)}, f32[32,1024]{1,0:T(8,128)S(1)}, u32[]{:S(2)}, u32[]{:S(2)}) collective-permute-start(f32[32,1024]{1,0:T(8,128)S(1)} %get-tuple-element.35.p0), channel_id=1, source_target_pairs={{32,0},{48,16},{64,32},{80,48},{96,64},{112,80},{0,96},{16,112},{3... | collective-permute-start | bytes 393224 | tf_op jit(solution)/shard_map/ppermute | solution.py:32
  124.4 6.4 %collective-permute-start.25 = (f32[32,1024]{1,0:T(8,128)S(1)}, f32[32,1024]{1,0:T(8,128)S(1)}, u32[]{:S(2)}, u32[]{:S(2)}) collective-permute-start(f32[32,1024]{1,0:T(8,128)S(1)} %get-tuple-element.35.p0), channel_id=1, source_target_pairs={{96,0},{112,16},{0,32},{16,48},{32,64},{48,80},{64,96},{80,112},{9... | collective-permute-start | bytes 393224 | tf_op jit(solution)/shard_map/ppermute | solution.py:32
  124.4 6.4 %collective-permute-start.26 = (f32[32,1024]{1,0:T(8,128)S(1)}, f32[32,1024]{1,0:T(8,128)S(1)}, u32[]{:S(2)}, u32[]{:S(2)}) collective-permute-start(f32[32,1024]{1,0:T(8,128)S(1)} %get-tuple-element.35.p0), channel_id=1, source_target_pairs={{64,0},{80,16},{96,32},{112,48},{0,64},{16,80},{32,96},{48,112},{6... | collective-permute-start | bytes 393224 | tf_op jit(solution)/shard_map/ppermute | solution.py:32
  159.7 22.1 %collective-permute-start.28 = (f32[16,2,32,256]{3,2,1,0:T(8,128)S(1)}, f32[16,2,32,256]{3,2,1,0:T(8,128)}, u32[]{:S(2)}, u32[]{:S(2)}) collective-permute-start(f32[16,2,32,256]{3,2,1,0:T(8,128)S(1)} %all_to_all.20.refs_0_), channel_id=1, source_target_pairs={{32,0},{48,16},{64,32},{80,48},{96,64},{112,80},{0,96},{16,112},{3... | collective-permute-start | bytes 3145736 | tf_op jit(solution)/shard_map/ppermute | solution.py:32
  162.4 22.6 %collective-permute-start.31 = (f32[16,2,32,256]{3,2,1,0:T(8,128)S(1)}, f32[16,2,32,256]{3,2,1,0:T(8,128)}, u32[]{:S(2)}, u32[]{:S(2)}) collective-permute-start(f32[16,2,32,256]{3,2,1,0:T(8,128)S(1)} %all_to_all.20.refs_0_), channel_id=1, source_target_pairs={{96,0},{112,16},{0,32},{16,48},{32,64},{48,80},{64,96},{80,112},{9... | collective-permute-start | bytes 3145736 | tf_op jit(solution)/shard_map/ppermute | solution.py:32
  163.5 17.2 %all-to-all-start.2 = ((f32[16,2,32,256]{3,2,1,0:T(8,128)}), f32[16,2,32,256]{3,2,1,0:T(8,128)S(1)}, u32[]{:S(2)}, u32[]{:S(2)}) async-start(f32[16,2,32,256]{3,2,1,0:T(8,128)} %broadcast_in_dim.5), calls=%async_computation.2 | async-start | bytes 2097152 | tf_op jit(solution)/shard_map/all_to_all | solution.py:315
  180.7 57.8 %copy-start.10 = (f32[16,2,32,256]{3,2,1,0:T(8,128)}, f32[16,2,32,256]{3,2,1,0:T(8,128)S(1)}, u32[]{:S(2)}) copy-start(f32[16,2,32,256]{3,2,1,0:T(8,128)S(1)} %all-to-all-done.2.refs_0_) | copy-start | bytes 3145732
  185.1 71.5 %all-to-all-start.3 = ((f32[16,2,64,512]{3,2,1,0:T(8,128)}), f32[16,2,64,512]{3,2,1,0:T(8,128)}, u32[]{:S(2)}, u32[]{:S(2)}) async-start(f32[16,2,64,512]{3,2,1,0:T(8,128)} %copy-done.8), calls=%async_computation.3 | async-start | bytes 8388608 | tf_op jit(solution)/shard_map/all_to_all | solution.py:316
  189.6 22.3 %collective-permute-start.27 = (f32[16,2,32,256]{3,2,1,0:T(8,128)S(1)}, f32[16,2,32,256]{3,2,1,0:T(8,128)S(1)}, u32[]{:S(2)}, u32[]{:S(2)}) collective-permute-start(f32[16,2,32,256]{3,2,1,0:T(8,128)S(1)} %all_to_all.20.refs_0_), channel_id=1, source_target_pairs={{0,16},{16,0},{32,48},{48,32},{64,80},{80,64},{96,112},{112,96},{1... | collective-permute-start | bytes 3145736 | tf_op jit(solution)/shard_map/ppermute | solution.py:36
  195.0 13.7 %collective-permute-start.30 = (f32[8,2,32,256]{3,2,1,0:T(8,128)S(1)}, f32[8,2,32,256]{3,2,1,0:T(8,128)S(1)}, u32[]{:S(2)}, u32[]{:S(2)}) collective-permute-start(f32[8,2,32,256]{3,2,1,0:T(8,128)S(1)} %slice.56), channel_id=1, source_target_pairs={{32,0},{48,16},{64,32},{80,48},{96,64},{112,80},{0,96},{16,112},{3... | collective-permute-start | bytes 1572872 | tf_op jit(solution)/shard_map/ppermute | solution.py:32
  196.2 14.6 %collective-permute-start.32 = (f32[8,2,32,256]{3,2,1,0:T(8,128)S(1)}, f32[8,2,32,256]{3,2,1,0:T(8,128)S(1)}, u32[]{:S(2)}, u32[]{:S(2)}) collective-permute-start(f32[8,2,32,256]{3,2,1,0:T(8,128)S(1)} %slice.57), channel_id=1, source_target_pairs={{96,0},{112,16},{0,32},{16,48},{32,64},{48,80},{64,96},{80,112},{9... | collective-permute-start | bytes 1572872 | tf_op jit(solution)/shard_map/ppermute | solution.py:32
  197.7 15.7 %collective-permute-start.29 = (f32[16,2,32,256]{3,2,1,0:T(8,128)}, f32[16,2,32,256]{3,2,1,0:T(8,128)S(1)}, u32[]{:S(2)}, u32[]{:S(2)}) collective-permute-start(f32[16,2,32,256]{3,2,1,0:T(8,128)} %collective-permute-done.28.refs_2_), channel_id=1, source_target_pairs={{0,16},{16,0},{32,48},{48,32},{64,80},{80,64},{96,112},{112,96},{1... | collective-permute-start | bytes 3145736 | tf_op jit(solution)/shard_map/ppermute | solution.py:36
  198.3 15.2 %collective-permute-start.34 = (f32[16,2,32,256]{3,2,1,0:T(8,128)}, f32[16,2,32,256]{3,2,1,0:T(8,128)S(1)}, u32[]{:S(2)}, u32[]{:S(2)}) collective-permute-start(f32[16,2,32,256]{3,2,1,0:T(8,128)} %collective-permute-done.31.refs_6_), channel_id=1, source_target_pairs={{0,16},{16,0},{32,48},{48,32},{64,80},{80,64},{96,112},{112,96},{1... | collective-permute-start | bytes 3145736 | tf_op jit(solution)/shard_map/ppermute | solution.py:36
  210.9 3.5 %collective-permute-start.33 = (f32[16,2,32,256]{3,2,1,0:T(8,128)S(1)}, f32[16,2,32,256]{3,2,1,0:T(8,128)}, u32[]{:S(2)}, u32[]{:S(2)}) collective-permute-start(f32[16,2,32,256]{3,2,1,0:T(8,128)S(1)} %constant_dynamic-update-slice_fusion.refs_4_), channel_id=1, source_target_pairs={{0,16},{16,0},{32,48},{48,32},{64,80},{80,64},{96,112},{112,96},{1... | collective-permute-start | bytes 3145736 | tf_op jit(solution)/shard_map/ppermute | solution.py:36
  212.0 24.8 %collective-permute-start.36 = (f32[16,2,32,256]{3,2,1,0:T(8,128)S(1)}, f32[16,2,32,256]{3,2,1,0:T(8,128)S(1)}, u32[]{:S(2)}, u32[]{:S(2)}) collective-permute-start(f32[16,2,32,256]{3,2,1,0:T(8,128)S(1)} %all-to-all-done.2.refs_0_), channel_id=1, source_target_pairs={{32,0},{48,16},{64,32},{80,48},{96,64},{112,80},{0,96},{16,112},{3... | collective-permute-start | bytes 3145736 | tf_op jit(solution)/shard_map/ppermute | solution.py:32
  212.0 26.3 %collective-permute-start.39 = (f32[16,2,32,256]{3,2,1,0:T(8,128)S(1)}, f32[16,2,32,256]{3,2,1,0:T(8,128)S(1)}, u32[]{:S(2)}, u32[]{:S(2)}) collective-permute-start(f32[16,2,32,256]{3,2,1,0:T(8,128)S(1)} %all-to-all-done.2.refs_0_), channel_id=1, source_target_pairs={{96,0},{112,16},{0,32},{16,48},{32,64},{48,80},{64,96},{80,112},{9... | collective-permute-start | bytes 3145736 | tf_op jit(solution)/shard_map/ppermute | solution.py:32
  236.8 12.8 %collective-permute-start.38 = (f32[8,2,32,256]{3,2,1,0:T(8,128)S(1)}, f32[8,2,32,256]{3,2,1,0:T(8,128)S(1)}, u32[]{:S(2)}, u32[]{:S(2)}) collective-permute-start(f32[8,2,32,256]{3,2,1,0:T(8,128)S(1)} %slice.54), channel_id=1, source_target_pairs={{32,0},{48,16},{64,32},{80,48},{96,64},{112,80},{0,96},{16,112},{3... | collective-permute-start | bytes 1572872 | tf_op jit(solution)/shard_map/ppermute | solution.py:32
  238.3 13.9 %collective-permute-start.40 = (f32[8,2,32,256]{3,2,1,0:T(8,128)S(1)}, f32[8,2,32,256]{3,2,1,0:T(8,128)S(1)}, u32[]{:S(2)}, u32[]{:S(2)}) collective-permute-start(f32[8,2,32,256]{3,2,1,0:T(8,128)S(1)} %slice.58), channel_id=1, source_target_pairs={{96,0},{112,16},{0,32},{16,48},{32,64},{48,80},{64,96},{80,112},{9... | collective-permute-start | bytes 1572872 | tf_op jit(solution)/shard_map/ppermute | solution.py:32
  238.5 15.6 %collective-permute-start.35 = (f32[16,2,32,256]{3,2,1,0:T(8,128)S(1)}, f32[16,2,32,256]{3,2,1,0:T(8,128)S(1)}, u32[]{:S(2)}, u32[]{:S(2)}) collective-permute-start(f32[16,2,32,256]{3,2,1,0:T(8,128)S(1)} %all-to-all-done.2.refs_0_), channel_id=1, source_target_pairs={{0,16},{16,0},{32,48},{48,32},{64,80},{80,64},{96,112},{112,96},{1... | collective-permute-start | bytes 3145736 | tf_op jit(solution)/shard_map/ppermute | solution.py:36
  239.8 14.3 %collective-permute-start.37 = (f32[16,2,32,256]{3,2,1,0:T(8,128)S(1)}, f32[16,2,32,256]{3,2,1,0:T(8,128)S(1)}, u32[]{:S(2)}, u32[]{:S(2)}) collective-permute-start(f32[16,2,32,256]{3,2,1,0:T(8,128)S(1)} %collective-permute-done.36.refs_2_), channel_id=1, source_target_pairs={{0,16},{16,0},{32,48},{48,32},{64,80},{80,64},{96,112},{112,96},{1... | collective-permute-start | bytes 3145736 | tf_op jit(solution)/shard_map/ppermute | solution.py:36
  239.8 14.3 %collective-permute-start.42 = (f32[16,2,32,256]{3,2,1,0:T(8,128)S(1)}, f32[16,2,32,256]{3,2,1,0:T(8,128)S(1)}, u32[]{:S(2)}, u32[]{:S(2)}) collective-permute-start(f32[16,2,32,256]{3,2,1,0:T(8,128)S(1)} %collective-permute-done.39.refs_6_), channel_id=1, source_target_pairs={{0,16},{16,0},{32,48},{48,32},{64,80},{80,64},{96,112},{112,96},{1... | collective-permute-start | bytes 3145736 | tf_op jit(solution)/shard_map/ppermute | solution.py:36
  252.3 4.2 %collective-permute-start.41 = (f32[16,2,32,256]{3,2,1,0:T(8,128)S(1)}, f32[16,2,32,256]{3,2,1,0:T(8,128)}, u32[]{:S(2)}, u32[]{:S(2)}) collective-permute-start(f32[16,2,32,256]{3,2,1,0:T(8,128)S(1)} %constant_dynamic-update-slice_fusion.2.refs_4_), channel_id=1, source_target_pairs={{0,16},{16,0},{32,48},{48,32},{64,80},{80,64},{96,112},{112,96},{1... | collective-permute-start | bytes 3145736 | tf_op jit(solution)/shard_map/ppermute | solution.py:36
  (23 other events, 186.5 us)

commit v3 on v2

--- a/solution.py
+++ b/solution.py
@@ -317,7 +317,6 @@
     across_01 = far_part(up_01, down_01)
     xs_01 = core_pairs([x_01, up_01, across_01, down_01])
     out, solved_0 = update(place, factor_01, 0, xs_01, 0, 2, trail_right, *block)
-    x_23 = after(x_23, across_01)
     up_23, down_23 = from_y(x_23, 1), from_y(x_23, 3)
     across_23 = far_part(after(up_23, out), down_23)
     xs_23 = core_pairs([x_23, up_23, across_23, down_23])

time: 273 us -> 273 us (level)
  no operation moved by 1% of the time
where the time goes in v3:
time: 273 us; the launch traced here: 272 us
  waiting for transfers between devices  112 us (41%)
  starting transfers between devices  63.1 us (23%)
  Pallas kernels  41.2 us (15%)
  local copies, waits for them, and re-layouts  27 us (10%)
  blocking collectives  25.1 us (9%)
    ppermute x20, waiting for transfers between devices, from_y(): return lax.ppermute(value, 'row', y_perm(d))  57.8 us
    ppermute x6, waiting for transfers between devices, from_z(): return lax.ppermute(value, 'col', col_perm(0, d))  35.9 us
    pallas_call x2, Pallas kernels, update(): pl.pallas_call(update_kernel, grid_spec=grid_spec, out_shape=[jax.ShapeDt...  27.8 us
    all_to_all x1, blocking collectives, per_device(): lax.all_to_all(after(spread(pieces[0:2]), factor_01, pieces[3]), 'col', 0...  25.1 us
    ppermute x20, starting transfers between devices, from_y(): return lax.ppermute(value, 'row', y_perm(d))  20.1 us
    unnamed x50, local copies, waits for them, and re-layouts  18.1 us
    ppermute x11, starting transfers between devices, from_core(): return lax.ppermute(value, 'row', CORE_PERM)  12.2 us
    pallas_call x8, Pallas kernels, small_call(): pl.pallas_call(kernel, grid_spec=pltpu.PrefetchScalarGridSpec(num_scalar_...  11.4 us
  transfers between devices with their start and end apart: 46, of which 24 were waited for; matrix products, arithmetic and copies ran while one was open for 3% of the time, Pallas kernels for 10%

profile of v3, /device:TPU:1, one launch (start us, length us, event | category | flops | bytes accessed | tf_op | source)
XLA Modules:
  0.0 272.0 jit_solution(242913299003509602)
XLA Ops:
  3.1 3.4 %collective-permute-start = (f32[5,64,128]{2,1,0:T(8,128)S(1)}, f32[5,64,128]{2,1,0:T(8,128)S(1)}, u32[]{:S(2)}, u32[]{:S(2)}) collective-permute-start(f32[5,64,128]{2,1,0:T(8,128)S(1)} %get-tuple-element.49), channel_id=1, source_target_pairs={{4,0},{5,1},{6,2},{7,3},{8,4},{9,5},{10,6},{11,7},{12,8},{13,9},{1... | collective-permute-start | bytes 491528 | tf_op jit(solution)/shard_map/ppermute | solution.py:24
  9.0 1.6 collective-permute-start.6
  10.6 3.8 %collective-permute-start.3 = (f32[5,64,128]{2,1,0:T(8,128)S(1)}, f32[5,64,128]{2,1,0:T(8,128)S(1)}, u32[]{:S(2)}, u32[]{:S(2)}) collective-permute-start(f32[5,64,128]{2,1,0:T(8,128)S(1)} %get-tuple-element.47), channel_id=1, source_target_pairs={{1,0},{2,1},{3,2},{0,3},{5,4},{6,5},{7,6},{4,7},{9,8},{10,9},{11,1... | collective-permute-start | bytes 491528 | tf_op jit(solution)/shard_map/ppermute | solution.py:28
  14.5 3.4 %copy-done.5 = f32[4,64,8192]{2,1,0:T(8,128)S(1)} copy-done((f32[4,64,8192]{2,1,0:T(8,128)S(1)}, f32[4,64,8192]{2,1,0:T(8,128)}, u32[]{:S(2)}) %copy-start.5) | copy-done | bytes 8388632
  19.8 6.2 %collective-permute-done.4 = f32[5,64,128]{2,1,0:T(8,128)S(1)} collective-permute-done((f32[5,64,128]{2,1,0:T(8,128)S(1)}, f32[5,64,128]{2,1,0:T(8,128)S(1)}, u32[]{:S(2)}, u32[]{:S(2)}) %collective-permute-start.4) | collective-permute-done | bytes 163872 | tf_op jit(solution)/shard_map/ppermute | solution.py:28
  26.0 3.7 %collective-permute-done.5 = f32[5,64,128]{2,1,0:T(8,128)S(1)} collective-permute-done((f32[5,64,128]{2,1,0:T(8,128)S(1)}, f32[5,64,128]{2,1,0:T(8,128)S(1)}, u32[]{:S(2)}, u32[]{:S(2)}) %collective-permute-start.5) | collective-permute-done | bytes 163872 | tf_op jit(solution)/shard_map/ppermute | solution.py:28
  31.3 2.1 collective-permute-start.10
  34.6 10.8 %collective-permute-done.7 = f32[4,5,64,128]{3,2,1,0:T(8,128)S(1)} collective-permute-done((f32[4,5,64,128]{3,2,1,0:T(8,128)S(1)}, f32[4,5,64,128]{3,2,1,0:T(8,128)S(1)}, u32[]{:S(2)}, u32[]{:S(2)}) %collective-permute-start.7) | collective-permute-done | bytes 655392 | tf_op jit(solution)/shard_map/ppermute | solution.py:28
  45.4 1.5 collective-permute-start.12
  46.9 15.2 %collective-permute-done.9 = f32[4,5,64,128]{3,2,1,0:T(8,128)S(1)} collective-permute-done((f32[4,5,64,128]{3,2,1,0:T(8,128)S(1)}, f32[4,5,64,128]{3,2,1,0:T(8,128)S(1)}, u32[]{:S(2)}, u32[]{:S(2)}) %collective-permute-start.9) | collective-permute-done | bytes 655392 | tf_op jit(solution)/shard_map/ppermute | solution.py:28
  62.5 1.6 copy.9
  64.5 7.2 %all-to-all-start = ((f32[16,2,64,512]{3,2,1,0:T(8,128)}), f32[16,2,64,512]{3,2,1,0:T(8,128)}, u32[]{:S(2)}, u32[]{:S(2)}) async-start(f32[16,2,64,512]{3,2,1,0:T(8,128)} %copy-done.7), calls=%async_computation | async-start | bytes 8388608 | tf_op jit(solution)/shard_map/all_to_all | solution.py:277
  72.7 7.5 %collective-permute-done.13.inv_far.low_far = f32[16,5,64,128]{3,2,1,0:T(8,128)S(1)} collective-permute-done((f32[16,5,64,128]{3,2,1,0:T(8,128)}, f32[16,5,64,128]{3,2,1,0:T(8,128)S(1)}, u32[]{:S(2)}, u32[]{:S(2)}) %collective-permute-start.13) | collective-permute-done | bytes 2621472 | tf_op jit(solution)/shard_map/ppermute | solution.py:36
  80.2 2.7 copy-done
  83.5 2.8 %collective-permute-start.14 = (f32[32,1024]{1,0:T(8,128)S(1)}, f32[32,1024]{1,0:T(8,128)S(1)}, u32[]{:S(2)}, u32[]{:S(2)}) collective-permute-start(f32[32,1024]{1,0:T(8,128)S(1)} %shard_map.69.p0), channel_id=1, source_target_pairs={{32,0},{48,16},{64,32},{80,48},{96,64},{112,80},{0,96},{16,112},{3... | collective-permute-start | bytes 393224 | tf_op jit(solution)/shard_map/ppermute | solution.py:32
  86.3 1.6 collective-permute-start.16
  88.8 6.2 %collective-permute-done.15.p2 = f32[32,1024]{1,0:T(8,128)S(1)} collective-permute-done((f32[32,1024]{1,0:T(8,128)S(1)}, f32[32,1024]{1,0:T(8,128)S(1)}, u32[]{:S(2)}, u32[]{:S(2)}) %collective-permute-start.15) | collective-permute-done | bytes 131104 | tf_op jit(solution)/shard_map/ppermute | solution.py:32
  95.0 1.7 copy-done.1
  96.8 1.7 copy-done.4
  102.2 2.0 collective-permute-done.17.p1
  105.5 2.3 collective-permute-done.19.p3
  107.8 2.6 shard_map.72
  110.4 2.0 collective-permute-start.21
  116.6 3.1 %collective-permute-done.22.p2 = f32[32,1024]{1,0:T(8,128)S(1)} collective-permute-done((f32[32,1024]{1,0:T(8,128)S(1)}, f32[32,1024]{1,0:T(8,128)S(1)}, u32[]{:S(2)}, u32[]{:S(2)}) %collective-permute-start.22) | collective-permute-done | bytes 131104 | tf_op jit(solution)/shard_map/ppermute | solution.py:32
  119.7 2.9 %shard_map.75 = (f32[32,1024]{1,0:T(8,128)}, f32[32,256]{1,0:T(8,128)S(1)}, f32[32,1024]{1,0:T(8,128)S(1)}) custom-call(s32[5]{0:T(128)S(1)} %stack.101.place_ref, f32[32,1024]{1,0:T(8,128)S(1)} %get-tuple-element.32.p0, f32[32,1024]{1,0:T(8,128)S(1)} %collective-permute-done.21.p1, f32[32,1024]{1,0:T(8,128)S(1)} %collective-permute-done.22.p2, ...), custom_call_target="tpu_custom_call" | custom-call | tf_op jit(solution)/shard_map/pallas_call | solution.py:133
  122.6 1.8 collective-permute-start.24
  126.4 4.4 %collective-permute-done.25.p2 = f32[32,1024]{1,0:T(8,128)S(1)} collective-permute-done((f32[32,1024]{1,0:T(8,128)S(1)}, f32[32,1024]{1,0:T(8,128)S(1)}, u32[]{:S(2)}, u32[]{:S(2)}) %collective-permute-start.25) | collective-permute-done | bytes 131104 | tf_op jit(solution)/shard_map/ppermute | solution.py:32
  131.5 3.0 %all-to-all-done.f_ref = f32[16,2,64,512]{3,2,1,0:T(8,128)} async-done(((f32[16,2,64,512]{3,2,1,0:T(8,128)}), f32[16,2,64,512]{3,2,1,0:T(8,128)}, u32[]{:S(2)}, u32[]{:S(2)}) %all-to-all-start) | async-done | bytes 4194336 | tf_op jit(solution)/shard_map/all_to_all | solution.py:277
  134.6 25.1 %all_to_all.20.refs_0_ = f32[16,2,32,256]{3,2,1,0:T(8,128)S(1)} all-to-all(f32[16,2,32,256]{3,2,1,0:T(8,128)S(1)} %broadcast_in_dim.4), channel_id=1, replica_groups=mesh['row'=8,'col'=16] {'col'}, dimensions={0} | all-to-all | bytes 2097152 | tf_op jit(solution)/shard_map/all_to_all | solution.py:313
  159.7 2.7 %collective-permute-start.28 = (f32[16,2,32,256]{3,2,1,0:T(8,128)S(1)}, f32[16,2,32,256]{3,2,1,0:T(8,128)}, u32[]{:S(2)}, u32[]{:S(2)}) collective-permute-start(f32[16,2,32,256]{3,2,1,0:T(8,128)S(1)} %all_to_all.20.refs_0_), channel_id=1, source_target_pairs={{32,0},{48,16},{64,32},{80,48},{96,64},{112,80},{0,96},{16,112},{3... | collective-permute-start | bytes 3145736 | tf_op jit(solution)/shard_map/ppermute | solution.py:32
  163.5 3.7 %all-to-all-start.2 = ((f32[16,2,32,256]{3,2,1,0:T(8,128)}), f32[16,2,32,256]{3,2,1,0:T(8,128)S(1)}, u32[]{:S(2)}, u32[]{:S(2)}) async-start(f32[16,2,32,256]{3,2,1,0:T(8,128)} %broadcast_in_dim.5), calls=%async_computation.2 | async-start | bytes 2097152 | tf_op jit(solution)/shard_map/all_to_all | solution.py:315
  167.2 3.4 %copy-done.6 = f32[4,64,8192]{2,1,0:T(8,128)S(1)} copy-done((f32[4,64,8192]{2,1,0:T(8,128)S(1)}, f32[4,64,8192]{2,1,0:T(8,128)}, u32[]{:S(2)}) %copy-start.6) | copy-done | bytes 8388632
  171.6 2.1 copy-done.8
  173.7 7.0 %all-to-all-done.2.refs_0_ = f32[16,2,32,256]{3,2,1,0:T(8,128)S(1)} async-done(((f32[16,2,32,256]{3,2,1,0:T(8,128)}), f32[16,2,32,256]{3,2,1,0:T(8,128)S(1)}, u32[]{:S(2)}, u32[]{:S(2)}) %all-to-all-start.2) | async-done | bytes 1048608 | tf_op jit(solution)/shard_map/all_to_all | solution.py:315
  181.8 3.2 %collective-permute-done.31.refs_6_ = f32[16,2,32,256]{3,2,1,0:T(8,128)} collective-permute-done((f32[16,2,32,256]{3,2,1,0:T(8,128)S(1)}, f32[16,2,32,256]{3,2,1,0:T(8,128)}, u32[]{:S(2)}, u32[]{:S(2)}) %collective-permute-start.31) | collective-permute-done | bytes 1048608 | tf_op jit(solution)/shard_map/ppermute | solution.py:32
  185.1 4.5 %all-to-all-start.3 = ((f32[16,2,64,512]{3,2,1,0:T(8,128)}), f32[16,2,64,512]{3,2,1,0:T(8,128)}, u32[]{:S(2)}, u32[]{:S(2)}) async-start(f32[16,2,64,512]{3,2,1,0:T(8,128)} %copy-done.8), calls=%async_computation.3 | async-start | bytes 8388608 | tf_op jit(solution)/shard_map/all_to_all | solution.py:316
  189.6 4.3 %collective-permute-start.27 = (f32[16,2,32,256]{3,2,1,0:T(8,128)S(1)}, f32[16,2,32,256]{3,2,1,0:T(8,128)S(1)}, u32[]{:S(2)}, u32[]{:S(2)}) collective-permute-start(f32[16,2,32,256]{3,2,1,0:T(8,128)S(1)} %all_to_all.20.refs_0_), channel_id=1, source_target_pairs={{0,16},{16,0},{32,48},{48,32},{64,80},{80,64},{96,112},{112,96},{1... | collective-permute-start | bytes 3145736 | tf_op jit(solution)/shard_map/ppermute | solution.py:36
  196.2 1.5 collective-permute-start.32
  198.3 10.5 %collective-permute-done.30 = f32[8,2,32,256]{3,2,1,0:T(8,128)S(1)} collective-permute-done((f32[8,2,32,256]{3,2,1,0:T(8,128)S(1)}, f32[8,2,32,256]{3,2,1,0:T(8,128)S(1)}, u32[]{:S(2)}, u32[]{:S(2)}) %collective-permute-start.30) | collective-permute-done | bytes 524320 | tf_op jit(solution)/shard_map/ppermute | solution.py:32
  208.8 2.0 collective-permute-done.32
  212.0 1.5 collective-permute-start.39
  214.8 13.9 %shard_map.77 = (f32[512,1024]{1,0:T(8,128)}, f32[2,64,128]{2,1,0:T(8,128)}) custom-call(s32[5]{0:T(128)} %copy-done.9, f32[16,2,64,512]{3,2,1,0:T(8,128)} %all-to-all-done.f_ref, f32[16,2,32,256]{3,2,1,0:T(8,128)} %copy-done.11, f32[16,2,32,256]{3,2,1,0:T(8,128)} %copy-done.16, f32[16,2,32,256]{3,2,1,0:T(8,128)} %collective-permute-done.28.refs_2_, ...), custom_call_target="tpu_custom_call" | custom-call | tf_op jit(solution)/shard_map/pallas_call | solution.py:230
  228.6 8.1 %collective-permute-done.36.refs_2_ = f32[16,2,32,256]{3,2,1,0:T(8,128)S(1)} collective-permute-done((f32[16,2,32,256]{3,2,1,0:T(8,128)S(1)}, f32[16,2,32,256]{3,2,1,0:T(8,128)S(1)}, u32[]{:S(2)}, u32[]{:S(2)}) %collective-permute-start.36) | collective-permute-done | bytes 1048608 | tf_op jit(solution)/shard_map/ppermute | solution.py:32
  240.3 9.3 %collective-permute-done.38 = f32[8,2,32,256]{3,2,1,0:T(8,128)S(1)} collective-permute-done((f32[8,2,32,256]{3,2,1,0:T(8,128)S(1)}, f32[8,2,32,256]{3,2,1,0:T(8,128)S(1)}, u32[]{:S(2)}, u32[]{:S(2)}) %collective-permute-start.38) | collective-permute-done | bytes 524320 | tf_op jit(solution)/shard_map/ppermute | solution.py:32
  249.6 2.6 collective-permute-done.40
  252.3 1.8 collective-permute-start.41
  256.5 13.9 %shard_map.79 = (f32[512,1024]{1,0:T(8,128)}, f32[2,64,128]{2,1,0:T(8,128)}) custom-call(s32[5]{0:T(128)} %copy-done.9, f32[16,2,64,512]{3,2,1,0:T(8,128)} %all-to-all-done.3.f_ref, f32[16,2,32,256]{3,2,1,0:T(8,128)} %copy-done.10, f32[16,2,32,256]{3,2,1,0:T(8,128)} %copy-done.17, f32[16,2,32,256]{3,2,1,0:T(8,128)} %copy-done.12, ...), custom_call_target="tpu_custom_call" | custom-call | tf_op jit(solution)/shard_map/pallas_call | solution.py:230
  270.5 1.5 pad_maximum_fusion.6
  (136 shorter events, 39.3 us)
Async XLA Ops:
  3.1 15.9 %collective-permute-start = (f32[5,64,128]{2,1,0:T(8,128)S(1)}, f32[5,64,128]{2,1,0:T(8,128)S(1)}, u32[]{:S(2)}, u32[]{:S(2)}) collective-permute-start(f32[5,64,128]{2,1,0:T(8,128)S(1)} %get-tuple-element.49), channel_id=1, source_target_pairs={{4,0},{5,1},{6,2},{7,3},{8,4},{9,5},{10,6},{11,7},{12,8},{13,9},{1... | collective-permute-start | bytes 491528 | tf_op jit(solution)/shard_map/ppermute | solution.py:24
  6.5 13.2 %collective-permute-start.1 = (f32[5,64,128]{2,1,0:T(8,128)S(1)}, f32[5,64,128]{2,1,0:T(8,128)S(1)}, u32[]{:S(2)}, u32[]{:S(2)}) collective-permute-start(f32[5,64,128]{2,1,0:T(8,128)S(1)} %get-tuple-element.49), channel_id=1, source_target_pairs={{8,0},{9,1},{10,2},{11,3},{12,4},{13,5},{14,6},{15,7},{0,8},{1,9},... | collective-permute-start | bytes 491528 | tf_op jit(solution)/shard_map/ppermute | solution.py:24
  7.0 12.7 %collective-permute-start.2 = (f32[5,64,128]{2,1,0:T(8,128)S(1)}, f32[5,64,128]{2,1,0:T(8,128)S(1)}, u32[]{:S(2)}, u32[]{:S(2)}) collective-permute-start(f32[5,64,128]{2,1,0:T(8,128)S(1)} %get-tuple-element.49), channel_id=1, source_target_pairs={{12,0},{13,1},{14,2},{15,3},{0,4},{1,5},{2,6},{3,7},{4,8},{5,9},{6... | collective-permute-start | bytes 491528 | tf_op jit(solution)/shard_map/ppermute | solution.py:24
  9.0 10.0 %collective-permute-start.6 = (f32[4,32,128]{2,1,0:T(8,128)S(1)}, f32[4,32,128]{2,1,0:T(8,128)S(1)}, u32[]{:S(2)}, u32[]{:S(2)}) collective-permute-start(f32[4,32,128]{2,1,0:T(8,128)S(1)} %bitcast.64), channel_id=1, source_target_pairs={{0,16},{16,0},{32,48},{48,32},{64,80},{80,64},{96,112},{112,96},{1... | collective-permute-start | bytes 196616 | tf_op jit(solution)/shard_map/ppermute | solution.py:36
  10.6 9.2 %collective-permute-start.3 = (f32[5,64,128]{2,1,0:T(8,128)S(1)}, f32[5,64,128]{2,1,0:T(8,128)S(1)}, u32[]{:S(2)}, u32[]{:S(2)}) collective-permute-start(f32[5,64,128]{2,1,0:T(8,128)S(1)} %get-tuple-element.47), channel_id=1, source_target_pairs={{1,0},{2,1},{3,2},{0,3},{5,4},{6,5},{7,6},{4,7},{9,8},{10,9},{11,1... | collective-permute-start | bytes 491528 | tf_op jit(solution)/shard_map/ppermute | solution.py:28
  18.9 43.6 %copy-start.7 = (f32[16,2,64,512]{3,2,1,0:T(8,128)}, f32[16,2,64,512]{3,2,1,0:T(8,128)S(1)}, u32[]{:S(2)}) copy-start(f32[16,2,64,512]{3,2,1,0:T(8,128)S(1)} %shard_map.68) | copy-start | bytes 12582916
  18.9 7.1 %collective-permute-start.4 = (f32[5,64,128]{2,1,0:T(8,128)S(1)}, f32[5,64,128]{2,1,0:T(8,128)S(1)}, u32[]{:S(2)}, u32[]{:S(2)}) collective-permute-start(f32[5,64,128]{2,1,0:T(8,128)S(1)} %get-tuple-element.47), channel_id=1, source_target_pairs={{2,0},{3,1},{0,2},{1,3},{6,4},{7,5},{4,6},{5,7},{10,8},{11,9},{8,1... | collective-permute-start | bytes 491528 | tf_op jit(solution)/shard_map/ppermute | solution.py:28
  19.0 10.7 %collective-permute-start.5 = (f32[5,64,128]{2,1,0:T(8,128)S(1)}, f32[5,64,128]{2,1,0:T(8,128)S(1)}, u32[]{:S(2)}, u32[]{:S(2)}) collective-permute-start(f32[5,64,128]{2,1,0:T(8,128)S(1)} %get-tuple-element.47), channel_id=1, source_target_pairs={{3,0},{0,1},{1,2},{2,3},{7,4},{4,5},{5,6},{6,7},{11,8},{8,9},{9,10... | collective-permute-start | bytes 491528 | tf_op jit(solution)/shard_map/ppermute | solution.py:28
  29.8 15.6 %collective-permute-start.7 = (f32[4,5,64,128]{3,2,1,0:T(8,128)S(1)}, f32[4,5,64,128]{3,2,1,0:T(8,128)S(1)}, u32[]{:S(2)}, u32[]{:S(2)}) collective-permute-start(f32[4,5,64,128]{3,2,1,0:T(8,128)S(1)} %pad_maximum_fusion.1), channel_id=1, source_target_pairs={{1,0},{2,1},{3,2},{0,3},{5,4},{6,5},{7,6},{4,7},{9,8},{10,9},{11,1... | collective-permute-start | bytes 1966088 | tf_op jit(solution)/shard_map/ppermute | solution.py:28
  29.9 17.0 %collective-permute-start.8 = (f32[4,5,64,128]{3,2,1,0:T(8,128)S(1)}, f32[4,5,64,128]{3,2,1,0:T(8,128)S(1)}, u32[]{:S(2)}, u32[]{:S(2)}) collective-permute-start(f32[4,5,64,128]{3,2,1,0:T(8,128)S(1)} %pad_maximum_fusion.1), channel_id=1, source_target_pairs={{2,0},{3,1},{0,2},{1,3},{6,4},{7,5},{4,6},{5,7},{10,8},{11,9},{8,1... | collective-permute-start | bytes 1966088 | tf_op jit(solution)/shard_map/ppermute | solution.py:28
  30.4 31.8 %collective-permute-start.9 = (f32[4,5,64,128]{3,2,1,0:T(8,128)S(1)}, f32[4,5,64,128]{3,2,1,0:T(8,128)S(1)}, u32[]{:S(2)}, u32[]{:S(2)}) collective-permute-start(f32[4,5,64,128]{3,2,1,0:T(8,128)S(1)} %pad_maximum_fusion.1), channel_id=1, source_target_pairs={{3,0},{0,1},{1,2},{2,3},{7,4},{4,5},{5,6},{6,7},{11,8},{8,9},{9,10... | collective-permute-start | bytes 1966088 | tf_op jit(solution)/shard_map/ppermute | solution.py:28
  31.3 32.8 %collective-permute-start.10 = (f32[4,5,64,128]{3,2,1,0:T(8,128)S(1)}, f32[4,5,64,128]{3,2,1,0:T(8,128)S(1)}, u32[]{:S(2)}, u32[]{:S(2)}) collective-permute-start(f32[4,5,64,128]{3,2,1,0:T(8,128)S(1)} %pad_maximum_fusion.2), channel_id=1, source_target_pairs={{4,0},{5,1},{6,2},{7,3},{8,4},{9,5},{10,6},{11,7},{12,8},{13,9},{1... | collective-permute-start | bytes 1966088 | tf_op jit(solution)/shard_map/ppermute | solution.py:24
  33.4 30.7 %collective-permute-start.11 = (f32[4,5,64,128]{3,2,1,0:T(8,128)S(1)}, f32[4,5,64,128]{3,2,1,0:T(8,128)S(1)}, u32[]{:S(2)}, u32[]{:S(2)}) collective-permute-start(f32[4,5,64,128]{3,2,1,0:T(8,128)S(1)} %pad_maximum_fusion.2), channel_id=1, source_target_pairs={{8,0},{9,1},{10,2},{11,3},{12,4},{13,5},{14,6},{15,7},{0,8},{1,9},... | collective-permute-start | bytes 1966088 | tf_op jit(solution)/shard_map/ppermute | solution.py:24
  45.4 18.9 %collective-permute-start.12 = (f32[4,5,64,128]{3,2,1,0:T(8,128)S(1)}, f32[4,5,64,128]{3,2,1,0:T(8,128)S(1)}, u32[]{:S(2)}, u32[]{:S(2)}) collective-permute-start(f32[4,5,64,128]{3,2,1,0:T(8,128)S(1)} %pad_maximum_fusion.2), channel_id=1, source_target_pairs={{12,0},{13,1},{14,2},{15,3},{0,4},{1,5},{2,6},{3,7},{4,8},{5,9},{6... | collective-permute-start | bytes 1966088 | tf_op jit(solution)/shard_map/ppermute | solution.py:24
  64.5 69.9 %all-to-all-start = ((f32[16,2,64,512]{3,2,1,0:T(8,128)}), f32[16,2,64,512]{3,2,1,0:T(8,128)}, u32[]{:S(2)}, u32[]{:S(2)}) async-start(f32[16,2,64,512]{3,2,1,0:T(8,128)} %copy-done.7), calls=%async_computation | async-start | bytes 8388608 | tf_op jit(solution)/shard_map/all_to_all | solution.py:277
  71.8 8.4 %collective-permute-start.13 = (f32[16,5,64,128]{3,2,1,0:T(8,128)}, f32[16,5,64,128]{3,2,1,0:T(8,128)S(1)}, u32[]{:S(2)}, u32[]{:S(2)}) collective-permute-start(f32[16,5,64,128]{3,2,1,0:T(8,128)} %bitcast.39), channel_id=1, source_target_pairs={{0,16},{16,0},{32,48},{48,32},{64,80},{80,64},{96,112},{112,96},{1... | collective-permute-start | bytes 7864328 | tf_op jit(solution)/shard_map/ppermute | solution.py:36
  72.6 29.6 %collective-permute-start.20 = (f32[16,5,64,128]{3,2,1,0:T(8,128)S(1)}, f32[16,5,64,128]{3,2,1,0:T(8,128)}, u32[]{:S(2)}, u32[]{:S(2)}) collective-permute-start(f32[16,5,64,128]{3,2,1,0:T(8,128)S(1)} %bitcast.33), channel_id=1, source_target_pairs={{0,16},{16,0},{32,48},{48,32},{64,80},{80,64},{96,112},{112,96},{1... | collective-permute-start | bytes 7864328 | tf_op jit(solution)/shard_map/ppermute | solution.py:36
  83.5 5.3 %collective-permute-start.14 = (f32[32,1024]{1,0:T(8,128)S(1)}, f32[32,1024]{1,0:T(8,128)S(1)}, u32[]{:S(2)}, u32[]{:S(2)}) collective-permute-start(f32[32,1024]{1,0:T(8,128)S(1)} %shard_map.69.p0), channel_id=1, source_target_pairs={{32,0},{48,16},{64,32},{80,48},{96,64},{112,80},{0,96},{16,112},{3... | collective-permute-start | bytes 393224 | tf_op jit(solution)/shard_map/ppermute | solution.py:32
  86.3 8.7 %collective-permute-start.15 = (f32[32,1024]{1,0:T(8,128)S(1)}, f32[32,1024]{1,0:T(8,128)S(1)}, u32[]{:S(2)}, u32[]{:S(2)}) collective-permute-start(f32[32,1024]{1,0:T(8,128)S(1)} %shard_map.69.p0), channel_id=1, source_target_pairs={{96,0},{112,16},{0,32},{16,48},{32,64},{48,80},{64,96},{80,112},{9... | collective-permute-start | bytes 393224 | tf_op jit(solution)/shard_map/ppermute | solution.py:32
  86.3 8.7 %collective-permute-start.16 = (f32[32,1024]{1,0:T(8,128)S(1)}, f32[32,1024]{1,0:T(8,128)S(1)}, u32[]{:S(2)}, u32[]{:S(2)}) collective-permute-start(f32[32,1024]{1,0:T(8,128)S(1)} %shard_map.69.p0), channel_id=1, source_target_pairs={{64,0},{80,16},{96,32},{112,48},{0,64},{16,80},{32,96},{48,112},{6... | collective-permute-start | bytes 393224 | tf_op jit(solution)/shard_map/ppermute | solution.py:32
  99.9 4.3 %collective-permute-start.17 = (f32[32,1024]{1,0:T(8,128)S(1)}, f32[32,1024]{1,0:T(8,128)S(1)}, u32[]{:S(2)}, u32[]{:S(2)}) collective-permute-start(f32[32,1024]{1,0:T(8,128)S(1)} %get-tuple-element.29.p0), channel_id=1, source_target_pairs={{32,0},{48,16},{64,32},{80,48},{96,64},{112,80},{0,96},{16,112},{3... | collective-permute-start | bytes 393224 | tf_op jit(solution)/shard_map/ppermute | solution.py:32
  100.0 5.5 %collective-permute-start.18 = (f32[32,1024]{1,0:T(8,128)S(1)}, f32[32,1024]{1,0:T(8,128)S(1)}, u32[]{:S(2)}, u32[]{:S(2)}) collective-permute-start(f32[32,1024]{1,0:T(8,128)S(1)} %get-tuple-element.29.p0), channel_id=1, source_target_pairs={{96,0},{112,16},{0,32},{16,48},{32,64},{48,80},{64,96},{80,112},{9... | collective-permute-start | bytes 393224 | tf_op jit(solution)/shard_map/ppermute | solution.py:32
  101.5 6.4 %collective-permute-start.19 = (f32[32,1024]{1,0:T(8,128)S(1)}, f32[32,1024]{1,0:T(8,128)S(1)}, u32[]{:S(2)}, u32[]{:S(2)}) collective-permute-start(f32[32,1024]{1,0:T(8,128)S(1)} %get-tuple-element.29.p0), channel_id=1, source_target_pairs={{64,0},{80,16},{96,32},{112,48},{0,64},{16,80},{32,96},{48,112},{6... | collective-permute-start | bytes 393224 | tf_op jit(solution)/shard_map/ppermute | solution.py:32
  110.4 6.2 %collective-permute-start.21 = (f32[32,1024]{1,0:T(8,128)S(1)}, f32[32,1024]{1,0:T(8,128)S(1)}, u32[]{:S(2)}, u32[]{:S(2)}) collective-permute-start(f32[32,1024]{1,0:T(8,128)S(1)} %get-tuple-element.32.p0), channel_id=1, source_target_pairs={{32,0},{48,16},{64,32},{80,48},{96,64},{112,80},{0,96},{16,112},{3... | collective-permute-start | bytes 393224 | tf_op jit(solution)/shard_map/ppermute | solution.py:32
  112.4 7.3 %collective-permute-start.22 = (f32[32,1024]{1,0:T(8,128)S(1)}, f32[32,1024]{1,0:T(8,128)S(1)}, u32[]{:S(2)}, u32[]{:S(2)}) collective-permute-start(f32[32,1024]{1,0:T(8,128)S(1)} %get-tuple-element.32.p0), channel_id=1, source_target_pairs={{96,0},{112,16},{0,32},{16,48},{32,64},{48,80},{64,96},{80,112},{9... | collective-permute-start | bytes 393224 | tf_op jit(solution)/shard_map/ppermute | solution.py:32
  112.4 7.3 %collective-permute-start.23 = (f32[32,1024]{1,0:T(8,128)S(1)}, f32[32,1024]{1,0:T(8,128)S(1)}, u32[]{:S(2)}, u32[]{:S(2)}) collective-permute-start(f32[32,1024]{1,0:T(8,128)S(1)} %get-tuple-element.32.p0), channel_id=1, source_target_pairs={{64,0},{80,16},{96,32},{112,48},{0,64},{16,80},{32,96},{48,112},{6... | collective-permute-start | bytes 393224 | tf_op jit(solution)/shard_map/ppermute | solution.py:32
  122.6 3.8 %collective-permute-start.24 = (f32[32,1024]{1,0:T(8,128)S(1)}, f32[32,1024]{1,0:T(8,128)S(1)}, u32[]{:S(2)}, u32[]{:S(2)}) collective-permute-start(f32[32,1024]{1,0:T(8,128)S(1)} %get-tuple-element.34.p0), channel_id=1, source_target_pairs={{32,0},{48,16},{64,32},{80,48},{96,64},{112,80},{0,96},{16,112},{3... | collective-permute-start | bytes 393224 | tf_op jit(solution)/shard_map/ppermute | solution.py:32
  124.4 6.4 %collective-permute-start.25 = (f32[32,1024]{1,0:T(8,128)S(1)}, f32[32,1024]{1,0:T(8,128)S(1)}, u32[]{:S(2)}, u32[]{:S(2)}) collective-permute-start(f32[32,1024]{1,0:T(8,128)S(1)} %get-tuple-element.34.p0), channel_id=1, source_target_pairs={{96,0},{112,16},{0,32},{16,48},{32,64},{48,80},{64,96},{80,112},{9... | collective-permute-start | bytes 393224 | tf_op jit(solution)/shard_map/ppermute | solution.py:32
  124.4 6.4 %collective-permute-start.26 = (f32[32,1024]{1,0:T(8,128)S(1)}, f32[32,1024]{1,0:T(8,128)S(1)}, u32[]{:S(2)}, u32[]{:S(2)}) collective-permute-start(f32[32,1024]{1,0:T(8,128)S(1)} %get-tuple-element.34.p0), channel_id=1, source_target_pairs={{64,0},{80,16},{96,32},{112,48},{0,64},{16,80},{32,96},{48,112},{6... | collective-permute-start | bytes 393224 | tf_op jit(solution)/shard_map/ppermute | solution.py:32
  159.7 22.1 %collective-permute-start.28 = (f32[16,2,32,256]{3,2,1,0:T(8,128)S(1)}, f32[16,2,32,256]{3,2,1,0:T(8,128)}, u32[]{:S(2)}, u32[]{:S(2)}) collective-permute-start(f32[16,2,32,256]{3,2,1,0:T(8,128)S(1)} %all_to_all.20.refs_0_), channel_id=1, source_target_pairs={{32,0},{48,16},{64,32},{80,48},{96,64},{112,80},{0,96},{16,112},{3... | collective-permute-start | bytes 3145736 | tf_op jit(solution)/shard_map/ppermute | solution.py:32
  162.4 22.6 %collective-permute-start.31 = (f32[16,2,32,256]{3,2,1,0:T(8,128)S(1)}, f32[16,2,32,256]{3,2,1,0:T(8,128)}, u32[]{:S(2)}, u32[]{:S(2)}) collective-permute-start(f32[16,2,32,256]{3,2,1,0:T(8,128)S(1)} %all_to_all.20.refs_0_), channel_id=1, source_target_pairs={{96,0},{112,16},{0,32},{16,48},{32,64},{48,80},{64,96},{80,112},{9... | collective-permute-start | bytes 3145736 | tf_op jit(solution)/shard_map/ppermute | solution.py:32
  163.5 17.2 %all-to-all-start.2 = ((f32[16,2,32,256]{3,2,1,0:T(8,128)}), f32[16,2,32,256]{3,2,1,0:T(8,128)S(1)}, u32[]{:S(2)}, u32[]{:S(2)}) async-start(f32[16,2,32,256]{3,2,1,0:T(8,128)} %broadcast_in_dim.5), calls=%async_computation.2 | async-start | bytes 2097152 | tf_op jit(solution)/shard_map/all_to_all | solution.py:315
  180.7 57.8 %copy-start.10 = (f32[16,2,32,256]{3,2,1,0:T(8,128)}, f32[16,2,32,256]{3,2,1,0:T(8,128)S(1)}, u32[]{:S(2)}) copy-start(f32[16,2,32,256]{3,2,1,0:T(8,128)S(1)} %all-to-all-done.2.refs_0_) | copy-start | bytes 3145732
  185.1 71.5 %all-to-all-start.3 = ((f32[16,2,64,512]{3,2,1,0:T(8,128)}), f32[16,2,64,512]{3,2,1,0:T(8,128)}, u32[]{:S(2)}, u32[]{:S(2)}) async-start(f32[16,2,64,512]{3,2,1,0:T(8,128)} %copy-done.8), calls=%async_computation.3 | async-start | bytes 8388608 | tf_op jit(solution)/shard_map/all_to_all | solution.py:316
  189.6 22.3 %collective-permute-start.27 = (f32[16,2,32,256]{3,2,1,0:T(8,128)S(1)}, f32[16,2,32,256]{3,2,1,0:T(8,128)S(1)}, u32[]{:S(2)}, u32[]{:S(2)}) collective-permute-start(f32[16,2,32,256]{3,2,1,0:T(8,128)S(1)} %all_to_all.20.refs_0_), channel_id=1, source_target_pairs={{0,16},{16,0},{32,48},{48,32},{64,80},{80,64},{96,112},{112,96},{1... | collective-permute-start | bytes 3145736 | tf_op jit(solution)/shard_map/ppermute | solution.py:36
  195.0 13.7 %collective-permute-start.30 = (f32[8,2,32,256]{3,2,1,0:T(8,128)S(1)}, f32[8,2,32,256]{3,2,1,0:T(8,128)S(1)}, u32[]{:S(2)}, u32[]{:S(2)}) collective-permute-start(f32[8,2,32,256]{3,2,1,0:T(8,128)S(1)} %slice.56), channel_id=1, source_target_pairs={{32,0},{48,16},{64,32},{80,48},{96,64},{112,80},{0,96},{16,112},{3... | collective-permute-start | bytes 1572872 | tf_op jit(solution)/shard_map/ppermute | solution.py:32
  196.2 14.6 %collective-permute-start.32 = (f32[8,2,32,256]{3,2,1,0:T(8,128)S(1)}, f32[8,2,32,256]{3,2,1,0:T(8,128)S(1)}, u32[]{:S(2)}, u32[]{:S(2)}) collective-permute-start(f32[8,2,32,256]{3,2,1,0:T(8,128)S(1)} %slice.57), channel_id=1, source_target_pairs={{96,0},{112,16},{0,32},{16,48},{32,64},{48,80},{64,96},{80,112},{9... | collective-permute-start | bytes 1572872 | tf_op jit(solution)/shard_map/ppermute | solution.py:32
  197.7 15.7 %collective-permute-start.29 = (f32[16,2,32,256]{3,2,1,0:T(8,128)}, f32[16,2,32,256]{3,2,1,0:T(8,128)S(1)}, u32[]{:S(2)}, u32[]{:S(2)}) collective-permute-start(f32[16,2,32,256]{3,2,1,0:T(8,128)} %collective-permute-done.28.refs_2_), channel_id=1, source_target_pairs={{0,16},{16,0},{32,48},{48,32},{64,80},{80,64},{96,112},{112,96},{1... | collective-permute-start | bytes 3145736 | tf_op jit(solution)/shard_map/ppermute | solution.py:36
  198.3 15.2 %collective-permute-start.34 = (f32[16,2,32,256]{3,2,1,0:T(8,128)}, f32[16,2,32,256]{3,2,1,0:T(8,128)S(1)}, u32[]{:S(2)}, u32[]{:S(2)}) collective-permute-start(f32[16,2,32,256]{3,2,1,0:T(8,128)} %collective-permute-done.31.refs_6_), channel_id=1, source_target_pairs={{0,16},{16,0},{32,48},{48,32},{64,80},{80,64},{96,112},{112,96},{1... | collective-permute-start | bytes 3145736 | tf_op jit(solution)/shard_map/ppermute | solution.py:36
  210.9 3.5 %collective-permute-start.33 = (f32[16,2,32,256]{3,2,1,0:T(8,128)S(1)}, f32[16,2,32,256]{3,2,1,0:T(8,128)}, u32[]{:S(2)}, u32[]{:S(2)}) collective-permute-start(f32[16,2,32,256]{3,2,1,0:T(8,128)S(1)} %constant_dynamic-update-slice_fusion.refs_4_), channel_id=1, source_target_pairs={{0,16},{16,0},{32,48},{48,32},{64,80},{80,64},{96,112},{112,96},{1... | collective-permute-start | bytes 3145736 | tf_op jit(solution)/shard_map/ppermute | solution.py:36
  212.0 24.8 %collective-permute-start.36 = (f32[16,2,32,256]{3,2,1,0:T(8,128)S(1)}, f32[16,2,32,256]{3,2,1,0:T(8,128)S(1)}, u32[]{:S(2)}, u32[]{:S(2)}) collective-permute-start(f32[16,2,32,256]{3,2,1,0:T(8,128)S(1)} %all-to-all-done.2.refs_0_), channel_id=1, source_target_pairs={{32,0},{48,16},{64,32},{80,48},{96,64},{112,80},{0,96},{16,112},{3... | collective-permute-start | bytes 3145736 | tf_op jit(solution)/shard_map/ppermute | solution.py:32
  212.0 26.3 %collective-permute-start.39 = (f32[16,2,32,256]{3,2,1,0:T(8,128)S(1)}, f32[16,2,32,256]{3,2,1,0:T(8,128)S(1)}, u32[]{:S(2)}, u32[]{:S(2)}) collective-permute-start(f32[16,2,32,256]{3,2,1,0:T(8,128)S(1)} %all-to-all-done.2.refs_0_), channel_id=1, source_target_pairs={{96,0},{112,16},{0,32},{16,48},{32,64},{48,80},{64,96},{80,112},{9... | collective-permute-start | bytes 3145736 | tf_op jit(solution)/shard_map/ppermute | solution.py:32
  236.8 12.8 %collective-permute-start.38 = (f32[8,2,32,256]{3,2,1,0:T(8,128)S(1)}, f32[8,2,32,256]{3,2,1,0:T(8,128)S(1)}, u32[]{:S(2)}, u32[]{:S(2)}) collective-permute-start(f32[8,2,32,256]{3,2,1,0:T(8,128)S(1)} %slice.54), channel_id=1, source_target_pairs={{32,0},{48,16},{64,32},{80,48},{96,64},{112,80},{0,96},{16,112},{3... | collective-permute-start | bytes 1572872 | tf_op jit(solution)/shard_map/ppermute | solution.py:32
  238.3 13.9 %collective-permute-start.40 = (f32[8,2,32,256]{3,2,1,0:T(8,128)S(1)}, f32[8,2,32,256]{3,2,1,0:T(8,128)S(1)}, u32[]{:S(2)}, u32[]{:S(2)}) collective-permute-start(f32[8,2,32,256]{3,2,1,0:T(8,128)S(1)} %slice.58), channel_id=1, source_target_pairs={{96,0},{112,16},{0,32},{16,48},{32,64},{48,80},{64,96},{80,112},{9... | collective-permute-start | bytes 1572872 | tf_op jit(solution)/shard_map/ppermute | solution.py:32
  238.5 15.6 %collective-permute-start.35 = (f32[16,2,32,256]{3,2,1,0:T(8,128)S(1)}, f32[16,2,32,256]{3,2,1,0:T(8,128)S(1)}, u32[]{:S(2)}, u32[]{:S(2)}) collective-permute-start(f32[16,2,32,256]{3,2,1,0:T(8,128)S(1)} %all-to-all-done.2.refs_0_), channel_id=1, source_target_pairs={{0,16},{16,0},{32,48},{48,32},{64,80},{80,64},{96,112},{112,96},{1... | collective-permute-start | bytes 3145736 | tf_op jit(solution)/shard_map/ppermute | solution.py:36
  239.8 14.3 %collective-permute-start.37 = (f32[16,2,32,256]{3,2,1,0:T(8,128)S(1)}, f32[16,2,32,256]{3,2,1,0:T(8,128)S(1)}, u32[]{:S(2)}, u32[]{:S(2)}) collective-permute-start(f32[16,2,32,256]{3,2,1,0:T(8,128)S(1)} %collective-permute-done.36.refs_2_), channel_id=1, source_target_pairs={{0,16},{16,0},{32,48},{48,32},{64,80},{80,64},{96,112},{112,96},{1... | collective-permute-start | bytes 3145736 | tf_op jit(solution)/shard_map/ppermute | solution.py:36
  239.8 14.3 %collective-permute-start.42 = (f32[16,2,32,256]{3,2,1,0:T(8,128)S(1)}, f32[16,2,32,256]{3,2,1,0:T(8,128)S(1)}, u32[]{:S(2)}, u32[]{:S(2)}) collective-permute-start(f32[16,2,32,256]{3,2,1,0:T(8,128)S(1)} %collective-permute-done.39.refs_6_), channel_id=1, source_target_pairs={{0,16},{16,0},{32,48},{48,32},{64,80},{80,64},{96,112},{112,96},{1... | collective-permute-start | bytes 3145736 | tf_op jit(solution)/shard_map/ppermute | solution.py:36
  252.3 4.2 %collective-permute-start.41 = (f32[16,2,32,256]{3,2,1,0:T(8,128)S(1)}, f32[16,2,32,256]{3,2,1,0:T(8,128)}, u32[]{:S(2)}, u32[]{:S(2)}) collective-permute-start(f32[16,2,32,256]{3,2,1,0:T(8,128)S(1)} %constant_dynamic-update-slice_fusion.2.refs_4_), channel_id=1, source_target_pairs={{0,16},{16,0},{32,48},{48,32},{64,80},{80,64},{96,112},{112,96},{1... | collective-permute-start | bytes 3145736 | tf_op jit(solution)/shard_map/ppermute | solution.py:36
  (23 other events, 186.5 us)

commit v4 on v2

--- a/solution.py
+++ b/solution.py
@@ -41,10 +41,10 @@
     return jnp.stack([value, far[1], far[2], far[3]])
 
 
-def gather_blocks(set_a, set_b, *others):
+def gather_blocks(set_a, set_b, prepare):
     near_a = ring_stack(set_a, from_x)
     near_b = ring_stack(set_b, from_z)
-    near_a, near_b, *others = lax.optimization_barrier((near_a, near_b) + others)
+    near_a, near_b, *others = lax.optimization_barrier((near_a, near_b) + prepare(near_a))
     all_a = jnp.swapaxes(ring_stack(near_a, from_z), 0, 1)
     all_b = ring_stack(near_b, from_x)
     return all_a.reshape((-1,) + set_a.shape), all_b.reshape((-1,) + set_b.shape), *others
@@ -259,9 +259,13 @@
 
     set_a = jnp.concatenate([inverses[0:1], lower_blocks[0:1], inverses[1:2], lower_blocks[1:3]])
     set_b = jnp.concatenate([inverses[2:4], lower_blocks[3:6]])
-    split_0 = split_by_owner(trail_factor, 0, 2, 16)
+
+    def prepare(near):
+        factor = lax.optimization_barrier((trail_factor, near))[0]
+        return right, split_by_owner(factor, 0, 2, 16)
+
     split_2 = split_by_owner(trail_factor, 2, 2, 16)
-    got_a, got_b, right, split_0 = gather_blocks(set_a, set_b, right, split_0)
+    got_a, got_b, right, split_0 = gather_blocks(set_a, set_b, prepare)
     far_a = from_core(got_a)
     far_b = from_core(got_b)
     inv = [(0, 0), (0, 2), (1, 0), (1, 1)]

time: 273 us -> 269 us (0.985)
  waiting for transfers between devices: 112 us -> 108 us
    ppermute x6, waiting for transfers between devices: 35.9 us -> 29.7 us  [from_z(): return lax.ppermute(value, 'col', col_perm(0, d))]
where the time goes in v4:
time: 269 us; the launch traced here: 268 us
  waiting for transfers between devices  108 us (40%)
  starting transfers between devices  63.4 us (24%)
  Pallas kernels  41.2 us (15%)
  local copies, waits for them, and re-layouts  27 us (10%)
  blocking collectives  25.1 us (9%)
    ppermute x20, waiting for transfers between devices, from_y(): return lax.ppermute(value, 'row', y_perm(d))  57.8 us
    ppermute x6, waiting for transfers between devices, from_z(): return lax.ppermute(value, 'col', col_perm(0, d))  29.7 us
    pallas_call x2, Pallas kernels, update(): pl.pallas_call(update_kernel, grid_spec=grid_spec, out_shape=[jax.ShapeDt...  27.8 us
    all_to_all x1, blocking collectives, per_device(): lax.all_to_all(after(spread(pieces[0:2]), factor_01, pieces[3]), 'col', 0...  25.1 us
    ppermute x20, starting transfers between devices, from_y(): return lax.ppermute(value, 'row', y_perm(d))  20.1 us
    unnamed x50, local copies, waits for them, and re-layouts  18.1 us
    ppermute x11, starting transfers between devices, from_core(): return lax.ppermute(value, 'row', CORE_PERM)  12.2 us
    pallas_call x8, Pallas kernels, small_call(): pl.pallas_call(kernel, grid_spec=pltpu.PrefetchScalarGridSpec(num_scalar_...  11.4 us
  transfers between devices with their start and end apart: 46, of which 24 were waited for; matrix products, arithmetic and copies ran while one was open for 3% of the time, Pallas kernels for 10%

profile of v4, /device:TPU:1, one launch (start us, length us, event | category | flops | bytes accessed | tf_op | source)
XLA Modules:
  0.0 267.9 jit_solution(4392364911785378021)
XLA Ops:
  3.1 3.4 %collective-permute-start = (f32[5,64,128]{2,1,0:T(8,128)S(1)}, f32[5,64,128]{2,1,0:T(8,128)S(1)}, u32[]{:S(2)}, u32[]{:S(2)}) collective-permute-start(f32[5,64,128]{2,1,0:T(8,128)S(1)} %get-tuple-element.53), channel_id=1, source_target_pairs={{4,0},{5,1},{6,2},{7,3},{8,4},{9,5},{10,6},{11,7},{12,8},{13,9},{1... | collective-permute-start | bytes 491528 | tf_op jit(solution)/shard_map/ppermute | solution.py:24
  9.0 1.6 collective-permute-start.6
  10.6 3.8 %collective-permute-start.3 = (f32[5,64,128]{2,1,0:T(8,128)S(1)}, f32[5,64,128]{2,1,0:T(8,128)S(1)}, u32[]{:S(2)}, u32[]{:S(2)}) collective-permute-start(f32[5,64,128]{2,1,0:T(8,128)S(1)} %get-tuple-element.51), channel_id=1, source_target_pairs={{1,0},{2,1},{3,2},{0,3},{5,4},{6,5},{7,6},{4,7},{9,8},{10,9},{11,1... | collective-permute-start | bytes 491528 | tf_op jit(solution)/shard_map/ppermute | solution.py:28
  15.8 1.8 collective-permute-done.2
  17.7 3.4 %copy-done.5 = f32[4,64,8192]{2,1,0:T(8,128)S(1)} copy-done((f32[4,64,8192]{2,1,0:T(8,128)S(1)}, f32[4,64,8192]{2,1,0:T(8,128)}, u32[]{:S(2)}) %copy-start.5) | copy-done | bytes 8388632
  22.1 3.6 %collective-permute-done.5 = f32[5,64,128]{2,1,0:T(8,128)S(1)} collective-permute-done((f32[5,64,128]{2,1,0:T(8,128)S(1)}, f32[5,64,128]{2,1,0:T(8,128)S(1)}, u32[]{:S(2)}, u32[]{:S(2)}) %collective-permute-start.5) | collective-permute-done | bytes 163872 | tf_op jit(solution)/shard_map/ppermute | solution.py:28
  27.3 2.1 collective-permute-start.10
  30.6 11.0 %collective-permute-done.7 = f32[4,5,64,128]{3,2,1,0:T(8,128)S(1)} collective-permute-done((f32[4,5,64,128]{3,2,1,0:T(8,128)S(1)}, f32[4,5,64,128]{3,2,1,0:T(8,128)S(1)}, u32[]{:S(2)}, u32[]{:S(2)}) %collective-permute-start.7) | collective-permute-done | bytes 655392 | tf_op jit(solution)/shard_map/ppermute | solution.py:28
  41.6 1.5 collective-permute-start.12
  43.2 15.0 %collective-permute-done.9 = f32[4,5,64,128]{3,2,1,0:T(8,128)S(1)} collective-permute-done((f32[4,5,64,128]{3,2,1,0:T(8,128)S(1)}, f32[4,5,64,128]{3,2,1,0:T(8,128)S(1)}, u32[]{:S(2)}, u32[]{:S(2)}) %collective-permute-start.9) | collective-permute-done | bytes 655392 | tf_op jit(solution)/shard_map/ppermute | solution.py:28
  58.4 1.6 copy.9
  60.7 7.0 %all-to-all-start = ((f32[16,2,64,512]{3,2,1,0:T(8,128)}), f32[16,2,64,512]{3,2,1,0:T(8,128)}, u32[]{:S(2)}, u32[]{:S(2)}) async-start(f32[16,2,64,512]{3,2,1,0:T(8,128)} %copy-done.7), calls=%async_computation | async-start | bytes 8388608 | tf_op jit(solution)/shard_map/all_to_all | solution.py:281
  68.7 7.5 %collective-permute-done.13.inv_far.low_far = f32[16,5,64,128]{3,2,1,0:T(8,128)S(1)} collective-permute-done((f32[16,5,64,128]{3,2,1,0:T(8,128)}, f32[16,5,64,128]{3,2,1,0:T(8,128)S(1)}, u32[]{:S(2)}, u32[]{:S(2)}) %collective-permute-start.13) | collective-permute-done | bytes 2621472 | tf_op jit(solution)/shard_map/ppermute | solution.py:36
  76.2 2.7 %copy-done = f32[4,4,5,64,128]{4,3,2,1,0:T(8,128)S(1)} copy-done((f32[4,4,5,64,128]{4,3,2,1,0:T(8,128)S(1)}, f32[4,4,5,64,128]{4,3,2,1,0:T(8,128)}, u32[]{:S(2)}) %copy-start) | copy-done | bytes 2621464
  79.5 2.8 %collective-permute-start.14 = (f32[32,1024]{1,0:T(8,128)S(1)}, f32[32,1024]{1,0:T(8,128)S(1)}, u32[]{:S(2)}, u32[]{:S(2)}) collective-permute-start(f32[32,1024]{1,0:T(8,128)S(1)} %shard_map.69.p0), channel_id=1, source_target_pairs={{32,0},{48,16},{64,32},{80,48},{96,64},{112,80},{0,96},{16,112},{3... | collective-permute-start | bytes 393224 | tf_op jit(solution)/shard_map/ppermute | solution.py:32
  82.3 1.6 collective-permute-start.16
  84.8 6.2 %collective-permute-done.15.p2 = f32[32,1024]{1,0:T(8,128)S(1)} collective-permute-done((f32[32,1024]{1,0:T(8,128)S(1)}, f32[32,1024]{1,0:T(8,128)S(1)}, u32[]{:S(2)}, u32[]{:S(2)}) %collective-permute-start.15) | collective-permute-done | bytes 131104 | tf_op jit(solution)/shard_map/ppermute | solution.py:32
  91.0 1.7 copy-done.1
  92.8 1.7 copy-done.4
  98.2 2.0 collective-permute-done.17.p1
  101.5 2.3 collective-permute-done.19.p3
  103.8 2.6 shard_map.72
  106.4 2.0 collective-permute-start.21
  112.6 3.1 %collective-permute-done.22.p2 = f32[32,1024]{1,0:T(8,128)S(1)} collective-permute-done((f32[32,1024]{1,0:T(8,128)S(1)}, f32[32,1024]{1,0:T(8,128)S(1)}, u32[]{:S(2)}, u32[]{:S(2)}) %collective-permute-start.22) | collective-permute-done | bytes 131104 | tf_op jit(solution)/shard_map/ppermute | solution.py:32
  115.7 2.9 %shard_map.75 = (f32[32,1024]{1,0:T(8,128)}, f32[32,256]{1,0:T(8,128)S(1)}, f32[32,1024]{1,0:T(8,128)S(1)}) custom-call(s32[5]{0:T(128)S(1)} %stack.101.place_ref, f32[32,1024]{1,0:T(8,128)S(1)} %get-tuple-element.35.p0, f32[32,1024]{1,0:T(8,128)S(1)} %collective-permute-done.21.p1, f32[32,1024]{1,0:T(8,128)S(1)} %collective-permute-done.22.p2, ...), custom_call_target="tpu_custom_call" | custom-call | tf_op jit(solution)/shard_map/pallas_call | solution.py:133
  118.5 1.8 collective-permute-start.24
  122.4 4.4 %collective-permute-done.25.p2 = f32[32,1024]{1,0:T(8,128)S(1)} collective-permute-done((f32[32,1024]{1,0:T(8,128)S(1)}, f32[32,1024]{1,0:T(8,128)S(1)}, u32[]{:S(2)}, u32[]{:S(2)}) %collective-permute-start.25) | collective-permute-done | bytes 131104 | tf_op jit(solution)/shard_map/ppermute | solution.py:32
  127.4 3.0 %all-to-all-done.f_ref = f32[16,2,64,512]{3,2,1,0:T(8,128)} async-done(((f32[16,2,64,512]{3,2,1,0:T(8,128)}), f32[16,2,64,512]{3,2,1,0:T(8,128)}, u32[]{:S(2)}, u32[]{:S(2)}) %all-to-all-start) | async-done | bytes 4194336 | tf_op jit(solution)/shard_map/all_to_all | solution.py:281
  130.6 25.1 %all_to_all.20.refs_0_ = f32[16,2,32,256]{3,2,1,0:T(8,128)S(1)} all-to-all(f32[16,2,32,256]{3,2,1,0:T(8,128)S(1)} %broadcast_in_dim.4), channel_id=1, replica_groups=mesh['row'=8,'col'=16] {'col'}, dimensions={0} | all-to-all | bytes 2097152 | tf_op jit(solution)/shard_map/all_to_all | solution.py:317
  155.7 2.7 %collective-permute-start.28 = (f32[16,2,32,256]{3,2,1,0:T(8,128)S(1)}, f32[16,2,32,256]{3,2,1,0:T(8,128)}, u32[]{:S(2)}, u32[]{:S(2)}) collective-permute-start(f32[16,2,32,256]{3,2,1,0:T(8,128)S(1)} %all_to_all.20.refs_0_), channel_id=1, source_target_pairs={{32,0},{48,16},{64,32},{80,48},{96,64},{112,80},{0,96},{16,112},{3... | collective-permute-start | bytes 3145736 | tf_op jit(solution)/shard_map/ppermute | solution.py:32
  159.5 3.7 %all-to-all-start.2 = ((f32[16,2,32,256]{3,2,1,0:T(8,128)}), f32[16,2,32,256]{3,2,1,0:T(8,128)S(1)}, u32[]{:S(2)}, u32[]{:S(2)}) async-start(f32[16,2,32,256]{3,2,1,0:T(8,128)} %broadcast_in_dim.5), calls=%async_computation.2 | async-start | bytes 2097152 | tf_op jit(solution)/shard_map/all_to_all | solution.py:319
  163.2 3.4 %copy-done.6 = f32[4,64,8192]{2,1,0:T(8,128)S(1)} copy-done((f32[4,64,8192]{2,1,0:T(8,128)S(1)}, f32[4,64,8192]{2,1,0:T(8,128)}, u32[]{:S(2)}) %copy-start.6) | copy-done | bytes 8388632
  167.6 2.1 copy-done.8
  169.7 7.0 %all-to-all-done.2.refs_0_ = f32[16,2,32,256]{3,2,1,0:T(8,128)S(1)} async-done(((f32[16,2,32,256]{3,2,1,0:T(8,128)}), f32[16,2,32,256]{3,2,1,0:T(8,128)S(1)}, u32[]{:S(2)}, u32[]{:S(2)}) %all-to-all-start.2) | async-done | bytes 1048608 | tf_op jit(solution)/shard_map/all_to_all | solution.py:319
  177.8 3.2 %collective-permute-done.31.refs_6_ = f32[16,2,32,256]{3,2,1,0:T(8,128)} collective-permute-done((f32[16,2,32,256]{3,2,1,0:T(8,128)S(1)}, f32[16,2,32,256]{3,2,1,0:T(8,128)}, u32[]{:S(2)}, u32[]{:S(2)}) %collective-permute-start.31) | collective-permute-done | bytes 1048608 | tf_op jit(solution)/shard_map/ppermute | solution.py:32
  181.0 4.5 %all-to-all-start.3 = ((f32[16,2,64,512]{3,2,1,0:T(8,128)}), f32[16,2,64,512]{3,2,1,0:T(8,128)}, u32[]{:S(2)}, u32[]{:S(2)}) async-start(f32[16,2,64,512]{3,2,1,0:T(8,128)} %copy-done.8), calls=%async_computation.3 | async-start | bytes 8388608 | tf_op jit(solution)/shard_map/all_to_all | solution.py:320
  185.6 4.3 %collective-permute-start.27 = (f32[16,2,32,256]{3,2,1,0:T(8,128)S(1)}, f32[16,2,32,256]{3,2,1,0:T(8,128)S(1)}, u32[]{:S(2)}, u32[]{:S(2)}) collective-permute-start(f32[16,2,32,256]{3,2,1,0:T(8,128)S(1)} %all_to_all.20.refs_0_), channel_id=1, source_target_pairs={{0,16},{16,0},{32,48},{48,32},{64,80},{80,64},{96,112},{112,96},{1... | collective-permute-start | bytes 3145736 | tf_op jit(solution)/shard_map/ppermute | solution.py:36
  192.2 1.5 collective-permute-start.32
  194.3 10.5 %collective-permute-done.30 = f32[8,2,32,256]{3,2,1,0:T(8,128)S(1)} collective-permute-done((f32[8,2,32,256]{3,2,1,0:T(8,128)S(1)}, f32[8,2,32,256]{3,2,1,0:T(8,128)S(1)}, u32[]{:S(2)}, u32[]{:S(2)}) %collective-permute-start.30) | collective-permute-done | bytes 524320 | tf_op jit(solution)/shard_map/ppermute | solution.py:32
  204.8 2.0 collective-permute-done.32
  207.9 1.5 collective-permute-start.39
  210.7 13.9 %shard_map.77 = (f32[512,1024]{1,0:T(8,128)}, f32[2,64,128]{2,1,0:T(8,128)}) custom-call(s32[5]{0:T(128)} %copy-done.9, f32[16,2,64,512]{3,2,1,0:T(8,128)} %all-to-all-done.f_ref, f32[16,2,32,256]{3,2,1,0:T(8,128)} %copy-done.11, f32[16,2,32,256]{3,2,1,0:T(8,128)} %copy-done.16, f32[16,2,32,256]{3,2,1,0:T(8,128)} %collective-permute-done.28.refs_2_, ...), custom_call_target="tpu_custom_call" | custom-call | tf_op jit(solution)/shard_map/pallas_call | solution.py:230
  224.6 8.1 %collective-permute-done.36.refs_2_ = f32[16,2,32,256]{3,2,1,0:T(8,128)S(1)} collective-permute-done((f32[16,2,32,256]{3,2,1,0:T(8,128)S(1)}, f32[16,2,32,256]{3,2,1,0:T(8,128)S(1)}, u32[]{:S(2)}, u32[]{:S(2)}) %collective-permute-start.36) | collective-permute-done | bytes 1048608 | tf_op jit(solution)/shard_map/ppermute | solution.py:32
  236.3 9.3 %collective-permute-done.38 = f32[8,2,32,256]{3,2,1,0:T(8,128)S(1)} collective-permute-done((f32[8,2,32,256]{3,2,1,0:T(8,128)S(1)}, f32[8,2,32,256]{3,2,1,0:T(8,128)S(1)}, u32[]{:S(2)}, u32[]{:S(2)}) %collective-permute-start.38) | collective-permute-done | bytes 524320 | tf_op jit(solution)/shard_map/ppermute | solution.py:32
  245.6 2.6 collective-permute-done.40
  248.3 1.8 collective-permute-start.41
  252.5 13.9 %shard_map.79 = (f32[512,1024]{1,0:T(8,128)}, f32[2,64,128]{2,1,0:T(8,128)}) custom-call(s32[5]{0:T(128)} %copy-done.9, f32[16,2,64,512]{3,2,1,0:T(8,128)} %all-to-all-done.3.f_ref, f32[16,2,32,256]{3,2,1,0:T(8,128)} %copy-done.10, f32[16,2,32,256]{3,2,1,0:T(8,128)} %copy-done.17, f32[16,2,32,256]{3,2,1,0:T(8,128)} %copy-done.12, ...), custom_call_target="tpu_custom_call" | custom-call | tf_op jit(solution)/shard_map/pallas_call | solution.py:230
  266.4 1.5 pad_maximum_fusion.6
  (136 shorter events, 40.0 us)
Async XLA Ops:
  3.1 11.9 %collective-permute-start = (f32[5,64,128]{2,1,0:T(8,128)S(1)}, f32[5,64,128]{2,1,0:T(8,128)S(1)}, u32[]{:S(2)}, u32[]{:S(2)}) collective-permute-start(f32[5,64,128]{2,1,0:T(8,128)S(1)} %get-tuple-element.53), channel_id=1, source_target_pairs={{4,0},{5,1},{6,2},{7,3},{8,4},{9,5},{10,6},{11,7},{12,8},{13,9},{1... | collective-permute-start | bytes 491528 | tf_op jit(solution)/shard_map/ppermute | solution.py:24
  6.5 9.3 %collective-permute-start.1 = (f32[5,64,128]{2,1,0:T(8,128)S(1)}, f32[5,64,128]{2,1,0:T(8,128)S(1)}, u32[]{:S(2)}, u32[]{:S(2)}) collective-permute-start(f32[5,64,128]{2,1,0:T(8,128)S(1)} %get-tuple-element.53), channel_id=1, source_target_pairs={{8,0},{9,1},{10,2},{11,3},{12,4},{13,5},{14,6},{15,7},{0,8},{1,9},... | collective-permute-start | bytes 491528 | tf_op jit(solution)/shard_map/ppermute | solution.py:24
  7.0 10.6 %collective-permute-start.2 = (f32[5,64,128]{2,1,0:T(8,128)S(1)}, f32[5,64,128]{2,1,0:T(8,128)S(1)}, u32[]{:S(2)}, u32[]{:S(2)}) collective-permute-start(f32[5,64,128]{2,1,0:T(8,128)S(1)} %get-tuple-element.53), channel_id=1, source_target_pairs={{12,0},{13,1},{14,2},{15,3},{0,4},{1,5},{2,6},{3,7},{4,8},{5,9},{6... | collective-permute-start | bytes 491528 | tf_op jit(solution)/shard_map/ppermute | solution.py:24
  9.0 5.5 %collective-permute-start.6 = (f32[4,32,128]{2,1,0:T(8,128)S(1)}, f32[4,32,128]{2,1,0:T(8,128)S(1)}, u32[]{:S(2)}, u32[]{:S(2)}) collective-permute-start(f32[4,32,128]{2,1,0:T(8,128)S(1)} %bitcast.64), channel_id=1, source_target_pairs={{0,16},{16,0},{32,48},{48,32},{64,80},{80,64},{96,112},{112,96},{1... | collective-permute-start | bytes 196616 | tf_op jit(solution)/shard_map/ppermute | solution.py:36
  10.6 11.5 %collective-permute-start.3 = (f32[5,64,128]{2,1,0:T(8,128)S(1)}, f32[5,64,128]{2,1,0:T(8,128)S(1)}, u32[]{:S(2)}, u32[]{:S(2)}) collective-permute-start(f32[5,64,128]{2,1,0:T(8,128)S(1)} %get-tuple-element.51), channel_id=1, source_target_pairs={{1,0},{2,1},{3,2},{0,3},{5,4},{6,5},{7,6},{4,7},{9,8},{10,9},{11,1... | collective-permute-start | bytes 491528 | tf_op jit(solution)/shard_map/ppermute | solution.py:28
  14.5 7.6 %collective-permute-start.4 = (f32[5,64,128]{2,1,0:T(8,128)S(1)}, f32[5,64,128]{2,1,0:T(8,128)S(1)}, u32[]{:S(2)}, u32[]{:S(2)}) collective-permute-start(f32[5,64,128]{2,1,0:T(8,128)S(1)} %get-tuple-element.51), channel_id=1, source_target_pairs={{2,0},{3,1},{0,2},{1,3},{6,4},{7,5},{4,6},{5,7},{10,8},{11,9},{8,1... | collective-permute-start | bytes 491528 | tf_op jit(solution)/shard_map/ppermute | solution.py:28
  15.0 10.7 %collective-permute-start.5 = (f32[5,64,128]{2,1,0:T(8,128)S(1)}, f32[5,64,128]{2,1,0:T(8,128)S(1)}, u32[]{:S(2)}, u32[]{:S(2)}) collective-permute-start(f32[5,64,128]{2,1,0:T(8,128)S(1)} %get-tuple-element.51), channel_id=1, source_target_pairs={{3,0},{0,1},{1,2},{2,3},{7,4},{4,5},{5,6},{6,7},{11,8},{8,9},{9,10... | collective-permute-start | bytes 491528 | tf_op jit(solution)/shard_map/ppermute | solution.py:28
  25.8 15.9 %collective-permute-start.7 = (f32[4,5,64,128]{3,2,1,0:T(8,128)S(1)}, f32[4,5,64,128]{3,2,1,0:T(8,128)S(1)}, u32[]{:S(2)}, u32[]{:S(2)}) collective-permute-start(f32[4,5,64,128]{3,2,1,0:T(8,128)S(1)} %pad_maximum_fusion.1), channel_id=1, source_target_pairs={{1,0},{2,1},{3,2},{0,3},{5,4},{6,5},{7,6},{4,7},{9,8},{10,9},{11,1... | collective-permute-start | bytes 1966088 | tf_op jit(solution)/shard_map/ppermute | solution.py:28
  26.0 17.2 %collective-permute-start.8 = (f32[4,5,64,128]{3,2,1,0:T(8,128)S(1)}, f32[4,5,64,128]{3,2,1,0:T(8,128)S(1)}, u32[]{:S(2)}, u32[]{:S(2)}) collective-permute-start(f32[4,5,64,128]{3,2,1,0:T(8,128)S(1)} %pad_maximum_fusion.1), channel_id=1, source_target_pairs={{2,0},{3,1},{0,2},{1,3},{6,4},{7,5},{4,6},{5,7},{10,8},{11,9},{8,1... | collective-permute-start | bytes 1966088 | tf_op jit(solution)/shard_map/ppermute | solution.py:28
  26.4 31.8 %collective-permute-start.9 = (f32[4,5,64,128]{3,2,1,0:T(8,128)S(1)}, f32[4,5,64,128]{3,2,1,0:T(8,128)S(1)}, u32[]{:S(2)}, u32[]{:S(2)}) collective-permute-start(f32[4,5,64,128]{3,2,1,0:T(8,128)S(1)} %pad_maximum_fusion.1), channel_id=1, source_target_pairs={{3,0},{0,1},{1,2},{2,3},{7,4},{4,5},{5,6},{6,7},{11,8},{8,9},{9,10... | collective-permute-start | bytes 1966088 | tf_op jit(solution)/shard_map/ppermute | solution.py:28
  27.3 32.7 %collective-permute-start.10 = (f32[4,5,64,128]{3,2,1,0:T(8,128)S(1)}, f32[4,5,64,128]{3,2,1,0:T(8,128)S(1)}, u32[]{:S(2)}, u32[]{:S(2)}) collective-permute-start(f32[4,5,64,128]{3,2,1,0:T(8,128)S(1)} %pad_maximum_fusion.2), channel_id=1, source_target_pairs={{4,0},{5,1},{6,2},{7,3},{8,4},{9,5},{10,6},{11,7},{12,8},{13,9},{1... | collective-permute-start | bytes 1966088 | tf_op jit(solution)/shard_map/ppermute | solution.py:24
  29.4 30.6 %collective-permute-start.11 = (f32[4,5,64,128]{3,2,1,0:T(8,128)S(1)}, f32[4,5,64,128]{3,2,1,0:T(8,128)S(1)}, u32[]{:S(2)}, u32[]{:S(2)}) collective-permute-start(f32[4,5,64,128]{3,2,1,0:T(8,128)S(1)} %pad_maximum_fusion.2), channel_id=1, source_target_pairs={{8,0},{9,1},{10,2},{11,3},{12,4},{13,5},{14,6},{15,7},{0,8},{1,9},... | collective-permute-start | bytes 1966088 | tf_op jit(solution)/shard_map/ppermute | solution.py:24
  41.6 18.9 %collective-permute-start.12 = (f32[4,5,64,128]{3,2,1,0:T(8,128)S(1)}, f32[4,5,64,128]{3,2,1,0:T(8,128)S(1)}, u32[]{:S(2)}, u32[]{:S(2)}) collective-permute-start(f32[4,5,64,128]{3,2,1,0:T(8,128)S(1)} %pad_maximum_fusion.2), channel_id=1, source_target_pairs={{12,0},{13,1},{14,2},{15,3},{0,4},{1,5},{2,6},{3,7},{4,8},{5,9},{6... | collective-permute-start | bytes 1966088 | tf_op jit(solution)/shard_map/ppermute | solution.py:24
  60.7 69.7 %all-to-all-start = ((f32[16,2,64,512]{3,2,1,0:T(8,128)}), f32[16,2,64,512]{3,2,1,0:T(8,128)}, u32[]{:S(2)}, u32[]{:S(2)}) async-start(f32[16,2,64,512]{3,2,1,0:T(8,128)} %copy-done.7), calls=%async_computation | async-start | bytes 8388608 | tf_op jit(solution)/shard_map/all_to_all | solution.py:281
  67.7 8.4 %collective-permute-start.13 = (f32[16,5,64,128]{3,2,1,0:T(8,128)}, f32[16,5,64,128]{3,2,1,0:T(8,128)S(1)}, u32[]{:S(2)}, u32[]{:S(2)}) collective-permute-start(f32[16,5,64,128]{3,2,1,0:T(8,128)} %bitcast.39), channel_id=1, source_target_pairs={{0,16},{16,0},{32,48},{48,32},{64,80},{80,64},{96,112},{112,96},{1... | collective-permute-start | bytes 7864328 | tf_op jit(solution)/shard_map/ppermute | solution.py:36
  68.6 29.6 %collective-permute-start.20 = (f32[16,5,64,128]{3,2,1,0:T(8,128)S(1)}, f32[16,5,64,128]{3,2,1,0:T(8,128)}, u32[]{:S(2)}, u32[]{:S(2)}) collective-permute-start(f32[16,5,64,128]{3,2,1,0:T(8,128)S(1)} %bitcast.33), channel_id=1, source_target_pairs={{0,16},{16,0},{32,48},{48,32},{64,80},{80,64},{96,112},{112,96},{1... | collective-permute-start | bytes 7864328 | tf_op jit(solution)/shard_map/ppermute | solution.py:36
  79.5 5.3 %collective-permute-start.14 = (f32[32,1024]{1,0:T(8,128)S(1)}, f32[32,1024]{1,0:T(8,128)S(1)}, u32[]{:S(2)}, u32[]{:S(2)}) collective-permute-start(f32[32,1024]{1,0:T(8,128)S(1)} %shard_map.69.p0), channel_id=1, source_target_pairs={{32,0},{48,16},{64,32},{80,48},{96,64},{112,80},{0,96},{16,112},{3... | collective-permute-start | bytes 393224 | tf_op jit(solution)/shard_map/ppermute | solution.py:32
  82.3 8.7 %collective-permute-start.15 = (f32[32,1024]{1,0:T(8,128)S(1)}, f32[32,1024]{1,0:T(8,128)S(1)}, u32[]{:S(2)}, u32[]{:S(2)}) collective-permute-start(f32[32,1024]{1,0:T(8,128)S(1)} %shard_map.69.p0), channel_id=1, source_target_pairs={{96,0},{112,16},{0,32},{16,48},{32,64},{48,80},{64,96},{80,112},{9... | collective-permute-start | bytes 393224 | tf_op jit(solution)/shard_map/ppermute | solution.py:32
  82.3 8.7 %collective-permute-start.16 = (f32[32,1024]{1,0:T(8,128)S(1)}, f32[32,1024]{1,0:T(8,128)S(1)}, u32[]{:S(2)}, u32[]{:S(2)}) collective-permute-start(f32[32,1024]{1,0:T(8,128)S(1)} %shard_map.69.p0), channel_id=1, source_target_pairs={{64,0},{80,16},{96,32},{112,48},{0,64},{16,80},{32,96},{48,112},{6... | collective-permute-start | bytes 393224 | tf_op jit(solution)/shard_map/ppermute | solution.py:32
  84.0 42.8 %copy-start.9 = (s32[5]{0:T(128)}, s32[5]{0:T(128)S(1)}, u32[]{:S(2)}) copy-start(s32[5]{0:T(128)S(1)} %stack.101.place_ref) | copy-start | bytes 64
  95.9 4.3 %collective-permute-start.17 = (f32[32,1024]{1,0:T(8,128)S(1)}, f32[32,1024]{1,0:T(8,128)S(1)}, u32[]{:S(2)}, u32[]{:S(2)}) collective-permute-start(f32[32,1024]{1,0:T(8,128)S(1)} %get-tuple-element.32.p0), channel_id=1, source_target_pairs={{32,0},{48,16},{64,32},{80,48},{96,64},{112,80},{0,96},{16,112},{3... | collective-permute-start | bytes 393224 | tf_op jit(solution)/shard_map/ppermute | solution.py:32
  96.0 5.5 %collective-permute-start.18 = (f32[32,1024]{1,0:T(8,128)S(1)}, f32[32,1024]{1,0:T(8,128)S(1)}, u32[]{:S(2)}, u32[]{:S(2)}) collective-permute-start(f32[32,1024]{1,0:T(8,128)S(1)} %get-tuple-element.32.p0), channel_id=1, source_target_pairs={{96,0},{112,16},{0,32},{16,48},{32,64},{48,80},{64,96},{80,112},{9... | collective-permute-start | bytes 393224 | tf_op jit(solution)/shard_map/ppermute | solution.py:32
  97.4 6.4 %collective-permute-start.19 = (f32[32,1024]{1,0:T(8,128)S(1)}, f32[32,1024]{1,0:T(8,128)S(1)}, u32[]{:S(2)}, u32[]{:S(2)}) collective-permute-start(f32[32,1024]{1,0:T(8,128)S(1)} %get-tuple-element.32.p0), channel_id=1, source_target_pairs={{64,0},{80,16},{96,32},{112,48},{0,64},{16,80},{32,96},{48,112},{6... | collective-permute-start | bytes 393224 | tf_op jit(solution)/shard_map/ppermute | solution.py:32
  106.4 6.2 %collective-permute-start.21 = (f32[32,1024]{1,0:T(8,128)S(1)}, f32[32,1024]{1,0:T(8,128)S(1)}, u32[]{:S(2)}, u32[]{:S(2)}) collective-permute-start(f32[32,1024]{1,0:T(8,128)S(1)} %get-tuple-element.35.p0), channel_id=1, source_target_pairs={{32,0},{48,16},{64,32},{80,48},{96,64},{112,80},{0,96},{16,112},{3... | collective-permute-start | bytes 393224 | tf_op jit(solution)/shard_map/ppermute | solution.py:32
  108.4 7.3 %collective-permute-start.22 = (f32[32,1024]{1,0:T(8,128)S(1)}, f32[32,1024]{1,0:T(8,128)S(1)}, u32[]{:S(2)}, u32[]{:S(2)}) collective-permute-start(f32[32,1024]{1,0:T(8,128)S(1)} %get-tuple-element.35.p0), channel_id=1, source_target_pairs={{96,0},{112,16},{0,32},{16,48},{32,64},{48,80},{64,96},{80,112},{9... | collective-permute-start | bytes 393224 | tf_op jit(solution)/shard_map/ppermute | solution.py:32
  108.4 7.3 %collective-permute-start.23 = (f32[32,1024]{1,0:T(8,128)S(1)}, f32[32,1024]{1,0:T(8,128)S(1)}, u32[]{:S(2)}, u32[]{:S(2)}) collective-permute-start(f32[32,1024]{1,0:T(8,128)S(1)} %get-tuple-element.35.p0), channel_id=1, source_target_pairs={{64,0},{80,16},{96,32},{112,48},{0,64},{16,80},{32,96},{48,112},{6... | collective-permute-start | bytes 393224 | tf_op jit(solution)/shard_map/ppermute | solution.py:32
  118.5 3.8 %collective-permute-start.24 = (f32[32,1024]{1,0:T(8,128)S(1)}, f32[32,1024]{1,0:T(8,128)S(1)}, u32[]{:S(2)}, u32[]{:S(2)}) collective-permute-start(f32[32,1024]{1,0:T(8,128)S(1)} %get-tuple-element.37.p0), channel_id=1, source_target_pairs={{32,0},{48,16},{64,32},{80,48},{96,64},{112,80},{0,96},{16,112},{3... | collective-permute-start | bytes 393224 | tf_op jit(solution)/shard_map/ppermute | solution.py:32
  120.4 6.4 %collective-permute-start.25 = (f32[32,1024]{1,0:T(8,128)S(1)}, f32[32,1024]{1,0:T(8,128)S(1)}, u32[]{:S(2)}, u32[]{:S(2)}) collective-permute-start(f32[32,1024]{1,0:T(8,128)S(1)} %get-tuple-element.37.p0), channel_id=1, source_target_pairs={{96,0},{112,16},{0,32},{16,48},{32,64},{48,80},{64,96},{80,112},{9... | collective-permute-start | bytes 393224 | tf_op jit(solution)/shard_map/ppermute | solution.py:32
  120.4 6.4 %collective-permute-start.26 = (f32[32,1024]{1,0:T(8,128)S(1)}, f32[32,1024]{1,0:T(8,128)S(1)}, u32[]{:S(2)}, u32[]{:S(2)}) collective-permute-start(f32[32,1024]{1,0:T(8,128)S(1)} %get-tuple-element.37.p0), channel_id=1, source_target_pairs={{64,0},{80,16},{96,32},{112,48},{0,64},{16,80},{32,96},{48,112},{6... | collective-permute-start | bytes 393224 | tf_op jit(solution)/shard_map/ppermute | solution.py:32
  155.7 22.1 %collective-permute-start.28 = (f32[16,2,32,256]{3,2,1,0:T(8,128)S(1)}, f32[16,2,32,256]{3,2,1,0:T(8,128)}, u32[]{:S(2)}, u32[]{:S(2)}) collective-permute-start(f32[16,2,32,256]{3,2,1,0:T(8,128)S(1)} %all_to_all.20.refs_0_), channel_id=1, source_target_pairs={{32,0},{48,16},{64,32},{80,48},{96,64},{112,80},{0,96},{16,112},{3... | collective-permute-start | bytes 3145736 | tf_op jit(solution)/shard_map/ppermute | solution.py:32
  158.4 22.6 %collective-permute-start.31 = (f32[16,2,32,256]{3,2,1,0:T(8,128)S(1)}, f32[16,2,32,256]{3,2,1,0:T(8,128)}, u32[]{:S(2)}, u32[]{:S(2)}) collective-permute-start(f32[16,2,32,256]{3,2,1,0:T(8,128)S(1)} %all_to_all.20.refs_0_), channel_id=1, source_target_pairs={{96,0},{112,16},{0,32},{16,48},{32,64},{48,80},{64,96},{80,112},{9... | collective-permute-start | bytes 3145736 | tf_op jit(solution)/shard_map/ppermute | solution.py:32
  159.5 17.2 %all-to-all-start.2 = ((f32[16,2,32,256]{3,2,1,0:T(8,128)}), f32[16,2,32,256]{3,2,1,0:T(8,128)S(1)}, u32[]{:S(2)}, u32[]{:S(2)}) async-start(f32[16,2,32,256]{3,2,1,0:T(8,128)} %broadcast_in_dim.5), calls=%async_computation.2 | async-start | bytes 2097152 | tf_op jit(solution)/shard_map/all_to_all | solution.py:319
  176.7 57.8 %copy-start.10 = (f32[16,2,32,256]{3,2,1,0:T(8,128)}, f32[16,2,32,256]{3,2,1,0:T(8,128)S(1)}, u32[]{:S(2)}) copy-start(f32[16,2,32,256]{3,2,1,0:T(8,128)S(1)} %all-to-all-done.2.refs_0_) | copy-start | bytes 3145732
  181.0 71.5 %all-to-all-start.3 = ((f32[16,2,64,512]{3,2,1,0:T(8,128)}), f32[16,2,64,512]{3,2,1,0:T(8,128)}, u32[]{:S(2)}, u32[]{:S(2)}) async-start(f32[16,2,64,512]{3,2,1,0:T(8,128)} %copy-done.8), calls=%async_computation.3 | async-start | bytes 8388608 | tf_op jit(solution)/shard_map/all_to_all | solution.py:320
  185.6 22.3 %collective-permute-start.27 = (f32[16,2,32,256]{3,2,1,0:T(8,128)S(1)}, f32[16,2,32,256]{3,2,1,0:T(8,128)S(1)}, u32[]{:S(2)}, u32[]{:S(2)}) collective-permute-start(f32[16,2,32,256]{3,2,1,0:T(8,128)S(1)} %all_to_all.20.refs_0_), channel_id=1, source_target_pairs={{0,16},{16,0},{32,48},{48,32},{64,80},{80,64},{96,112},{112,96},{1... | collective-permute-start | bytes 3145736 | tf_op jit(solution)/shard_map/ppermute | solution.py:36
  191.0 13.7 %collective-permute-start.30 = (f32[8,2,32,256]{3,2,1,0:T(8,128)S(1)}, f32[8,2,32,256]{3,2,1,0:T(8,128)S(1)}, u32[]{:S(2)}, u32[]{:S(2)}) collective-permute-start(f32[8,2,32,256]{3,2,1,0:T(8,128)S(1)} %slice.56), channel_id=1, source_target_pairs={{32,0},{48,16},{64,32},{80,48},{96,64},{112,80},{0,96},{16,112},{3... | collective-permute-start | bytes 1572872 | tf_op jit(solution)/shard_map/ppermute | solution.py:32
  192.2 14.6 %collective-permute-start.32 = (f32[8,2,32,256]{3,2,1,0:T(8,128)S(1)}, f32[8,2,32,256]{3,2,1,0:T(8,128)S(1)}, u32[]{:S(2)}, u32[]{:S(2)}) collective-permute-start(f32[8,2,32,256]{3,2,1,0:T(8,128)S(1)} %slice.57), channel_id=1, source_target_pairs={{96,0},{112,16},{0,32},{16,48},{32,64},{48,80},{64,96},{80,112},{9... | collective-permute-start | bytes 1572872 | tf_op jit(solution)/shard_map/ppermute | solution.py:32
  193.7 15.7 %collective-permute-start.29 = (f32[16,2,32,256]{3,2,1,0:T(8,128)}, f32[16,2,32,256]{3,2,1,0:T(8,128)S(1)}, u32[]{:S(2)}, u32[]{:S(2)}) collective-permute-start(f32[16,2,32,256]{3,2,1,0:T(8,128)} %collective-permute-done.28.refs_2_), channel_id=1, source_target_pairs={{0,16},{16,0},{32,48},{48,32},{64,80},{80,64},{96,112},{112,96},{1... | collective-permute-start | bytes 3145736 | tf_op jit(solution)/shard_map/ppermute | solution.py:36
  194.3 15.2 %collective-permute-start.34 = (f32[16,2,32,256]{3,2,1,0:T(8,128)}, f32[16,2,32,256]{3,2,1,0:T(8,128)S(1)}, u32[]{:S(2)}, u32[]{:S(2)}) collective-permute-start(f32[16,2,32,256]{3,2,1,0:T(8,128)} %collective-permute-done.31.refs_6_), channel_id=1, source_target_pairs={{0,16},{16,0},{32,48},{48,32},{64,80},{80,64},{96,112},{112,96},{1... | collective-permute-start | bytes 3145736 | tf_op jit(solution)/shard_map/ppermute | solution.py:36
  206.9 3.5 %collective-permute-start.33 = (f32[16,2,32,256]{3,2,1,0:T(8,128)S(1)}, f32[16,2,32,256]{3,2,1,0:T(8,128)}, u32[]{:S(2)}, u32[]{:S(2)}) collective-permute-start(f32[16,2,32,256]{3,2,1,0:T(8,128)S(1)} %constant_dynamic-update-slice_fusion.refs_4_), channel_id=1, source_target_pairs={{0,16},{16,0},{32,48},{48,32},{64,80},{80,64},{96,112},{112,96},{1... | collective-permute-start | bytes 3145736 | tf_op jit(solution)/shard_map/ppermute | solution.py:36
  207.9 24.8 %collective-permute-start.36 = (f32[16,2,32,256]{3,2,1,0:T(8,128)S(1)}, f32[16,2,32,256]{3,2,1,0:T(8,128)S(1)}, u32[]{:S(2)}, u32[]{:S(2)}) collective-permute-start(f32[16,2,32,256]{3,2,1,0:T(8,128)S(1)} %all-to-all-done.2.refs_0_), channel_id=1, source_target_pairs={{32,0},{48,16},{64,32},{80,48},{96,64},{112,80},{0,96},{16,112},{3... | collective-permute-start | bytes 3145736 | tf_op jit(solution)/shard_map/ppermute | solution.py:32
  207.9 26.3 %collective-permute-start.39 = (f32[16,2,32,256]{3,2,1,0:T(8,128)S(1)}, f32[16,2,32,256]{3,2,1,0:T(8,128)S(1)}, u32[]{:S(2)}, u32[]{:S(2)}) collective-permute-start(f32[16,2,32,256]{3,2,1,0:T(8,128)S(1)} %all-to-all-done.2.refs_0_), channel_id=1, source_target_pairs={{96,0},{112,16},{0,32},{16,48},{32,64},{48,80},{64,96},{80,112},{9... | collective-permute-start | bytes 3145736 | tf_op jit(solution)/shard_map/ppermute | solution.py:32
  232.8 12.8 %collective-permute-start.38 = (f32[8,2,32,256]{3,2,1,0:T(8,128)S(1)}, f32[8,2,32,256]{3,2,1,0:T(8,128)S(1)}, u32[]{:S(2)}, u32[]{:S(2)}) collective-permute-start(f32[8,2,32,256]{3,2,1,0:T(8,128)S(1)} %slice.54), channel_id=1, source_target_pairs={{32,0},{48,16},{64,32},{80,48},{96,64},{112,80},{0,96},{16,112},{3... | collective-permute-start | bytes 1572872 | tf_op jit(solution)/shard_map/ppermute | solution.py:32
  234.3 13.9 %collective-permute-start.40 = (f32[8,2,32,256]{3,2,1,0:T(8,128)S(1)}, f32[8,2,32,256]{3,2,1,0:T(8,128)S(1)}, u32[]{:S(2)}, u32[]{:S(2)}) collective-permute-start(f32[8,2,32,256]{3,2,1,0:T(8,128)S(1)} %slice.58), channel_id=1, source_target_pairs={{96,0},{112,16},{0,32},{16,48},{32,64},{48,80},{64,96},{80,112},{9... | collective-permute-start | bytes 1572872 | tf_op jit(solution)/shard_map/ppermute | solution.py:32
  234.5 15.6 %collective-permute-start.35 = (f32[16,2,32,256]{3,2,1,0:T(8,128)S(1)}, f32[16,2,32,256]{3,2,1,0:T(8,128)S(1)}, u32[]{:S(2)}, u32[]{:S(2)}) collective-permute-start(f32[16,2,32,256]{3,2,1,0:T(8,128)S(1)} %all-to-all-done.2.refs_0_), channel_id=1, source_target_pairs={{0,16},{16,0},{32,48},{48,32},{64,80},{80,64},{96,112},{112,96},{1... | collective-permute-start | bytes 3145736 | tf_op jit(solution)/shard_map/ppermute | solution.py:36
  235.8 14.3 %collective-permute-start.37 = (f32[16,2,32,256]{3,2,1,0:T(8,128)S(1)}, f32[16,2,32,256]{3,2,1,0:T(8,128)S(1)}, u32[]{:S(2)}, u32[]{:S(2)}) collective-permute-start(f32[16,2,32,256]{3,2,1,0:T(8,128)S(1)} %collective-permute-done.36.refs_2_), channel_id=1, source_target_pairs={{0,16},{16,0},{32,48},{48,32},{64,80},{80,64},{96,112},{112,96},{1... | collective-permute-start | bytes 3145736 | tf_op jit(solution)/shard_map/ppermute | solution.py:36
  235.8 14.3 %collective-permute-start.42 = (f32[16,2,32,256]{3,2,1,0:T(8,128)S(1)}, f32[16,2,32,256]{3,2,1,0:T(8,128)S(1)}, u32[]{:S(2)}, u32[]{:S(2)}) collective-permute-start(f32[16,2,32,256]{3,2,1,0:T(8,128)S(1)} %collective-permute-done.39.refs_6_), channel_id=1, source_target_pairs={{0,16},{16,0},{32,48},{48,32},{64,80},{80,64},{96,112},{112,96},{1... | collective-permute-start | bytes 3145736 | tf_op jit(solution)/shard_map/ppermute | solution.py:36
  248.3 4.2 %collective-permute-start.41 = (f32[16,2,32,256]{3,2,1,0:T(8,128)S(1)}, f32[16,2,32,256]{3,2,1,0:T(8,128)}, u32[]{:S(2)}, u32[]{:S(2)}) collective-permute-start(f32[16,2,32,256]{3,2,1,0:T(8,128)S(1)} %constant_dynamic-update-slice_fusion.2.refs_4_), channel_id=1, source_target_pairs={{0,16},{16,0},{32,48},{48,32},{64,80},{80,64},{96,112},{112,96},{1... | collective-permute-start | bytes 3145736 | tf_op jit(solution)/shard_map/ppermute | solution.py:36
  (23 other events, 180.0 us)
